TPU v7x, 32 devices: a whole 2x2x4 slice. The times are simulated.
32 devices in a mesh: group: 2 (over x), lat: 16 (over z, y, core).
Axes of the slice: x: 2, y: 2, z: 4, core: 2. Of those that a mesh axis runs over, the one named last changes fastest.
Arguments:
- field: bfloat16 [1024, 512, 512], P(('group', 'lat')), parts along dimension 0, may hold values from -6 to 6
- lat_modes: float32 [64, 16, 16], replicated, may hold values from -1.5 to 1.5
- lat_gains: float32 [64, 16], replicated, may hold values from 2 to 16
- lat_local: float32 [16, 16], replicated, may hold values from -1.5 to 1.5
- depth_modes: float32 [16, 16, 16], replicated, may hold values from -1.5 to 1.5
- depth_local: float32 [16, 16], replicated, may hold values from -1.5 to 1.5
Outputs:
- result: bfloat16 [1024, 512, 512], P(('group', 'lat')), parts along dimension 0
There are 2 independent parts, one for each index of `group`. A program takes and returns all parts, laid end to end along the dimension named above; an argument that names none is the same for every part. Nothing has to cross between parts.
All inputs are finite; a program needn't handle non-finite values.
Results may differ from a plain program's by a relative error of at most 0.001.
Values may be sent and summed in bfloat16 or wider, within the bound.
No kernel may reach another device: no remote copies, remote signals or barrier semaphores. Data moves between devices by JAX's collectives and lax.ppermute only.
A program may use at most 192 MiB of HBM per device.

v0:
```python
import math

import jax
import jax.numpy as jnp
from jax import lax
from jax.sharding import PartitionSpec as P


def cosine_basis(length, modes):
    order = jnp.arange(modes, dtype=jnp.float32)[:, None]
    place = jnp.arange(length, dtype=jnp.float32)[None, :]
    scales = jnp.where(order == 0.0, math.sqrt(1.0 / length), math.sqrt(2.0 / length))
    return jnp.cos(math.pi * order * (place + 0.5) / length) * scales


def row_tail(u_rows, spect, lat_local, depth_modes, depth_local, depth_basis):
    highest = lax.Precision.HIGHEST
    rows, width, cells = u_rows.shape
    chans = lat_local.shape[0]
    depth = cells // chans
    u4 = u_rows.reshape(rows, width, depth, chans)
    s4 = spect.reshape(rows, width, depth, chans)
    first = u4 + jax.nn.gelu(s4 + jnp.einsum("xyzc,cd->xyzd", u4, lat_local, precision=highest))
    dcoef = jnp.einsum("kz,xyzc->xykc", depth_basis, first, precision=highest)
    dmix = jnp.einsum("xykc,kcd->xykd", dcoef, depth_modes, precision=highest)
    dspect = jnp.einsum("kz,xykd->xyzd", depth_basis, dmix, precision=highest)
    final = first + jax.nn.gelu(
        dspect + jnp.einsum("xyzc,cd->xyzd", first, depth_local, precision=highest)
    )
    return final.reshape(rows, width, cells).astype(jnp.bfloat16)


def one_hot(ids, count):
    return (ids[:, None] == jnp.arange(count, dtype=jnp.int32)[None, :]).astype(jnp.float32)


def shards(field, lat_modes, lat_gains, lat_local, depth_modes, depth_local):
    highest = lax.Precision.HIGHEST
    devices = lax.axis_size("lat")
    rows_dev, width_y, cells = field.shape
    modes_x, chans, _ = lat_modes.shape
    modes_y = lat_gains.shape[0]
    modes_z = depth_modes.shape[0]
    depth = cells // chans
    width_x = rows_dev * devices
    basis_x = cosine_basis(width_x, modes_x)
    basis_y = cosine_basis(width_y, modes_y)
    basis_z = cosine_basis(depth, modes_z)
    start = lax.axis_index("lat")
    u_rows = field.astype(jnp.float32)
    coef_y = jnp.einsum("qy,xyw->xqw", basis_y, u_rows, precision=highest)
    packed = coef_y.reshape(rows_dev, modes_y * cells)
    gathered = lax.all_to_all(packed, "lat", split_axis=1, concat_axis=0, tiled=True)
    span = gathered.shape[1]
    pairs = span // chans
    coef = jnp.dot(basis_x, gathered, precision=highest).reshape(modes_x, pairs, chans)
    mode_ids = (start * pairs + jnp.arange(pairs, dtype=jnp.int32)) // depth
    gain_rows = jnp.dot(one_hot(mode_ids, modes_y), lat_gains, precision=highest)
    mixed = jnp.einsum("jpc,jcd->jpd", coef * gain_rows[None, :, :], lat_modes, precision=highest)
    back_x = jnp.dot(basis_x.T, mixed.reshape(modes_x, span), precision=highest)
    returned = lax.all_to_all(back_x, "lat", split_axis=0, concat_axis=1, tiled=True)
    spect = jnp.einsum(
        "qy,xqw->xyw", basis_y, returned.reshape(rows_dev, modes_y, cells), precision=highest
    )
    return row_tail(u_rows, spect, lat_local, depth_modes, depth_local, basis_z)


def solution(mesh):
    placed = (P(("group", "lat"), None, None), P(), P(), P(), P(), P())
    return jax.shard_map(
        shards,
        mesh=mesh,
        in_specs=placed,
        out_specs=P(("group", "lat"), None, None),
        check_vma=False,
    )
```

profile of v0, /device:TPU:15, one launch (start us, length us, event | category | flops | bytes accessed | tf_op | source)
XLA Modules:
  0.0 541.5 jit_solution(5286439165478162498)
XLA Ops:
  0.0 0.0 copy-start
  0.0 0.0 copy-start.1
  0.0 15.1 %convolution_bitcast_fusion = f32[32,64,512]{2,1,0:T(8,128)} fusion(bf16[32,512,512]{2,1,0:T(8,128)(2,1)} %param.6, f32[64]{0:T(128)S(1)} %get-tuple-element.5, f32[512]{0:T(512)S(1)} %iota_add_fusion, f32[64]{0:T(128)S(1)} %get-tuple-element.6), kind=kOutput, calls=%fused_computation.30 | convolution fusion | flops 6442549248 | bytes 20974080 | tf_op jit(solution)/shard_map/qy,xyw->xqw/dot_general | solution.py:51
  15.1 5.6 %all_to_all.24 = f32[32,16,2048]{2,1,0:T(8,128)} reshape(f32[32,64,512]{2,1,0:T(8,128)} %convolution_bitcast_fusion) | data formatting | bytes 8388608 | tf_op jit(solution)/shard_map/all_to_all | solution.py:53
  20.8 6.6 %copy.25 = f32[32,16,2048]{2,0,1:T(8,128)} copy(f32[32,16,2048]{2,1,0:T(8,128)} %all_to_all.24) | data formatting | bytes 8388608 | tf_op jit(solution)/shard_map/all_to_all | solution.py:53
  27.4 6.9 %all-to-all-start = ((f32[32,16,2048]{2,0,1:T(8,128)}), f32[32,16,2048]{2,0,1:T(8,128)}, u32[]{:S(2)}, u32[]{:S(2)}) async-start(f32[32,16,2048]{2,0,1:T(8,128)} %copy.25), calls=%async_computation | async-start | bytes 8388608 | tf_op jit(solution)/shard_map/all_to_all | solution.py:53
  34.3 0.0 copy-done.1
  34.3 0.3 copy.29
  34.7 0.0 copy-done.2
  34.7 0.2 fusion.62
  34.9 91.8 %all-to-all-done = f32[32,16,2048]{2,0,1:T(8,128)} async-done(((f32[32,16,2048]{2,0,1:T(8,128)}), f32[32,16,2048]{2,0,1:T(8,128)}, u32[]{:S(2)}, u32[]{:S(2)}) %all-to-all-start) | async-done | bytes 4194336 | tf_op jit(solution)/shard_map/all_to_all | solution.py:53
  126.6 5.3 copy.26
  132.0 9.0 %fusion.31 = f32[64,128,16]{1,0,2:T(8,128)S(1)} fusion(f32[128,16,512]{2,1,0:T(8,128)} %bitcast.60, f32[128,16]{0,1:T(8,128)S(1)} %fusion.62, f32[64]{0:T(128)S(1)} %get-tuple-element.5, f32[512]{0:T(512)S(1)} %iota_add_fusion, f32[64]{0:T(128)S(1)} %get-tuple-element.6), kind=kOutput, calls=%fused_computation.31 | convolution fusion | flops 805535744 | bytes 4729344 | tf_op jit(solution)/shard_map/dot_general | solution.py:56
  140.9 0.9 fusion.34
  141.8 0.6 copy.30
  142.4 6.9 %fusion.36 = f32[16,32,2048]{2,1,0:T(8,128)} fusion(f32[64,2048,1]{0,1,2:T(8,128)S(1)} %bitcast.61, f32[64]{0:T(128)S(1)} %get-tuple-element.5, f32[16,32]{1,0:T(8,128)S(1)} %add_add_fusion, f32[64]{0:T(128)S(1)} %get-tuple-element.6), kind=kOutput, calls=%fused_computation.34 | convolution fusion | flops 805404672 | bytes 4721152 | tf_op jit(solution)/shard_map/dot_general | solution.py:60
  149.3 5.4 %all-to-all-start.1 = ((f32[16,32,2048]{2,1,0:T(8,128)}), f32[16,32,2048]{2,1,0:T(8,128)}, u32[]{:S(2)}, u32[]{:S(2)}) async-start(f32[16,32,2048]{2,1,0:T(8,128)} %fusion.36), calls=%async_computation.1 | async-start | bytes 8388608 | tf_op jit(solution)/shard_map/all_to_all | solution.py:61
  154.7 22.5 %copy.24 = bf16[32,512,512]{1,2,0:T(8,128)(2,1)} copy(bf16[32,512,512]{2,1,0:T(8,128)(2,1)} %param.6) | data formatting | bytes 33554432 | tf_op args[0]
  177.3 69.8 %all-to-all-done.1 = f32[16,32,2048]{2,1,0:T(8,128)} async-done(((f32[16,32,2048]{2,1,0:T(8,128)}), f32[16,32,2048]{2,1,0:T(8,128)}, u32[]{:S(2)}, u32[]{:S(2)}) %all-to-all-start.1) | async-done | bytes 4194336 | tf_op jit(solution)/shard_map/all_to_all | solution.py:61
  247.1 6.6 %copy.32 = f32[32,16,2048]{2,1,0:T(8,128)} copy(f32[32,16,2048]{2,0,1:T(8,128)} %bitcast.9) | data formatting | bytes 8388608 | tf_op jit(solution)/shard_map/all_to_all | solution.py:61
  253.6 5.2 reshape.105
  258.8 33.1 %fusion.42 = f32[32,512,512]{2,1,0:T(8,128)} fusion(f32[32,64,512]{2,1,0:T(8,128)} %reshape.105, f32[64]{0:T(128)S(1)} %get-tuple-element.5, f32[512]{0:T(512)S(1)} %iota_add_fusion, f32[64]{0:T(128)S(1)} %get-tuple-element.6), kind=kOutput, calls=%fused_computation.40 | convolution fusion | flops 6442549248 | bytes 37751296 | tf_op jit(solution)/shard_map/qy,xqw->xyw/dot_general | solution.py:62
  292.0 0.0 copy-done.3
  292.0 40.9 %fusion.7 = f32[32,512,32,16]{1,3,2,0:T(8,128)} fusion(f32[32,512,32,16]{1,3,2,0:T(8,128)} %bitcast.57, bf16[32,512,32,16]{1,3,2,0:T(8,128)(2,1)} %bitcast.58, f32[16,16]{1,0:T(8,128)S(1)} %copy-done.3), kind=kOutput, calls=%fused_computation.9 | convolution fusion | flops 1702887424 | bytes 83887104 | tf_op jit(solution)/shard_map/xyzc,cd->xyzd/dot_general | solution.py:23
  332.9 36.5 %fusion.26 = f32[32,512,16,16]{1,2,3,0:T(8,128)} fusion(f32[32,512,32,16]{1,3,2,0:T(8,128)} %fusion.7, f32[16]{0:T(128)S(1)} %get-tuple-element.7, f32[32]{0:T(128)S(1)} %iota_add_fusion.1, f32[16]{0:T(128)S(1)} %get-tuple-element.8), kind=kOutput, calls=%fused_computation.27 | convolution fusion | flops 1610614272 | bytes 50331904 | tf_op jit(solution)/shard_map/kz,xyzc->xykc/dot_general | solution.py:24
  369.4 0.0 copy-done
  369.4 37.9 %fusion.23 = f32[32,512,16,16]{1,3,0,2:T(8,128)} fusion(f32[32,512,16,16]{1,2,3,0:T(8,128)} %fusion.26, f32[16,16,16]{2,1,0:T(8,128)S(1)} %copy-done), kind=kOutput, calls=%fused_computation.26 | convolution fusion | flops 805306368 | bytes 33570816 | tf_op jit(solution)/shard_map/xykc,kcd->xykd/dot_general | solution.py:25
  407.2 0.0 copy-start.4
  407.3 42.6 %fusion.19 = f32[32,512,16,32]{1,3,2,0:T(8,128)} fusion(f32[32,512,16,16]{1,3,0,2:T(8,128)} %fusion.23, f32[16]{0:T(128)S(1)} %get-tuple-element.7, f32[32]{0:T(128)S(1)} %iota_add_fusion.1, f32[16]{0:T(128)S(1)} %get-tuple-element.8), kind=kOutput, calls=%fused_computation.22 | convolution fusion | flops 1610614272 | bytes 50331904 | tf_op jit(solution)/shard_map/kz,xykd->xyzd/dot_general | solution.py:26
  449.8 0.0 copy-done.4
  449.8 69.0 %fusion.16 = bf16[32,512,32,16]{1,3,2,0:T(8,128)(2,1)} fusion(f32[32,512,32,16]{1,3,2,0:T(8,128)} %fusion.7, f32[32,512,16,32]{1,3,2,0:T(8,128)} %fusion.19, f32[16,16]{1,0:T(8,128)S(1)} %copy-done.4), kind=kOutput, calls=%fused_computation.18 | convolution fusion | flops 1702887424 | bytes 83887104 | tf_op jit(solution)/shard_map/xyzc,cd->xyzd/dot_general | solution.py:28
  518.8 22.5 %copy.40 = bf16[32,512,512]{2,1,0:T(8,128)(2,1)} copy(bf16[32,512,512]{1,2,0:T(8,128)(2,1)} %bitcast.59) | data formatting | bytes 33554432 | tf_op jit(solution)/shard_map/convert_element_type | solution.py:30
  (8 shorter events, 0.1 us)
Async XLA Ops:
  0.0 369.4 %copy-start = (f32[16,16,16]{2,1,0:T(8,128)S(1)}, f32[16,16,16]{2,1,0:T(8,128)}, u32[]{:S(2)}) copy-start(f32[16,16,16]{2,1,0:T(8,128)} %param.10) | copy-start | bytes 49156
  0.0 34.3 %copy-start.1 = (f32[64,16,16]{0,2,1:T(8,128)S(1)}, f32[64,16,16]{0,2,1:T(8,128)}, u32[]{:S(2)}) copy-start(f32[64,16,16]{0,2,1:T(8,128)} %param.7) | copy-start | bytes 196612
  0.0 34.7 %copy-start.2 = (f32[64,16]{0,1:T(8,128)S(1)}, f32[64,16]{0,1:T(8,128)}, u32[]{:S(2)}) copy-start(f32[64,16]{0,1:T(8,128)} %param.8) | copy-start | bytes 12292
  27.4 99.2 %all-to-all-start = ((f32[32,16,2048]{2,0,1:T(8,128)}), f32[32,16,2048]{2,0,1:T(8,128)}, u32[]{:S(2)}, u32[]{:S(2)}) async-start(f32[32,16,2048]{2,0,1:T(8,128)} %copy.25), calls=%async_computation | async-start | bytes 8388608 | tf_op jit(solution)/shard_map/all_to_all | solution.py:53
  149.3 97.8 %all-to-all-start.1 = ((f32[16,32,2048]{2,1,0:T(8,128)}), f32[16,32,2048]{2,1,0:T(8,128)}, u32[]{:S(2)}, u32[]{:S(2)}) async-start(f32[16,32,2048]{2,1,0:T(8,128)} %fusion.36), calls=%async_computation.1 | async-start | bytes 8388608 | tf_op jit(solution)/shard_map/all_to_all | solution.py:61
  177.2 114.7 %copy-start.3 = (f32[16,16]{1,0:T(8,128)S(1)}, f32[16,16]{1,0:T(8,128)}, u32[]{:S(2)}) copy-start(f32[16,16]{1,0:T(8,128)} %param.9) | copy-start | bytes 3076
  407.2 42.6 %copy-start.4 = (f32[16,16]{1,0:T(8,128)S(1)}, f32[16,16]{1,0:T(8,128)}, u32[]{:S(2)}) copy-start(f32[16,16]{1,0:T(8,128)} %param.11) | copy-start | bytes 3076
where the time goes:
time: 549 us; the launch traced here: 542 us
  matrix products  292 us (53%)
  waiting for transfers between devices  162 us (30%)
  local copies, waits for them, and re-layouts  75.3 us (14%)
  starting transfers between devices  12.4 us (2%)
    all_to_all x1, waiting for transfers between devices, shards(): lax.all_to_all(packed, 'lat', split_axis=1, concat_axis=0, tiled=True)  91.8 us
    all_to_all x1, waiting for transfers between devices, shards(): lax.all_to_all(back_x, 'lat', split_axis=0, concat_axis=1, tiled=True)  69.8 us
    dot_general x1, matrix products, row_tail(): jnp.einsum('xyzc,cd->xyzd', first, depth_local, precision=highest)  69 us
    dot_general x1, matrix products, row_tail(): dspect = jnp.einsum('kz,xykd->xyzd', depth_basis, dmix, precision=highest)  42.6 us
    dot_general x1, matrix products, row_tail(): jnp.einsum('xyzc,cd->xyzd', u4, lat_local, precision=highest)  40.9 us
    dot_general x1, matrix products, row_tail(): dmix = jnp.einsum('xykc,kcd->xykd', dcoef, depth_modes, precision=highest)  37.9 us
    dot_general x1, matrix products, row_tail(): dcoef = jnp.einsum('kz,xyzc->xykc', depth_basis, first, precision=highest)  36.5 us
    dot_general x1, matrix products, shards(): jnp.einsum('qy,xqw->xyw', basis_y, returned.reshape(rows_dev, modes_y, ce...  33.1 us
  transfers between devices with their start and end apart: 2, of which 2 were waited for; matrix products, arithmetic and copies ran while one was open for 4% of the time, Pallas kernels for 0%

commit v1 on v0

--- a/solution.py
+++ b/solution.py
@@ -1,8 +1,13 @@
+import functools
 import math
 
 import jax
 import jax.numpy as jnp
+import ml_dtypes
+import numpy as np
 from jax import lax
+from jax.experimental import pallas as pl
+from jax.experimental.pallas import tpu as pltpu
 from jax.sharding import PartitionSpec as P
 
 
@@ -34,7 +39,7 @@
     return (ids[:, None] == jnp.arange(count, dtype=jnp.int32)[None, :]).astype(jnp.float32)
 
 
-def shards(field, lat_modes, lat_gains, lat_local, depth_modes, depth_local):
+def plain_shards(field, lat_modes, lat_gains, lat_local, depth_modes, depth_local):
     highest = lax.Precision.HIGHEST
     devices = lax.axis_size("lat")
     rows_dev, width_y, cells = field.shape
@@ -65,6 +70,324 @@
     return row_tail(u_rows, spect, lat_local, depth_modes, depth_local, basis_z)
 
 
+BF16 = jnp.bfloat16
+F32 = jnp.float32
+LANE = 128
+GROUP = 8
+SPAN = 256
+TANH_A = 2.0 * math.sqrt(2.0 / math.pi)
+TANH_B = 8.0 * 0.044715 * math.sqrt(2.0 / math.pi)
+
+
+def basis64(length, modes):
+    order = np.arange(modes)[:, None]
+    place = np.arange(length)[None, :]
+    scales = np.where(order == 0, math.sqrt(1.0 / length), math.sqrt(2.0 / length))
+    return np.cos(math.pi * order * (place + 0.5) / length) * scales
+
+
+def split64(array):
+    high = array.astype(ml_dtypes.bfloat16)
+    return high, (array - high.astype(np.float64)).astype(ml_dtypes.bfloat16)
+
+
+def split(array):
+    high = array.astype(BF16)
+    return high, (array - high.astype(F32)).astype(BF16)
+
+
+def split_outside(array):
+    high = lax.reduce_precision(array, 8, 7)
+    return high.astype(BF16), (array - high).astype(BF16)
+
+
+def window_modes(rows, length, modes):
+    place = np.arange(rows) - (rows - 1) / 2
+    order = np.arange(modes)[:, None]
+    _, se, ve = np.linalg.svd(np.cos(math.pi * order * place / length))
+    _, so, vo = np.linalg.svd(np.sin(math.pi * order * place / length))
+    top = max(se[0], so[0])
+    half = rows // 2
+    count = max(int(np.sum(se[:half] > top * 2.0**-24)), int(np.sum(so[:half] > top * 2.0**-24)))
+    fine = max(int(np.sum(se[:half] > top * 0.1)), int(np.sum(so[:half] > top * 0.1)))
+    funcs = np.stack([ve[:count], vo[:count]], axis=1).reshape(2 * count, rows)
+    return funcs, 2 * fine
+
+
+def forward_kernel(funcs, fine, by_ref, u_ref, o_ref, cy_ref):
+    step = pl.program_id(0)
+    block = u_ref.shape[0]
+    rows, modes_y, _ = cy_ref.shape
+    for r in range(block):
+        z = jnp.dot(by_ref[...], u_ref[r], preferred_element_type=F32)
+        cy_ref[step * block + r] = z[:modes_y] + z[modes_y:]
+
+    @pl.when(step == pl.num_programs(0) - 1)
+    def _():
+        halves = cy_ref.shape[2] // SPAN
+        count = funcs.shape[0]
+
+        def compress(g, carry):
+            q0 = pl.multiple_of(g * GROUP, GROUP)
+            for h in range(halves):
+                for k in range(SPAN // LANE):
+                    lanes = slice(h * SPAN + k * LANE, h * SPAN + (k + 1) * LANE)
+                    totals = [None] * count
+                    for t in range(rows // 2):
+                        a = cy_ref[t, pl.ds(q0, GROUP), lanes]
+                        b = cy_ref[rows - 1 - t, pl.ds(q0, GROUP), lanes]
+                        pair = (a + b, a - b)
+                        for j in range(count):
+                            term = pair[j % 2] * float(funcs[j, t])
+                            totals[j] = term if t == 0 else totals[j] + term
+                    place = slice(k * LANE, (k + 1) * LANE)
+                    for j in range(0, count, 2):
+                        high, low = split(jnp.concatenate(totals[j : j + 2], axis=0))
+                        o_ref[g * halves + h, j * GROUP : (j + 2) * GROUP, place] = high
+                        if j < fine:
+                            at = (count + j) * GROUP
+                            o_ref[g * halves + h, at : at + 2 * GROUP, place] = low
+            return carry
+
+        lax.fori_loop(0, modes_y // GROUP, compress, 0)
+
+
+def mix_kernel(count, fine, r_ref, fh_ref, fl_ref, bh_ref, bl_ref, g_ref, wh_ref, wl_ref, o_ref, c_ref, mh_ref, ml_ref):
+    devices, packed, span = r_ref.shape
+    modes_x = wh_ref.shape[0]
+    got = r_ref[...].reshape(devices * packed, span)
+    for at in range(0, modes_x * GROUP, SPAN):
+        part = slice(at, at + SPAN)
+        c_ref[part] = jnp.dot(fh_ref[part], got, preferred_element_type=F32) + jnp.dot(
+            fl_ref[part], got, preferred_element_type=F32
+        )
+    gains = g_ref[...]
+
+    def mix(pair, carry):
+        done = []
+        for p in range(2):
+            at = pl.multiple_of((2 * pair + p) * GROUP, GROUP)
+            coef = c_ref[pl.ds(at, GROUP), :] * gains
+            high, low = split(jnp.concatenate([coef[:, :LANE], coef[:, LANE:]], axis=0))
+            both = jnp.concatenate([high, low], axis=0)
+            z = jnp.dot(both, wh_ref[2 * pair + p], preferred_element_type=F32)
+            z2 = jnp.dot(high, wl_ref[2 * pair + p], preferred_element_type=F32)
+            z = z[: 2 * GROUP] + z[2 * GROUP :] + z2
+            done.append(jnp.concatenate([z[:GROUP], z[GROUP:]], axis=1))
+        high, low = split(jnp.concatenate(done, axis=0))
+        at = pl.multiple_of(pair * 2 * GROUP, 2 * GROUP)
+        mh_ref[pl.ds(at, 2 * GROUP), :] = high
+        ml_ref[pl.ds(at, 2 * GROUP), :] = low
+        return carry
+
+    lax.fori_loop(0, modes_x // 2, mix, 0, unroll=4)
+    right = jnp.concatenate([mh_ref[...], mh_ref[...], ml_ref[...]], axis=0)
+    for i in range(devices):
+        rows = slice(i * count * GROUP, (i + 1) * count * GROUP)
+        left = jnp.concatenate([bh_ref[rows], bl_ref[rows], bh_ref[rows]], axis=1)
+        z = jnp.dot(left, right, preferred_element_type=F32)
+        high, low = split(z)
+        o_ref[i, : count * GROUP] = high
+        o_ref[i, count * GROUP :] = low[: fine * GROUP]
+
+
+def tail_kernel(funcs, fine, yb, r_ref, u_ref, by_ref, l_ref, me_ref, mo_ref, flip_ref, o_ref, b_ref):
+    step = pl.program_id(0)
+    count, rows = funcs.shape
+    modes_y = b_ref.shape[1] // 4
+    flip = flip_ref[...]
+
+    @pl.when(step == 0)
+    def _():
+        halves = b_ref.shape[2] // SPAN
+
+        def expand(g, carry):
+            at = pl.multiple_of(g * 2 * GROUP, 2 * GROUP)
+            for h in range(halves):
+                got = []
+                for k in range(2):
+                    block = r_ref[(2 * g + k) * halves + h]
+                    turned = jnp.dot(block, flip, preferred_element_type=F32) if h else block.astype(F32)
+                    got.append(turned)
+                for c in range(SPAN // LANE):
+                    part = slice(c * LANE, (c + 1) * LANE)
+                    modes = []
+                    for j in range(count):
+                        pieces = []
+                        for k in range(2):
+                            piece = got[k][j * GROUP : (j + 1) * GROUP, part]
+                            if j < fine:
+                                low = got[k][(count + j) * GROUP : (count + j + 1) * GROUP, part]
+                                piece = piece + low
+                            pieces.append(piece)
+                        modes.append(jnp.concatenate(pieces, axis=0))
+                    lanes = slice(h * SPAN + c * LANE, h * SPAN + (c + 1) * LANE)
+                    for t in range(rows // 2):
+                        sums = []
+                        for parity in range(2):
+                            total = modes[parity] * float(0.5 * funcs[parity, t])
+                            for j in range(parity + 2, count, 2):
+                                total = total + modes[j] * float(0.5 * funcs[j, t])
+                            sums.append(total)
+                        for row, value in ((t, sums[0] + sums[1]), (rows - 1 - t, sums[0] - sums[1])):
+                            high, low = split(value)
+                            for n, half in enumerate((high, high, low, low)):
+                                b_ref[row, pl.ds(at + n * modes_y, 2 * GROUP), lanes] = half
+            return carry
+
+        lax.fori_loop(0, modes_y // (2 * GROUP), expand, 0)
+
+    row = step
+    width = u_ref.shape[1]
+    for y0 in range(0, width, yb):
+        ys = slice(y0, y0 + yb)
+        firsts = []
+        for h in range(2):
+            lanes = slice(h * SPAN, (h + 1) * SPAN)
+            u = u_ref[0, ys, lanes]
+            left = jnp.concatenate([by_ref[ys], u, u], axis=1)
+            right = jnp.concatenate([b_ref[row, :, lanes], l_ref[h]], axis=0)
+            x = jnp.dot(left, right, preferred_element_type=F32)
+            seen = jnp.dot(u, flip, preferred_element_type=F32) if h else u.astype(F32)
+            firsts.append(seen + twice_gelu(x))
+        even, odd = firsts[0] + firsts[1], firsts[0] - firsts[1]
+        outs = []
+        for value, w_ref in ((even, me_ref), (odd, mo_ref)):
+            high, low = split(value)
+            left = jnp.concatenate([high, low, high], axis=1)
+            outs.append(jnp.dot(left, w_ref[...], preferred_element_type=F32))
+        near = firsts[0] + twice_gelu(outs[0] + outs[1])
+        far = firsts[1] + twice_gelu(outs[0] - outs[1])
+        o_ref[0, ys, :SPAN] = near.astype(BF16)
+        turned = jnp.dot(far.astype(BF16), flip, preferred_element_type=F32)
+        o_ref[0, ys, SPAN:] = turned.astype(BF16)
+
+
+def twice_gelu(half):
+    return half + half * jnp.tanh(half * (TANH_A + TANH_B * (half * half)))
+
+
+def kron_eye(matrix, count):
+    *lead, n, m = matrix.shape
+    eye = jnp.eye(count, dtype=matrix.dtype)
+    return (eye[:, None, :, None] * matrix[..., None, :, None, :]).reshape(*lead, count * n, count * m)
+
+
+def fits(mesh_lat, rows, width_y, cells, chans, modes_x, modes_y):
+    return (
+        cells == 2 * SPAN
+        and SPAN % (LANE // chans * chans) == 0
+        and mesh_lat * GROUP * SPAN == modes_y * cells
+        and rows % 4 == 0
+        and rows >= 16
+        and width_y % 256 == 0
+        and 4 * modes_y == SPAN
+        and modes_x % 8 == 0
+    )
+
+
+def shards(field, lat_modes, lat_gains, lat_local, depth_modes, depth_local):
+    highest = lax.Precision.HIGHEST
+    devices = lax.axis_size("lat")
+    rows, width_y, cells = field.shape
+    modes_x, chans, _ = lat_modes.shape
+    modes_y = lat_gains.shape[0]
+    modes_z = depth_modes.shape[0]
+    if not fits(devices, rows, width_y, cells, chans, modes_x, modes_y):
+        return plain_shards(field, lat_modes, lat_gains, lat_local, depth_modes, depth_local)
+    depth = cells // chans
+    width_x = rows * devices
+    basis_x = basis64(width_x, modes_x)
+    basis_y = basis64(width_y, modes_y)
+    basis_z = basis64(depth, modes_z)
+    funcs, fine = window_modes(rows, width_x, modes_x)
+    count = funcs.shape[0]
+    packed = (count + fine) * GROUP
+    halves = cells // SPAN
+    me = lax.axis_index("lat")
+
+    by_high, by_low = split64(basis_y)
+    by_forward = np.concatenate([by_high, by_low], axis=0)
+    block = 4
+    sent = pl.pallas_call(
+        functools.partial(forward_kernel, funcs, fine),
+        grid=(rows // block,),
+        in_specs=[
+            pl.BlockSpec((2 * modes_y, width_y), lambda s: (0, 0)),
+            pl.BlockSpec((block, width_y, cells), lambda s: (s, 0, 0)),
+        ],
+        out_specs=pl.BlockSpec((devices, packed, SPAN), lambda s: (0, 0, 0)),
+        out_shape=jax.ShapeDtypeStruct((devices, packed, SPAN), BF16),
+        scratch_shapes=[pltpu.VMEM((rows, modes_y, cells), F32)],
+        compiler_params=pltpu.CompilerParams(vmem_limit_bytes=48 * 2**20),
+        name="forward",
+    )(by_forward, field)
+    gathered = lax.all_to_all(sent, "lat", split_axis=0, concat_axis=0, tiled=True)
+
+    weights = np.einsum("pit,jt->pij", basis_x.reshape(modes_x, devices, rows), funcs)
+    eye = np.eye(GROUP)
+
+    def spread(array):
+        n, m = array.shape
+        return (array[:, None, :, None] * eye[None, :, None, :]).reshape(n * GROUP, m * GROUP)
+
+    both = np.concatenate([weights, weights[:, :, :fine]], axis=2)
+    fh, fl = split64(spread(both.reshape(modes_x, devices * (count + fine))))
+    bh, bl = split64(spread(weights.reshape(modes_x, devices * count).T))
+    gains = lax.dynamic_slice_in_dim(lat_gains, (me // halves) * GROUP, GROUP, axis=0)
+    gains = jnp.tile(gains, (1, SPAN // chans))
+    wh, wl = split_outside(kron_eye(lat_modes, LANE // chans))
+    mixed = pl.pallas_call(
+        functools.partial(mix_kernel, count, fine),
+        out_shape=jax.ShapeDtypeStruct((devices, packed, SPAN), BF16),
+        scratch_shapes=[
+            pltpu.VMEM((modes_x * GROUP, SPAN), F32),
+            pltpu.VMEM((modes_x * GROUP, SPAN), BF16),
+            pltpu.VMEM((modes_x * GROUP, SPAN), BF16),
+        ],
+        compiler_params=pltpu.CompilerParams(vmem_limit_bytes=48 * 2**20),
+        name="mix",
+    )(gathered, fh, fl, bh, bl, gains, wh, wl)
+    returned = lax.all_to_all(mixed, "lat", split_axis=0, concat_axis=0, tiled=True)
+
+    by_back = np.concatenate([by_high, by_low, by_high, by_low], axis=0).T.copy()
+    per = SPAN // chans
+    flip = np.kron(np.eye(per)[::-1], np.eye(chans)).astype(ml_dtypes.bfloat16)
+    local_high, local_low = split_outside(kron_eye(0.5 * lat_local, per))
+    local = jnp.concatenate([local_high, local_low], axis=0)
+    turned = local.reshape(2 * SPAN, per, chans)[:, ::-1].reshape(2 * SPAN, SPAN)
+    local = jnp.stack([local, turned])
+    near_z = basis_z[:, :per].astype(np.float32)
+
+    def depth_matrix(parity):
+        b = near_z[parity::2]
+        full = 0.5 * jnp.einsum(
+            "kz,kw,kcd->zcwd", b, b, depth_modes[parity::2], precision=highest
+        ).reshape(SPAN, SPAN) + 0.25 * kron_eye(depth_local, per)
+        high, low = split_outside(full)
+        return jnp.concatenate([high, high, low], axis=0)
+
+    yb = 256
+    return pl.pallas_call(
+        functools.partial(tail_kernel, funcs, fine, yb),
+        grid=(rows,),
+        in_specs=[
+            pl.BlockSpec((devices, packed, SPAN), lambda s: (0, 0, 0)),
+            pl.BlockSpec((1, width_y, cells), lambda s: (s, 0, 0)),
+            pl.BlockSpec((width_y, SPAN), lambda s: (0, 0)),
+            pl.BlockSpec((2, 2 * SPAN, SPAN), lambda s: (0, 0, 0)),
+            pl.BlockSpec((3 * SPAN, SPAN), lambda s: (0, 0)),
+            pl.BlockSpec((3 * SPAN, SPAN), lambda s: (0, 0)),
+            pl.BlockSpec((SPAN, SPAN), lambda s: (0, 0)),
+        ],
+        out_specs=pl.BlockSpec((1, width_y, cells), lambda s: (s, 0, 0)),
+        out_shape=jax.ShapeDtypeStruct(field.shape, BF16),
+        scratch_shapes=[pltpu.VMEM((rows, 4 * modes_y, cells), BF16)],
+        compiler_params=pltpu.CompilerParams(vmem_limit_bytes=48 * 2**20),
+        name="tail",
+    )(returned, field, by_back, local, depth_matrix(0), depth_matrix(1), flip)
+
+
 def solution(mesh):
     placed = (P(("group", "lat"), None, None), P(), P(), P(), P(), P())
     return jax.shard_map(

time: 549 us -> 161 us (0.29); the launches traced: 542 us -> 161 us
  matrix products: 292 us -> 4.39 us
  waiting for transfers between devices: 162 us -> 26.7 us
  Pallas kernels: 0 us -> 87.1 us
  local copies, waits for them, and re-layouts: 75.3 us -> 22.7 us
  other arithmetic: 0.05 us -> 8.07 us
    dot_general x11 -> x2, matrix products: 292 us -> 4.39 us  [depth_matrix(): jnp.einsum('kz,kw,kcd->zcwd', b, b, depth_modes[parity::2], precision=hig...]
    all_to_all x2, waiting for transfers between devices: 162 us -> 26.7 us  [the longest x1 14.3 us: shards(): lax.all_to_all(mixed, 'lat', split_axis=0, concat_axis=0, tiled=True)]
    pallas_call x0 -> x3, Pallas kernels: none -> 87.1 us  [the longest x1 63.6 us: shards(): pl.pallas_call(functools.partial(tail_kernel, funcs, fine, yb), grid=(row...]
    convert_element_type x1 -> x0, local copies, waits for them, and re-layouts: 22.5 us -> none  [row_tail(): return final.reshape(rows, width, cells).astype(jnp.bfloat16)]
    unnamed x12 -> x32, local copies, waits for them, and re-layouts: 22.8 us -> 0.99 us
    all_to_all x3 -> x0, local copies, waits for them, and re-layouts: 18.8 us -> none  [the longest x2 12.3 us: shards(): lax.all_to_all(packed, 'lat', split_axis=1, concat_axis=0, tiled=True)]
    mul x0 -> x11, local copies, waits for them, and re-layouts: none -> 15 us  [the longest x10 15 us: kron_eye(): eye[:, None, :, None] * matrix[..., None, :, None, :]]
    convert_element_type x0 -> x7, other arithmetic: none -> 6.73 us  [the longest x5 6.72 us: split_outside(): return (high.astype(BF16), (array - high).astype(BF16))]
  transfers between devices with their start and end apart: 2 -> 2, of which waited for: 2 -> 2; matrix products, arithmetic and copies ran while one was open for 4% -> 21% of each run, Pallas kernels for 0% -> 0%
where the time goes in v1:
time: 161 us
  Pallas kernels  87.1 us (54%)
  waiting for transfers between devices  26.7 us (17%)
  local copies, waits for them, and re-layouts  22.7 us (14%)
  starting transfers between devices  11.8 us (7%)
  other arithmetic  8.07 us (5%)
  matrix products  4.39 us (3%)
    pallas_call x1, Pallas kernels, shards(): pl.pallas_call(functools.partial(tail_kernel, funcs, fine, yb), grid=(row...  63.6 us
    mul x10, local copies, waits for them, and re-layouts, kron_eye(): eye[:, None, :, None] * matrix[..., None, :, None, :]  15 us
    all_to_all x1, waiting for transfers between devices, shards(): lax.all_to_all(mixed, 'lat', split_axis=0, concat_axis=0, tiled=True)  14.3 us
    pallas_call x1, Pallas kernels, shards(): pl.pallas_call(functools.partial(forward_kernel, funcs, fine), grid=(rows...  12.7 us
    all_to_all x1, waiting for transfers between devices, shards(): lax.all_to_all(sent, 'lat', split_axis=0, concat_axis=0, tiled=True)  12.4 us
    pallas_call x1, Pallas kernels, shards(): pl.pallas_call(functools.partial(mix_kernel, count, fine), out_shape=jax....  10.8 us
    convert_element_type x5, other arithmetic, split_outside(): return (high.astype(BF16), (array - high).astype(BF16))  6.72 us
    all_to_all x1, starting transfers between devices, shards(): lax.all_to_all(sent, 'lat', split_axis=0, concat_axis=0, tiled=True)  6.69 us
  transfers between devices with their start and end apart: 2, of which 2 were waited for; matrix products, arithmetic and copies ran while one was open for 21% of the time, Pallas kernels for 0%

profile of v1, /device:TPU:15, one launch (start us, length us, event | category | flops | bytes accessed | tf_op | source)
XLA Modules:
  0.0 160.9 jit_solution(3679634715568816124)
XLA Ops:
  0.0 0.9 copy-done.5
  0.9 12.7 %forward.1 = bf16[16,160,256]{2,1,0:T(8,128)(2,1)} custom-call(bf16[128,512]{1,0:T(8,128)(2,1)S(1)} %copy-done.5, bf16[32,512,512]{2,1,0:T(8,128)(2,1)} %u_ref.3), custom_call_target="tpu_custom_call" | custom-call | tf_op jit(solution)/shard_map/forward/pallas_call | solution.py:312
  13.6 6.7 %all-to-all-start = ((bf16[16,160,256]{2,1,0:T(8,128)(2,1)}), bf16[16,160,256]{2,1,0:T(8,128)(2,1)S(1)}, u32[]{:S(2)}, u32[]{:S(2)}) async-start(bf16[16,160,256]{2,1,0:T(8,128)(2,1)} %forward.1), calls=%async_computation | async-start | bytes 2621440 | tf_op jit(solution)/shard_map/all_to_all | solution.py:325
  20.3 0.1 constant_dynamic-slice_fusion
  20.4 0.1 copy.28
  20.4 0.1 copy.31
  20.5 0.1 tile.10.g_ref
  20.6 0.1 mul.120
  20.8 0.1 mul.116
  20.9 0.1 mul.117
  21.0 0.1 mul.104
  21.1 0.2 mul.105
  21.3 4.3 %mul.107 = f32[64,8,16,8,16]{0,4,3,2,1:T(8,128)} broadcast(f32[64,16,16]{0,2,1:T(8,128)S(1)} %copy-done.8), dimensions={0,2,4} | broadcast | bytes 4259840 | tf_op jit(solution)/shard_map/mul | solution.py:273
  25.6 7.3 %copy.29 = f32[64,128,128]{2,1,0:T(8,128)} copy(f32[64,128,128]{0,2,1:T(8,128)} %bitcast.36) | data formatting | bytes 8388608 | tf_op jit(solution)/shard_map/mul | solution.py:273
  32.9 5.6 %fusion = (bf16[64,128,128]{2,1,0:T(8,128)(2,1)}, bf16[64,128,128]{2,1,0:T(8,128)(2,1)}) fusion(f32[64,128,128]{2,1,0:T(8,128)} %copy.29, f32[128,128]{1,0:T(8,128)S(1)} %mul.105), kind=kLoop, calls=%fused_computation.2 | loop fusion | flops 5242880 | bytes 8454144 | tf_op jit(solution)/shard_map/convert_element_type | solution.py:101
  38.5 12.4 %all-to-all-done.r_ref = bf16[16,160,256]{2,1,0:T(8,128)(2,1)S(1)} async-done(((bf16[16,160,256]{2,1,0:T(8,128)(2,1)}), bf16[16,160,256]{2,1,0:T(8,128)(2,1)S(1)}, u32[]{:S(2)}, u32[]{:S(2)}) %all-to-all-start) | async-done | bytes 1310752 | tf_op jit(solution)/shard_map/all_to_all | solution.py:325
  50.9 10.8 %mix.1 = bf16[16,160,256]{2,1,0:T(8,128)(2,1)} custom-call(bf16[16,160,256]{2,1,0:T(8,128)(2,1)S(1)} %all-to-all-done.r_ref, bf16[512,2560]{1,0:T(8,128)(2,1)} %constant.47.clone.fh_ref, bf16[512,2560]{1,0:T(8,128)(2,1)} %constant.48.clone.fl_ref, bf16[1792,512]{1,0:T(8,128)(2,1)S(1)} %copy-done.2, bf16[1792,512]{1,0:T(8,128)(2,1)} %constant.50.clone.bl_ref, ...), custom_call_target="tpu_custom_call" | custom-call | tf_op jit(solution)/shard_map/mix/pallas_call | solution.py:340
  61.7 5.1 %all-to-all-start.1 = ((bf16[16,160,256]{2,1,0:T(8,128)(2,1)}), bf16[16,160,256]{2,1,0:T(8,128)(2,1)S(1)}, u32[]{:S(2)}, u32[]{:S(2)}) async-start(bf16[16,160,256]{2,1,0:T(8,128)(2,1)} %mix.1), calls=%async_computation.1 | async-start | bytes 2621440 | tf_op jit(solution)/shard_map/all_to_all | solution.py:351
  66.9 0.8 copy.32
  67.8 2.2 %bitcast_add_fusion = f32[16,16,16,16]{3,0,1,2:T(8,128)S(1)} fusion(f32[16,16]{1,0:T(8,128)S(1)} %copy-done.11, f32[16,16]{0,1:T(8,128)S(1)} %fusion.13, f32[8,16,16]{2,1,0:T(8,128)S(1)} %get-tuple-element.13, f32[8,16]{1,0:T(8,128)S(1)} %copy-done.15, f32[8,16]{0,1:T(8,128)S(1)} %copy-done.13), kind=kOutput, calls=%fused_computation.3 | convolution fusion | flops 6555648 | bytes 273408 | tf_op jit(solution)/shard_map/kz,kw,kcd->zcwd/dot_general | solution.py:364
  70.0 1.2 copy.38
  71.2 1.6 add.20
  72.8 2.2 %bitcast_add_fusion.1 = f32[16,16,16,16]{3,0,1,2:T(8,128)S(1)} fusion(f32[16,16]{1,0:T(8,128)S(1)} %copy-done.11, f32[16,16]{0,1:T(8,128)S(1)} %fusion.13, f32[8,16,16]{2,1,0:T(8,128)S(1)} %get-tuple-element.14, f32[8,16]{1,0:T(8,128)S(1)} %copy-done.14, f32[8,16]{0,1:T(8,128)S(1)} %copy-done.12), kind=kOutput, calls=%fused_computation.4 | convolution fusion | flops 6555648 | bytes 273408 | tf_op jit(solution)/shard_map/kz,kw,kcd->zcwd/dot_general | solution.py:364
  75.0 1.2 copy.35
  76.2 1.5 add.18
  77.7 0.2 broadcast_multiply_fusion
  77.9 1.2 copy.30
  79.2 1.5 mul.115
  80.7 1.0 reduce-precision_convert_fusion.4
  81.8 1.0 pad_maximum_fusion.l_ref
  83.0 14.3 %all-to-all-done.1.r_ref = bf16[16,160,256]{2,1,0:T(8,128)(2,1)S(1)} async-done(((bf16[16,160,256]{2,1,0:T(8,128)(2,1)}), bf16[16,160,256]{2,1,0:T(8,128)(2,1)S(1)}, u32[]{:S(2)}, u32[]{:S(2)}) %all-to-all-start.1) | async-done | bytes 1310752 | tf_op jit(solution)/shard_map/all_to_all | solution.py:351
  97.3 63.6 %tail.1 = bf16[32,512,512]{2,1,0:T(8,128)(2,1)} custom-call(bf16[16,160,256]{2,1,0:T(8,128)(2,1)S(1)} %all-to-all-done.1.r_ref, bf16[32,512,512]{2,1,0:T(8,128)(2,1)} %u_ref.3, bf16[512,256]{1,0:T(8,128)(2,1)S(1)} %copy-done.3, bf16[2,512,256]{2,1,0:T(8,128)(2,1)S(1)} %pad_maximum_fusion.l_ref, bf16[768,256]{1,0:T(8,128)(2,1)S(1)} %get-tuple-element.17.me_ref, ...), custom_call_target="tpu_custom_call" | custom-call | tf_op jit(solution)/shard_map/tail/pallas_call | solution.py:371
  (44 shorter events, 0.3 us)
Async XLA Ops:
  0.0 20.3 %copy-start = (f32[64,16]{0,1:T(8,128)S(1)}, f32[64,16]{0,1:T(8,128)}, u32[]{:S(2)}) copy-start(f32[64,16]{0,1:T(8,128)} %param.19) | copy-start | bytes 12292
  0.0 0.9 copy-start.5
  13.6 6.8 %copy-start.10 = (f32[16,16]{1,0:T(8,128)S(1)}, f32[16,16]{1,0:T(8,128)}, u32[]{:S(2)}) copy-start(f32[16,16]{1,0:T(8,128)} %param.20) | copy-start | bytes 3076
  13.6 7.7 %copy-start.8 = (f32[64,16,16]{0,2,1:T(8,128)S(1)}, f32[64,16,16]{0,2,1:T(8,128)}, u32[]{:S(2)}) copy-start(f32[64,16,16]{0,2,1:T(8,128)} %param.18) | copy-start | bytes 196612
  13.6 37.3 %all-to-all-start = ((bf16[16,160,256]{2,1,0:T(8,128)(2,1)}), bf16[16,160,256]{2,1,0:T(8,128)(2,1)S(1)}, u32[]{:S(2)}, u32[]{:S(2)}) async-start(bf16[16,160,256]{2,1,0:T(8,128)(2,1)} %forward.1), calls=%async_computation | async-start | bytes 2621440 | tf_op jit(solution)/shard_map/all_to_all | solution.py:325
  32.9 17.9 %copy-start.2 = (bf16[1792,512]{1,0:T(8,128)(2,1)S(1)}, bf16[1792,512]{1,0:T(8,128)(2,1)}, u32[]{:S(2)}) copy-start(bf16[1792,512]{1,0:T(8,128)(2,1)} %constant.49.clone.bh_ref) | copy-start | bytes 5505028
  61.7 6.0 %copy-start.9 = (f32[16,16,16]{2,1,0:T(8,128)S(1)}, f32[16,16,16]{2,1,0:T(8,128)}, u32[]{:S(2)}) copy-start(f32[16,16,16]{2,1,0:T(8,128)} %param.21) | copy-start | bytes 49156
  61.7 6.0 %copy-start.11 = (f32[16,16]{1,0:T(8,128)S(1)}, f32[16,16]{1,0:T(8,128)}, u32[]{:S(2)}) copy-start(f32[16,16]{1,0:T(8,128)} %param.22) | copy-start | bytes 3076
  61.7 6.1 %copy-start.13 = (f32[8,16]{0,1:T(8,128)S(1)}, f32[8,16]{0,1:T(8,128)}, u32[]{:S(2)}) copy-start(f32[8,16]{0,1:T(8,128)} %constant.56) | copy-start | bytes 1540
  61.7 6.1 %copy-start.15 = (f32[8,16]{1,0:T(8,128)S(1)}, f32[8,16]{1,0:T(8,128)}, u32[]{:S(2)}) copy-start(f32[8,16]{1,0:T(8,128)} %constant.52.clone) | copy-start | bytes 1540
  61.7 35.6 %all-to-all-start.1 = ((bf16[16,160,256]{2,1,0:T(8,128)(2,1)}), bf16[16,160,256]{2,1,0:T(8,128)(2,1)S(1)}, u32[]{:S(2)}, u32[]{:S(2)}) async-start(bf16[16,160,256]{2,1,0:T(8,128)(2,1)} %mix.1), calls=%async_computation.1 | async-start | bytes 2621440 | tf_op jit(solution)/shard_map/all_to_all | solution.py:351
  71.2 1.6 copy-start.12
  71.2 1.6 copy-start.14
  80.7 2.1 %copy-start.6 = (f32[256,256]{1,0:T(8,128)S(1)}, f32[256,256]{1,0:T(8,128)}, u32[]{:S(2)}) copy-start(f32[256,256]{1,0:T(8,128)} %add.20) | copy-start | bytes 786436
  80.7 2.2 %copy-start.7 = (f32[256,256]{1,0:T(8,128)S(1)}, f32[256,256]{1,0:T(8,128)}, u32[]{:S(2)}) copy-start(f32[256,256]{1,0:T(8,128)} %add.18) | copy-start | bytes 786436
  81.8 15.6 %copy-start.3 = (bf16[512,256]{1,0:T(8,128)(2,1)S(1)}, bf16[512,256]{1,0:T(8,128)(2,1)}, u32[]{:S(2)}) copy-start(bf16[512,256]{1,0:T(8,128)(2,1)} %constant.53.clone.by_ref) | copy-start | bytes 786436
  81.8 15.6 %copy-start.4 = (bf16[256,256]{1,0:T(8,128)(2,1)S(1)}, bf16[256,256]{1,0:T(8,128)(2,1)}, u32[]{:S(2)}) copy-start(bf16[256,256]{1,0:T(8,128)(2,1)} %constant.54.clone.flip_ref) | copy-start | bytes 393220
  97.3 63.6 %copy-start.1 = (f32[64,16]{0,1:T(8,128)S(1)}, f32[64,16]{0,1:T(8,128)}, u32[]{:S(2)}) copy-start(f32[64,16]{0,1:T(8,128)} %param.19) | copy-start | bytes 12292

commit v2 on v0

--- a/solution.py
+++ b/solution.py
@@ -1,8 +1,13 @@
+import functools
 import math
 
 import jax
 import jax.numpy as jnp
+import ml_dtypes
+import numpy as np
 from jax import lax
+from jax.experimental import pallas as pl
+from jax.experimental.pallas import tpu as pltpu
 from jax.sharding import PartitionSpec as P
 
 
@@ -34,7 +39,7 @@
     return (ids[:, None] == jnp.arange(count, dtype=jnp.int32)[None, :]).astype(jnp.float32)
 
 
-def shards(field, lat_modes, lat_gains, lat_local, depth_modes, depth_local):
+def plain_shards(field, lat_modes, lat_gains, lat_local, depth_modes, depth_local):
     highest = lax.Precision.HIGHEST
     devices = lax.axis_size("lat")
     rows_dev, width_y, cells = field.shape
@@ -65,6 +70,393 @@
     return row_tail(u_rows, spect, lat_local, depth_modes, depth_local, basis_z)
 
 
+BF16 = jnp.bfloat16
+F32 = jnp.float32
+LANE = 128
+GROUP = 8
+SPAN = 256
+TANH_A = 2.0 * math.sqrt(2.0 / math.pi)
+TANH_B = 8.0 * 0.044715 * math.sqrt(2.0 / math.pi)
+
+
+def basis64(length, modes):
+    order = np.arange(modes)[:, None]
+    place = np.arange(length)[None, :]
+    scales = np.where(order == 0, math.sqrt(1.0 / length), math.sqrt(2.0 / length))
+    return np.cos(math.pi * order * (place + 0.5) / length) * scales
+
+
+def split64(array):
+    high = array.astype(ml_dtypes.bfloat16)
+    return high, (array - high.astype(np.float64)).astype(ml_dtypes.bfloat16)
+
+
+def split(array):
+    high = array.astype(BF16)
+    return high, (array - high.astype(F32)).astype(BF16)
+
+
+def split_outside(array):
+    high = lax.reduce_precision(array, 8, 7)
+    return high.astype(BF16), (array - high).astype(BF16)
+
+
+def window_modes(rows, length, modes):
+    place = np.arange(rows) - (rows - 1) / 2
+    order = np.arange(modes)[:, None]
+    _, se, ve = np.linalg.svd(np.cos(math.pi * order * place / length))
+    _, so, vo = np.linalg.svd(np.sin(math.pi * order * place / length))
+    top = max(se[0], so[0])
+    half = rows // 2
+    count = max(int(np.sum(se[:half] > top * 2.0**-24)), int(np.sum(so[:half] > top * 2.0**-24)))
+    fine = max(int(np.sum(se[:half] > top * 0.1)), int(np.sum(so[:half] > top * 0.1)))
+    funcs = np.stack([ve[:count], vo[:count]], axis=1).reshape(2 * count, rows)
+    return funcs, 2 * fine
+
+
+def forward_kernel(funcs, fine, by_ref, near_ref, far_ref, o_ref, cy_ref, acc_ref):
+    step = pl.program_id(0)
+    pairs = near_ref.shape[0]
+    steps = funcs.shape[1] // (2 * pairs)
+    modes_y = by_ref.shape[0] // 2
+    count = funcs.shape[0]
+    halves = cy_ref.shape[2] // SPAN
+
+    def compress(before):
+        for g in range(modes_y // GROUP):
+            rows = slice(g * GROUP, (g + 1) * GROUP)
+            for c in range(halves * SPAN // LANE):
+                lanes = slice(c * LANE, (c + 1) * LANE)
+                totals = [None if before == 0 else acc_ref[j, rows, lanes] for j in range(count)]
+                for r in range(pairs):
+                    x, y = cy_ref[r, rows, lanes], cy_ref[pairs + r, rows, lanes]
+                    pair = (x + y, x - y)
+                    for j in range(count):
+                        term = pair[j % 2] * float(funcs[j, before * pairs + r])
+                        totals[j] = term if totals[j] is None else totals[j] + term
+                if before < steps - 1:
+                    for j in range(count):
+                        acc_ref[j, rows, lanes] = totals[j]
+                    continue
+                h, k = divmod(c, SPAN // LANE)
+                place = slice(k * LANE, (k + 1) * LANE)
+                for j in range(0, count, 2):
+                    high, low = split(jnp.concatenate(totals[j : j + 2], axis=0))
+                    o_ref[g * halves + h, j * GROUP : (j + 2) * GROUP, place] = high
+                    if j < fine:
+                        at = (count + j) * GROUP
+                        o_ref[g * halves + h, at : at + 2 * GROUP, place] = low
+
+    def body(at):
+        if at > 0:
+            compress(at - 1)
+        if at < steps:
+            for r in range(pairs):
+                for slot, row in ((r, near_ref[r]), (pairs + r, far_ref[pairs - 1 - r])):
+                    z = jnp.dot(by_ref[...], row, preferred_element_type=F32)
+                    cy_ref[slot] = z[:modes_y] + z[modes_y:]
+
+    for at in range(steps + 1):
+        pl.when(step == at)(functools.partial(body, at))
+
+
+def mix_kernel(count, fine, r_ref, a_ref, b_ref, g_ref, w_ref, o_ref, m_ref, back_ref):
+    devices, packed, span = r_ref.shape
+    modes_x = w_ref.shape[1]
+    depth = a_ref.shape[1]
+    highs, lows = count * GROUP, fine * GROUP
+    tiles = [(k, slice(k * LANE, (k + 1) * LANE)) for k in range(span // LANE)]
+    for i in range(devices):
+        got = r_ref[i].astype(F32)
+        for k, lanes in tiles:
+            m_ref[k, i * highs : i * highs + lows] = got[:lows, lanes] + got[highs:, lanes]
+            m_ref[k, i * highs + lows : (i + 1) * highs] = got[lows:highs, lanes]
+    if depth > devices * count:
+        for k, _ in tiles:
+            m_ref[k, devices * highs :] = jnp.zeros((depth * GROUP - devices * highs, LANE), F32)
+    shifts = w_ref.shape[0]
+    for q in range(GROUP):
+        modes = [m_ref[k, pl.ds(q, depth, stride=GROUP), :] for k, _ in tiles]
+        high, low = split(jnp.concatenate(modes, axis=1))
+        z = jnp.dot(a_ref[...], jnp.concatenate([high, low], axis=1), preferred_element_type=F32)
+        coef = z[:modes_x, :span] + z[modes_x:, :span] + z[:modes_x, span:]
+        coef = coef * g_ref[q : q + 1, :]
+        mixed = []
+        for k, lanes in tiles:
+            part = coef[:, lanes]
+            total = part * w_ref[shifts // 2]
+            for n in range(shifts):
+                shift = n - shifts // 2
+                if shift:
+                    total = total + pltpu.roll(part, shift % LANE, 1) * w_ref[n]
+            mixed.append(total)
+        high, low = split(jnp.concatenate(mixed, axis=1))
+        right = jnp.concatenate([high, high, low, low], axis=0)
+        z = jnp.dot(b_ref[...], right, preferred_element_type=F32)
+        for k, lanes in tiles:
+            back_ref[k, pl.ds(q, devices * count, stride=GROUP), :] = z[:, lanes]
+    for i in range(devices):
+        for k, lanes in tiles:
+            high, low = split(back_ref[k, i * highs : (i + 1) * highs])
+            o_ref[i, :highs, lanes] = high
+            o_ref[i, highs:, lanes] = low[:lows]
+
+
+def expand(funcs, fine, r_ref, flip_ref, b_ref):
+    count, rows = funcs.shape
+    modes_y = b_ref.shape[1] // 4
+    halves = b_ref.shape[2] // SPAN
+    flip = flip_ref[...]
+
+    def some(g, carry):
+        at = pl.multiple_of(g * 2 * GROUP, 2 * GROUP)
+        for h in range(halves):
+            got = []
+            for k in range(2):
+                block = r_ref[(2 * g + k) * halves + h]
+                turned = jnp.dot(block, flip, preferred_element_type=F32) if h else block.astype(F32)
+                got.append(turned)
+            for c in range(SPAN // LANE):
+                part = slice(c * LANE, (c + 1) * LANE)
+                modes = []
+                for j in range(count):
+                    pieces = []
+                    for k in range(2):
+                        piece = got[k][j * GROUP : (j + 1) * GROUP, part]
+                        if j < fine:
+                            low = got[k][(count + j) * GROUP : (count + j + 1) * GROUP, part]
+                            piece = piece + low
+                        pieces.append(piece)
+                    modes.append(jnp.concatenate(pieces, axis=0))
+                lanes = slice(h * SPAN + c * LANE, h * SPAN + (c + 1) * LANE)
+                for t in range(rows // 2):
+                    sums = []
+                    for parity in range(2):
+                        total = modes[parity] * float(0.5 * funcs[parity, t])
+                        for j in range(parity + 2, count, 2):
+                            total = total + modes[j] * float(0.5 * funcs[j, t])
+                        sums.append(total)
+                    for row, value in ((t, sums[0] + sums[1]), (rows - 1 - t, sums[0] - sums[1])):
+                        high, low = split(value)
+                        for n, half in enumerate((high, high, low, low)):
+                            b_ref[row, pl.ds(at + n * modes_y, 2 * GROUP), lanes] = half
+        return carry
+
+    lax.fori_loop(0, modes_y // (2 * GROUP), some, 0)
+
+
+def tail_kernel(funcs, fine, chunk, r_ref, u_ref, by_ref, l_ref, w_ref, flip_ref, o_ref, b_ref, *scratch):
+    step = pl.program_id(0)
+    last = pl.num_programs(0) - 1
+    width = u_ref.shape[1]
+    pre, seen, first, parts, post, done = (scratch[n : n + 2] for n in range(0, 12, 2))
+    near, far = slice(0, SPAN), slice(SPAN, 2 * SPAN)
+    chunks = [slice(y, y + chunk) for y in range(0, width, chunk)]
+
+    def lateral_product(n):
+        for h, lanes in enumerate((near, far)):
+            u = u_ref[n, :, lanes]
+            left = jnp.concatenate([by_ref[...], u, u], axis=1)
+            right = jnp.concatenate([b_ref[2 * step + n, :, lanes], l_ref[h]], axis=0)
+            pre[n][:, lanes] = jnp.dot(left, right, preferred_element_type=F32)
+        seen[n][...] = jnp.dot(u, flip_ref[...], preferred_element_type=F32)
+
+    def lateral_points(n):
+        for ys in chunks:
+            f0 = u_ref[n, ys, near].astype(F32) + twice_gelu(pre[n][ys, near])
+            f1 = seen[n][ys] + twice_gelu(pre[n][ys, far])
+            first[n][ys, near] = f0
+            first[n][ys, far] = f1
+            for m, value in enumerate((f0 + f1, f0 - f1)):
+                high, low = split(value)
+                parts[n][ys, 2 * m * SPAN : (2 * m + 1) * SPAN] = high
+                parts[n][ys, (2 * m + 1) * SPAN : (2 * m + 2) * SPAN] = low
+
+    def depth_product(n):
+        for m, lanes in enumerate((near, far)):
+            high = parts[n][:, 2 * m * SPAN : (2 * m + 1) * SPAN]
+            low = parts[n][:, (2 * m + 1) * SPAN : (2 * m + 2) * SPAN]
+            left = jnp.concatenate([high, low, high], axis=1)
+            post[n][:, lanes] = jnp.dot(left, w_ref[m], preferred_element_type=F32)
+
+    def depth_points(n):
+        for ys in chunks:
+            even, odd = post[n][ys, near], post[n][ys, far]
+            o_ref[n, ys, near] = (first[n][ys, near] + twice_gelu(even + odd)).astype(BF16)
+            done[n][ys] = (first[n][ys, far] + twice_gelu(even - odd)).astype(BF16)
+
+    def finish(n):
+        o_ref[n, :, far] = jnp.dot(done[n][...], flip_ref[...], preferred_element_type=F32).astype(BF16)
+
+    @pl.when(step == 0)
+    def _():
+        expand(funcs, fine, r_ref, flip_ref, b_ref)
+        lateral_product(0)
+        lateral_product(1)
+        lateral_points(0)
+        depth_product(0)
+        lateral_points(1)
+
+    @pl.when(jnp.logical_and(step > 0, step < last))
+    def _():
+        depth_product(1)
+        depth_points(0)
+        lateral_product(0)
+        depth_points(1)
+        finish(0)
+        lateral_product(1)
+        lateral_points(0)
+        finish(1)
+        depth_product(0)
+        lateral_points(1)
+
+    @pl.when(step == last)
+    def _():
+        depth_product(1)
+        depth_points(0)
+        finish(0)
+        depth_points(1)
+        finish(1)
+
+
+def twice_gelu(half):
+    return half + half * jnp.tanh(half * (TANH_A + TANH_B * (half * half)))
+
+
+def diagonals(matrices):
+    p, n, _ = matrices.shape
+    turned = jnp.pad(jnp.swapaxes(matrices, 1, 2)[:, :, ::-1], ((0, 0), (0, 0), (0, n)))
+    skewed = turned.reshape(p, 2 * n * n)[:, : n * (2 * n - 1)].reshape(p, n, 2 * n - 1)
+    return jnp.tile(jnp.transpose(skewed, (2, 0, 1)), (1, 1, LANE // n))
+
+
+def kron_eye(matrix, count):
+    *lead, n, m = matrix.shape
+    eye = jnp.eye(count, dtype=matrix.dtype)
+    return (eye[:, None, :, None] * matrix[..., None, :, None, :]).reshape(*lead, count * n, count * m)
+
+
+def fits(mesh_lat, rows, width_y, cells, chans, modes_x, modes_y):
+    return (
+        cells == 2 * SPAN
+        and SPAN % (LANE // chans * chans) == 0
+        and mesh_lat * GROUP * SPAN == modes_y * cells
+        and rows % 4 == 0
+        and rows >= 16
+        and width_y % 256 == 0
+        and 4 * modes_y == SPAN
+        and modes_x % 8 == 0
+    )
+
+
+def shards(field, lat_modes, lat_gains, lat_local, depth_modes, depth_local):
+    highest = lax.Precision.HIGHEST
+    devices = lax.axis_size("lat")
+    rows, width_y, cells = field.shape
+    modes_x, chans, _ = lat_modes.shape
+    modes_y = lat_gains.shape[0]
+    modes_z = depth_modes.shape[0]
+    if not fits(devices, rows, width_y, cells, chans, modes_x, modes_y):
+        return plain_shards(field, lat_modes, lat_gains, lat_local, depth_modes, depth_local)
+    depth = cells // chans
+    width_x = rows * devices
+    basis_x = basis64(width_x, modes_x)
+    basis_y = basis64(width_y, modes_y)
+    basis_z = basis64(depth, modes_z)
+    funcs, fine = window_modes(rows, width_x, modes_x)
+    count = funcs.shape[0]
+    packed = (count + fine) * GROUP
+    halves = cells // SPAN
+    me = lax.axis_index("lat")
+
+    by_high, by_low = split64(basis_y)
+    by_forward = np.concatenate([by_high, by_low], axis=0)
+    pairs = 2
+    steps = rows // (2 * pairs)
+    sent = pl.pallas_call(
+        functools.partial(forward_kernel, funcs, fine),
+        grid=(steps + 1,),
+        in_specs=[
+            pl.BlockSpec((2 * modes_y, width_y), lambda s: (0, 0)),
+            pl.BlockSpec((pairs, width_y, cells), lambda s: (jnp.minimum(s, steps - 1), 0, 0)),
+            pl.BlockSpec((pairs, width_y, cells), lambda s: (2 * steps - 1 - jnp.minimum(s, steps - 1), 0, 0)),
+        ],
+        out_specs=pl.BlockSpec((devices, packed, SPAN), lambda s: (0, 0, 0)),
+        out_shape=jax.ShapeDtypeStruct((devices, packed, SPAN), BF16),
+        scratch_shapes=[
+            pltpu.VMEM((2 * pairs, modes_y, cells), F32),
+            pltpu.VMEM((count, modes_y, cells), F32),
+        ],
+        compiler_params=pltpu.CompilerParams(vmem_limit_bytes=48 * 2**20),
+        name="forward",
+    )(by_forward, field, field)
+    gathered = lax.all_to_all(sent, "lat", split_axis=0, concat_axis=0, tiled=True)
+
+    weights = np.einsum("pit,jt->pij", basis_x.reshape(modes_x, devices, rows), funcs)
+    flat = weights.reshape(modes_x, devices * count)
+    ah, al = split64(np.pad(flat, ((0, 0), (0, -flat.shape[1] % LANE))))
+    a_forward = np.concatenate([ah, al], axis=0)
+    bh, bl = split64(flat.T)
+    a_back = np.concatenate([bh, bl, bh, bl], axis=1)
+    gains = lax.dynamic_slice_in_dim(lat_gains, (me // halves) * GROUP, GROUP, axis=0)
+    gains = jnp.tile(gains, (1, SPAN // chans))
+    mixed = pl.pallas_call(
+        functools.partial(mix_kernel, count, fine),
+        out_shape=jax.ShapeDtypeStruct((devices, packed, SPAN), BF16),
+        scratch_shapes=[
+            pltpu.VMEM((SPAN // LANE, a_forward.shape[1] * GROUP, LANE), F32),
+            pltpu.VMEM((SPAN // LANE, devices * count * GROUP, LANE), F32),
+        ],
+        compiler_params=pltpu.CompilerParams(vmem_limit_bytes=48 * 2**20),
+        name="mix",
+    )(gathered, a_forward, a_back, gains, diagonals(lat_modes))
+    returned = lax.all_to_all(mixed, "lat", split_axis=0, concat_axis=0, tiled=True)
+
+    by_back = np.concatenate([by_high, by_low, by_high, by_low], axis=0).T.copy()
+    per = SPAN // chans
+    flip = np.kron(np.eye(per)[::-1], np.eye(chans)).astype(ml_dtypes.bfloat16)
+    local_high, local_low = split_outside(kron_eye(0.5 * lat_local, per))
+    local = jnp.concatenate([local_high, local_low], axis=0)
+    turned = local.reshape(2 * SPAN, per, chans)[:, ::-1].reshape(2 * SPAN, SPAN)
+    local = jnp.stack([local, turned])
+    near_z = basis_z[:, :per].astype(np.float32)
+
+    def depth_matrix(parity):
+        b = near_z[parity::2]
+        full = 0.5 * jnp.einsum(
+            "kz,kw,kcd->zcwd", b, b, depth_modes[parity::2], precision=highest
+        ).reshape(SPAN, SPAN) + 0.25 * kron_eye(depth_local, per)
+        high, low = split_outside(full)
+        return jnp.concatenate([high, high, low], axis=0)
+
+    wide = (width_y, cells)
+    narrow = (width_y, SPAN)
+    steps = rows // 2
+    return pl.pallas_call(
+        functools.partial(tail_kernel, funcs, fine, 64),
+        grid=(steps + 1,),
+        in_specs=[
+            pl.BlockSpec((devices, packed, SPAN), lambda s: (0, 0, 0)),
+            pl.BlockSpec((2, width_y, cells), lambda s: (jnp.minimum(s, steps - 1), 0, 0)),
+            pl.BlockSpec((width_y, SPAN), lambda s: (0, 0)),
+            pl.BlockSpec((2, 2 * SPAN, SPAN), lambda s: (0, 0, 0)),
+            pl.BlockSpec((2, 3 * SPAN, SPAN), lambda s: (0, 0, 0)),
+            pl.BlockSpec((SPAN, SPAN), lambda s: (0, 0)),
+        ],
+        out_specs=pl.BlockSpec((2, width_y, cells), lambda s: (jnp.maximum(s - 1, 0), 0, 0)),
+        out_shape=jax.ShapeDtypeStruct(field.shape, BF16),
+        scratch_shapes=[pltpu.VMEM((rows, 4 * modes_y, cells), BF16)]
+        + 2 * [pltpu.VMEM(wide, F32)]
+        + 2 * [pltpu.VMEM(narrow, F32)]
+        + 2 * [pltpu.VMEM(wide, F32)]
+        + 2 * [pltpu.VMEM((width_y, 4 * SPAN), BF16)]
+        + 2 * [pltpu.VMEM(wide, F32)]
+        + 2 * [pltpu.VMEM(narrow, BF16)],
+        compiler_params=pltpu.CompilerParams(vmem_limit_bytes=52 * 2**20),
+        name="tail",
+    )(returned, field, by_back, local, jnp.stack([depth_matrix(0), depth_matrix(1)]), flip)
+
+
 def solution(mesh):
     placed = (P(("group", "lat"), None, None), P(), P(), P(), P(), P())
     return jax.shard_map(

time: 549 us -> 149 us (0.27); the launches traced: 542 us -> 149 us
  matrix products: 292 us -> 4.39 us
  waiting for transfers between devices: 162 us -> 40.2 us
  Pallas kernels: 0 us -> 73.7 us
  local copies, waits for them, and re-layouts: 75.3 us -> 15.7 us
    dot_general x11 -> x2, matrix products: 292 us -> 4.39 us  [depth_matrix(): jnp.einsum('kz,kw,kcd->zcwd', b, b, depth_modes[parity::2], precision=hig...]
    all_to_all x2, waiting for transfers between devices: 162 us -> 40.2 us  [the longest x1 25.9 us: shards(): lax.all_to_all(sent, 'lat', split_axis=0, concat_axis=0, tiled=True)]
    pallas_call x0 -> x3, Pallas kernels: none -> 73.7 us  [the longest x1 53.6 us: shards(): pl.pallas_call(functools.partial(tail_kernel, funcs, fine, 64), grid=(ste...]
    convert_element_type x1 -> x0, local copies, waits for them, and re-layouts: 22.5 us -> none  [row_tail(): return final.reshape(rows, width, cells).astype(jnp.bfloat16)]
    unnamed x12 -> x35, local copies, waits for them, and re-layouts: 22.8 us -> 2.11 us
    all_to_all x3 -> x0, local copies, waits for them, and re-layouts: 18.8 us -> none  [the longest x2 12.3 us: shards(): lax.all_to_all(packed, 'lat', split_axis=1, concat_axis=0, tiled=True)]
    dot_general x2 -> x0, local copies, waits for them, and re-layouts: 5.92 us -> none  [the longest x1 5.34 us: shards(): jnp.dot(basis_x, gathered, precision=highest).reshape(modes_x, pairs, chans)]
    add x0 -> x4, local copies, waits for them, and re-layouts: none -> 5.5 us  [depth_matrix(): 0.5 * jnp.einsum('kz,kw,kcd->zcwd', b, b, depth_modes[parity::2], precisi...]
  transfers between devices with their start and end apart: 2 -> 2, of which waited for: 2 -> 2; matrix products, arithmetic and copies ran while one was open for 4% -> 14% of each run, Pallas kernels for 0% -> 0%
where the time goes in v2:
time: 149 us
  Pallas kernels  73.7 us (49%)
  waiting for transfers between devices  40.2 us (27%)
  local copies, waits for them, and re-layouts  15.7 us (11%)
  starting transfers between devices  11.7 us (8%)
  matrix products  4.39 us (3%)
  other arithmetic  2.53 us (2%)
    pallas_call x1, Pallas kernels, shards(): pl.pallas_call(functools.partial(tail_kernel, funcs, fine, 64), grid=(ste...  53.6 us
    all_to_all x1, waiting for transfers between devices, shards(): lax.all_to_all(sent, 'lat', split_axis=0, concat_axis=0, tiled=True)  25.9 us
    all_to_all x1, waiting for transfers between devices, shards(): lax.all_to_all(mixed, 'lat', split_axis=0, concat_axis=0, tiled=True)  14.3 us
    pallas_call x1, Pallas kernels, shards(): pl.pallas_call(functools.partial(forward_kernel, funcs, fine), grid=(step...  11.7 us
    pallas_call x1, Pallas kernels, shards(): pl.pallas_call(functools.partial(mix_kernel, count, fine), out_shape=jax....  8.38 us
    all_to_all x1, starting transfers between devices, shards(): lax.all_to_all(sent, 'lat', split_axis=0, concat_axis=0, tiled=True)  6.7 us
    add x4, local copies, waits for them, and re-layouts, depth_matrix(): 0.5 * jnp.einsum('kz,kw,kcd->zcwd', b, b, depth_modes[parity::2], precisi...  5.5 us
    all_to_all x1, starting transfers between devices, shards(): lax.all_to_all(mixed, 'lat', split_axis=0, concat_axis=0, tiled=True)  5.01 us
  transfers between devices with their start and end apart: 2, of which 2 were waited for; matrix products, arithmetic and copies ran while one was open for 14% of the time, Pallas kernels for 0%

profile of v2, /device:TPU:15, one launch (start us, length us, event | category | flops | bytes accessed | tf_op | source)
XLA Modules:
  0.0 148.6 jit_solution(7705843108547912315)
XLA Ops:
  0.0 0.9 copy-done.3
  0.9 11.7 %forward.1 = bf16[16,160,256]{2,1,0:T(8,128)(2,1)} custom-call(bf16[128,512]{1,0:T(8,128)(2,1)S(1)} %copy-done.3, bf16[32,512,512]{2,1,0:T(8,128)(2,1)} %u_ref.1, bf16[32,512,512]{2,1,0:T(8,128)(2,1)} %u_ref.1), custom_call_target="tpu_custom_call" | custom-call | tf_op jit(solution)/shard_map/forward/pallas_call | solution.py:376
  12.6 6.7 %all-to-all-start = ((bf16[16,160,256]{2,1,0:T(8,128)(2,1)}), bf16[16,160,256]{2,1,0:T(8,128)(2,1)S(1)}, u32[]{:S(2)}, u32[]{:S(2)}) async-start(bf16[16,160,256]{2,1,0:T(8,128)(2,1)} %forward.1), calls=%async_computation | async-start | bytes 2621440 | tf_op jit(solution)/shard_map/all_to_all | solution.py:393
  19.3 0.1 constant_dynamic-slice_fusion
  19.4 0.1 copy.25
  19.5 0.1 copy.30
  19.6 0.1 tile.9.g_ref
  19.7 0.1 mul.94
  19.8 0.1 mul.90
  19.9 0.1 mul.91
  20.2 0.2 copy.27
  20.4 1.5 tile.20
  21.8 2.1 %copy.28.w_ref = f32[31,64,128]{2,1,0:T(8,128)S(1)} copy(f32[31,64,128]{1,2,0:T(8,128)} %bitcast.43) | data formatting | bytes 2031616 | tf_op jit(solution)/shard_map/tile | solution.py:330
  24.0 25.9 %all-to-all-done.r_ref = bf16[16,160,256]{2,1,0:T(8,128)(2,1)S(1)} async-done(((bf16[16,160,256]{2,1,0:T(8,128)(2,1)}), bf16[16,160,256]{2,1,0:T(8,128)(2,1)S(1)}, u32[]{:S(2)}, u32[]{:S(2)}) %all-to-all-start) | async-done | bytes 1310752 | tf_op jit(solution)/shard_map/all_to_all | solution.py:393
  49.9 8.4 %mix.1 = bf16[16,160,256]{2,1,0:T(8,128)(2,1)} custom-call(bf16[16,160,256]{2,1,0:T(8,128)(2,1)S(1)} %all-to-all-done.r_ref, bf16[128,256]{1,0:T(8,128)(2,1)S(1)} %copy-done.5, bf16[224,256]{1,0:T(8,128)(2,1)S(1)} %copy-done.4, f32[8,256]{1,0:T(8,128)S(1)} %tile.9.g_ref, f32[31,64,128]{2,1,0:T(8,128)S(1)} %copy.28.w_ref), custom_call_target="tpu_custom_call" | custom-call | tf_op jit(solution)/shard_map/mix/pallas_call | solution.py:403
  58.3 5.0 %all-to-all-start.1 = ((bf16[16,160,256]{2,1,0:T(8,128)(2,1)}), bf16[16,160,256]{2,1,0:T(8,128)(2,1)S(1)}, u32[]{:S(2)}, u32[]{:S(2)}) async-start(bf16[16,160,256]{2,1,0:T(8,128)(2,1)} %mix.1), calls=%async_computation.1 | async-start | bytes 2621440 | tf_op jit(solution)/shard_map/all_to_all | solution.py:413
  63.4 0.8 copy.31
  64.3 2.2 %bitcast_add_fusion.1 = f32[16,16,16,16]{3,0,1,2:T(8,128)S(1)} fusion(f32[16,16]{1,0:T(8,128)S(1)} %copy-done.12, f32[16,16]{0,1:T(8,128)S(1)} %fusion.12, f32[8,16,16]{2,1,0:T(8,128)S(1)} %get-tuple-element.11, f32[8,16]{1,0:T(8,128)S(1)} %copy-done.16, f32[8,16]{0,1:T(8,128)S(1)} %copy-done.14), kind=kOutput, calls=%fused_computation.1 | convolution fusion | flops 6555648 | bytes 273408 | tf_op jit(solution)/shard_map/kz,kw,kcd->zcwd/dot_general | solution.py:426
  66.5 1.2 copy.34
  67.8 1.5 %add.20 = f32[256,256]{1,0:T(8,128)} reshape(f32[16,16,16,16]{3,2,1,0:T(8,128)S(1)} %copy.34) | data formatting | bytes 524288 | tf_op jit(solution)/shard_map/add | solution.py:426
  69.3 2.2 %bitcast_add_fusion = f32[16,16,16,16]{3,0,1,2:T(8,128)S(1)} fusion(f32[16,16]{1,0:T(8,128)S(1)} %copy-done.12, f32[16,16]{0,1:T(8,128)S(1)} %fusion.12, f32[8,16,16]{2,1,0:T(8,128)S(1)} %get-tuple-element.12, f32[8,16]{1,0:T(8,128)S(1)} %copy-done.15, f32[8,16]{0,1:T(8,128)S(1)} %copy-done.13), kind=kOutput, calls=%fused_computation | convolution fusion | flops 6555648 | bytes 273408 | tf_op jit(solution)/shard_map/kz,kw,kcd->zcwd/dot_general | solution.py:426
  71.5 1.2 copy.37
  72.7 1.5 %add.22 = f32[256,256]{1,0:T(8,128)} reshape(f32[16,16,16,16]{3,2,1,0:T(8,128)S(1)} %copy.37) | data formatting | bytes 524288 | tf_op jit(solution)/shard_map/add | solution.py:426
  74.2 0.2 broadcast_multiply_fusion
  74.5 1.2 copy.29
  75.7 1.5 %mul.89 = f32[256,256]{1,0:T(8,128)} reshape(f32[16,16,16,16]{3,2,1,0:T(8,128)S(1)} %copy.29) | data formatting | bytes 524288 | tf_op jit(solution)/shard_map/mul | solution.py:336
  77.2 1.0 reduce-precision_convert_fusion.3
  78.3 1.0 pad_maximum_fusion.1.l_ref
  79.5 0.1 pad_maximum_fusion.w_ref
  79.6 14.3 %all-to-all-done.1.r_ref = bf16[16,160,256]{2,1,0:T(8,128)(2,1)S(1)} async-done(((bf16[16,160,256]{2,1,0:T(8,128)(2,1)}), bf16[16,160,256]{2,1,0:T(8,128)(2,1)S(1)}, u32[]{:S(2)}, u32[]{:S(2)}) %all-to-all-start.1) | async-done | bytes 1310752 | tf_op jit(solution)/shard_map/all_to_all | solution.py:413
  93.9 1.1 copy-done.6
  95.0 53.6 %tail.1 = bf16[32,512,512]{2,1,0:T(8,128)(2,1)} custom-call(bf16[16,160,256]{2,1,0:T(8,128)(2,1)} %copy-done.6, bf16[32,512,512]{2,1,0:T(8,128)(2,1)} %u_ref.1, bf16[512,256]{1,0:T(8,128)(2,1)S(1)} %copy-done.1, bf16[2,512,256]{2,1,0:T(8,128)(2,1)S(1)} %pad_maximum_fusion.1.l_ref, bf16[2,768,256]{2,1,0:T(8,128)(2,1)S(1)} %pad_maximum_fusion.w_ref, ...), custom_call_target="tpu_custom_call" | custom-call | tf_op jit(solution)/shard_map/tail/pallas_call | solution.py:435
  (49 shorter events, 0.5 us)
Async XLA Ops:
  0.0 19.3 %copy-start = (f32[64,16]{0,1:T(8,128)S(1)}, f32[64,16]{0,1:T(8,128)}, u32[]{:S(2)}) copy-start(f32[64,16]{0,1:T(8,128)} %param.17) | copy-start | bytes 12292
  0.0 0.9 copy-start.3
  12.6 6.9 %copy-start.11 = (f32[16,16]{1,0:T(8,128)S(1)}, f32[16,16]{1,0:T(8,128)}, u32[]{:S(2)}) copy-start(f32[16,16]{1,0:T(8,128)} %param.18) | copy-start | bytes 3076
  12.6 7.4 %copy-start.9 = (f32[64,16,16]{0,2,1:T(8,128)S(1)}, f32[64,16,16]{0,2,1:T(8,128)}, u32[]{:S(2)}) copy-start(f32[64,16,16]{0,2,1:T(8,128)} %param.16) | copy-start | bytes 196612
  12.6 37.3 %all-to-all-start = ((bf16[16,160,256]{2,1,0:T(8,128)(2,1)}), bf16[16,160,256]{2,1,0:T(8,128)(2,1)S(1)}, u32[]{:S(2)}, u32[]{:S(2)}) async-start(bf16[16,160,256]{2,1,0:T(8,128)(2,1)} %forward.1), calls=%async_computation | async-start | bytes 2621440 | tf_op jit(solution)/shard_map/all_to_all | solution.py:393
  20.3 29.6 %copy-start.4 = (bf16[224,256]{1,0:T(8,128)(2,1)S(1)}, bf16[224,256]{1,0:T(8,128)(2,1)}, u32[]{:S(2)}) copy-start(bf16[224,256]{1,0:T(8,128)(2,1)} %constant.46.clone.b_ref) | copy-start | bytes 344068
  20.4 29.5 %copy-start.5 = (bf16[128,256]{1,0:T(8,128)(2,1)S(1)}, bf16[128,256]{1,0:T(8,128)(2,1)}, u32[]{:S(2)}) copy-start(bf16[128,256]{1,0:T(8,128)(2,1)} %constant.45.clone.a_ref) | copy-start | bytes 196612
  58.3 6.0 %copy-start.10 = (f32[16,16,16]{2,1,0:T(8,128)S(1)}, f32[16,16,16]{2,1,0:T(8,128)}, u32[]{:S(2)}) copy-start(f32[16,16,16]{2,1,0:T(8,128)} %param.19) | copy-start | bytes 49156
  58.3 6.0 %copy-start.12 = (f32[16,16]{1,0:T(8,128)S(1)}, f32[16,16]{1,0:T(8,128)}, u32[]{:S(2)}) copy-start(f32[16,16]{1,0:T(8,128)} %param.20) | copy-start | bytes 3076
  58.3 6.0 %copy-start.14 = (f32[8,16]{0,1:T(8,128)S(1)}, f32[8,16]{0,1:T(8,128)}, u32[]{:S(2)}) copy-start(f32[8,16]{0,1:T(8,128)} %constant.53) | copy-start | bytes 1540
  58.3 6.0 %copy-start.16 = (f32[8,16]{1,0:T(8,128)S(1)}, f32[8,16]{1,0:T(8,128)}, u32[]{:S(2)}) copy-start(f32[8,16]{1,0:T(8,128)} %constant.47.clone) | copy-start | bytes 1540
  58.3 35.6 %all-to-all-start.1 = ((bf16[16,160,256]{2,1,0:T(8,128)(2,1)}), bf16[16,160,256]{2,1,0:T(8,128)(2,1)S(1)}, u32[]{:S(2)}, u32[]{:S(2)}) async-start(bf16[16,160,256]{2,1,0:T(8,128)(2,1)} %mix.1), calls=%async_computation.1 | async-start | bytes 2621440 | tf_op jit(solution)/shard_map/all_to_all | solution.py:413
  67.7 1.6 %copy-start.13 = (f32[8,16]{0,1:T(8,128)S(1)}, f32[8,16]{0,1:T(8,128)}, u32[]{:S(2)}) copy-start(f32[8,16]{0,1:T(8,128)} %constant.54) | copy-start | bytes 1540
  67.7 1.5 %copy-start.15 = (f32[8,16]{1,0:T(8,128)S(1)}, f32[8,16]{1,0:T(8,128)}, u32[]{:S(2)}) copy-start(f32[8,16]{1,0:T(8,128)} %constant.48.clone) | copy-start | bytes 1540
  77.2 2.1 %copy-start.7 = (f32[256,256]{1,0:T(8,128)S(1)}, f32[256,256]{1,0:T(8,128)}, u32[]{:S(2)}) copy-start(f32[256,256]{1,0:T(8,128)} %add.20) | copy-start | bytes 786436
  77.2 2.2 %copy-start.8 = (f32[256,256]{1,0:T(8,128)S(1)}, f32[256,256]{1,0:T(8,128)}, u32[]{:S(2)}) copy-start(f32[256,256]{1,0:T(8,128)} %add.22) | copy-start | bytes 786436
  79.3 15.6 %copy-start.1 = (bf16[512,256]{1,0:T(8,128)(2,1)S(1)}, bf16[512,256]{1,0:T(8,128)(2,1)}, u32[]{:S(2)}) copy-start(bf16[512,256]{1,0:T(8,128)(2,1)} %constant.49.clone.by_ref) | copy-start | bytes 786436
  79.3 15.6 %copy-start.2 = (bf16[256,256]{1,0:T(8,128)(2,1)S(1)}, bf16[256,256]{1,0:T(8,128)(2,1)}, u32[]{:S(2)}) copy-start(bf16[256,256]{1,0:T(8,128)(2,1)} %constant.50.clone.flip_ref) | copy-start | bytes 393220
  93.9 1.1 copy-start.6

commit v3 on v2

--- a/solution.py
+++ b/solution.py
@@ -160,14 +160,14 @@
         pl.when(step == at)(functools.partial(body, at))
 
 
-def mix_kernel(count, fine, r_ref, a_ref, b_ref, g_ref, w_ref, o_ref, m_ref, back_ref):
+def mix_kernel(count, fine, r_ref, a_ref, b_ref, g_ref, w_ref, order_ref, o_ref, m_ref, back_ref):
     devices, packed, span = r_ref.shape
     modes_x = w_ref.shape[1]
     depth = a_ref.shape[1]
     highs, lows = count * GROUP, fine * GROUP
     tiles = [(k, slice(k * LANE, (k + 1) * LANE)) for k in range(span // LANE)]
     for i in range(devices):
-        got = r_ref[i].astype(F32)
+        got = jnp.dot(r_ref[i], order_ref[...], preferred_element_type=F32)
         for k, lanes in tiles:
             m_ref[k, i * highs : i * highs + lows] = got[:lows, lanes] + got[highs:, lanes]
             m_ref[k, i * highs + lows : (i + 1) * highs] = got[lows:highs, lanes]
@@ -184,11 +184,9 @@
         mixed = []
         for k, lanes in tiles:
             part = coef[:, lanes]
-            total = part * w_ref[shifts // 2]
-            for n in range(shifts):
-                shift = n - shifts // 2
-                if shift:
-                    total = total + pltpu.roll(part, shift % LANE, 1) * w_ref[n]
+            total = part * w_ref[0]
+            for n in range(1, shifts):
+                total = total + pltpu.roll(part, n * (LANE // shifts), 1) * w_ref[n]
             mixed.append(total)
         high, low = split(jnp.concatenate(mixed, axis=1))
         right = jnp.concatenate([high, high, low, low], axis=0)
@@ -202,11 +200,10 @@
             o_ref[i, highs:, lanes] = low[:lows]
 
 
-def expand(funcs, fine, r_ref, flip_ref, b_ref):
+def expand(funcs, fine, r_ref, place_ref, b_ref):
     count, rows = funcs.shape
     modes_y = b_ref.shape[1] // 4
     halves = b_ref.shape[2] // SPAN
-    flip = flip_ref[...]
 
     def some(g, carry):
         at = pl.multiple_of(g * 2 * GROUP, 2 * GROUP)
@@ -214,8 +211,7 @@
             got = []
             for k in range(2):
                 block = r_ref[(2 * g + k) * halves + h]
-                turned = jnp.dot(block, flip, preferred_element_type=F32) if h else block.astype(F32)
-                got.append(turned)
+                got.append(jnp.dot(block, place_ref[h], preferred_element_type=F32))
             for c in range(SPAN // LANE):
                 part = slice(c * LANE, (c + 1) * LANE)
                 modes = []
@@ -245,78 +241,101 @@
     lax.fori_loop(0, modes_y // (2 * GROUP), some, 0)
 
 
-def tail_kernel(funcs, fine, chunk, r_ref, u_ref, by_ref, l_ref, w_ref, flip_ref, o_ref, b_ref, *scratch):
+def local_kernel(u_ref, l_ref, flip_ref, x_ref, f_ref):
+    rows, width, _ = u_ref.shape
+    for h in range(2):
+        lanes = slice(h * SPAN, (h + 1) * SPAN)
+        u = u_ref[:, :, lanes].reshape(rows * width, SPAN)
+        x = jnp.dot(jnp.concatenate([u, u], axis=1), l_ref[h], preferred_element_type=F32)
+        x_ref[:, :, lanes] = x.reshape(rows, width, SPAN)
+    f = jnp.dot(u, flip_ref[...], preferred_element_type=F32)
+    f_ref[...] = f.astype(BF16).reshape(rows, width, SPAN)
+
+
+def weave(one, other):
+    done = 0
+    for n, step in enumerate(one):
+        step()
+        until = len(other) * (n + 1) // len(one)
+        for at in range(done, until):
+            other[at]()
+        done = until
+
+
+def tail_kernel(funcs, fine, chunk, r_ref, x_ref, u_ref, f_ref, by_ref, w_ref, place_ref, flip_ref, o_ref, b_ref, *scratch):
     step = pl.program_id(0)
     last = pl.num_programs(0) - 1
     width = u_ref.shape[1]
-    pre, seen, first, parts, post, done = (scratch[n : n + 2] for n in range(0, 12, 2))
+    pre, first, parts, post, done = (scratch[n : n + 2] for n in range(0, 10, 2))
     near, far = slice(0, SPAN), slice(SPAN, 2 * SPAN)
-    chunks = [slice(y, y + chunk) for y in range(0, width, chunk)]
+    pieces = [(r, y) for r in range(2) for y in range(0, width, chunk)]
 
     def lateral_product(n):
-        for h, lanes in enumerate((near, far)):
-            u = u_ref[n, :, lanes]
-            left = jnp.concatenate([by_ref[...], u, u], axis=1)
-            right = jnp.concatenate([b_ref[2 * step + n, :, lanes], l_ref[h]], axis=0)
-            pre[n][:, lanes] = jnp.dot(left, right, preferred_element_type=F32)
-        seen[n][...] = jnp.dot(u, flip_ref[...], preferred_element_type=F32)
+        def piece(r, lanes):
+            right = b_ref[4 * step + 2 * n + r, :, lanes]
+            z = jnp.dot(by_ref[...], right, preferred_element_type=F32)
+            pre[n][r * width : (r + 1) * width, lanes] = z
+
+        return [functools.partial(piece, r, lanes) for r in range(2) for lanes in (near, far)]
 
     def lateral_points(n):
-        for ys in chunks:
-            f0 = u_ref[n, ys, near].astype(F32) + twice_gelu(pre[n][ys, near])
-            f1 = seen[n][ys] + twice_gelu(pre[n][ys, far])
-            first[n][ys, near] = f0
-            first[n][ys, far] = f1
+        def piece(r, y):
+            at, ys = slice(r * width + y, r * width + y + chunk), slice(y, y + chunk)
+            f0 = u_ref[2 * n + r, ys].astype(F32) + twice_gelu(pre[n][at, near] + x_ref[2 * n + r, ys, near])
+            f1 = f_ref[2 * n + r, ys].astype(F32) + twice_gelu(pre[n][at, far] + x_ref[2 * n + r, ys, far])
+            first[n][at, near] = f0
+            first[n][at, far] = f1
             for m, value in enumerate((f0 + f1, f0 - f1)):
                 high, low = split(value)
-                parts[n][ys, 2 * m * SPAN : (2 * m + 1) * SPAN] = high
-                parts[n][ys, (2 * m + 1) * SPAN : (2 * m + 2) * SPAN] = low
+                parts[n][at, 2 * m * SPAN : (2 * m + 1) * SPAN] = high
+                parts[n][at, (2 * m + 1) * SPAN : (2 * m + 2) * SPAN] = low
+
+        return [functools.partial(piece, r, y) for r, y in pieces]
 
     def depth_product(n):
-        for m, lanes in enumerate((near, far)):
+        def piece(m, lanes):
             high = parts[n][:, 2 * m * SPAN : (2 * m + 1) * SPAN]
             low = parts[n][:, (2 * m + 1) * SPAN : (2 * m + 2) * SPAN]
             left = jnp.concatenate([high, low, high], axis=1)
             post[n][:, lanes] = jnp.dot(left, w_ref[m], preferred_element_type=F32)
 
+        return [functools.partial(piece, m, lanes) for m, lanes in enumerate((near, far))]
+
     def depth_points(n):
-        for ys in chunks:
-            even, odd = post[n][ys, near], post[n][ys, far]
-            o_ref[n, ys, near] = (first[n][ys, near] + twice_gelu(even + odd)).astype(BF16)
-            done[n][ys] = (first[n][ys, far] + twice_gelu(even - odd)).astype(BF16)
+        def piece(r, y):
+            at, ys = slice(r * width + y, r * width + y + chunk), slice(y, y + chunk)
+            even, odd = post[n][at, near], post[n][at, far]
+            o_ref[2 * n + r, ys, near] = (first[n][at, near] + twice_gelu(even + odd)).astype(BF16)
+            done[n][at] = (first[n][at, far] + twice_gelu(even - odd)).astype(BF16)
+
+        return [functools.partial(piece, r, y) for r, y in pieces]
 
     def finish(n):
-        o_ref[n, :, far] = jnp.dot(done[n][...], flip_ref[...], preferred_element_type=F32).astype(BF16)
+        def piece():
+            z = jnp.dot(done[n][...], flip_ref[...], preferred_element_type=F32).astype(BF16)
+            o_ref[2 * n : 2 * n + 2, :, far] = z.reshape(2, width, SPAN)
+
+        return [piece]
 
     @pl.when(step == 0)
     def _():
-        expand(funcs, fine, r_ref, flip_ref, b_ref)
-        lateral_product(0)
-        lateral_product(1)
-        lateral_points(0)
-        depth_product(0)
-        lateral_points(1)
+        expand(funcs, fine, r_ref, place_ref, b_ref)
+        weave(lateral_product(0), [])
+        weave(lateral_product(1), lateral_points(0))
+        weave(depth_product(0), lateral_points(1))
 
     @pl.when(jnp.logical_and(step > 0, step < last))
     def _():
-        depth_product(1)
-        depth_points(0)
-        lateral_product(0)
-        depth_points(1)
-        finish(0)
-        lateral_product(1)
-        lateral_points(0)
-        finish(1)
-        depth_product(0)
-        lateral_points(1)
+        weave(depth_product(1), depth_points(0))
+        weave(lateral_product(0) + finish(0), depth_points(1))
+        weave(lateral_product(1) + finish(1), lateral_points(0))
+        weave(depth_product(0), lateral_points(1))
 
     @pl.when(step == last)
     def _():
-        depth_product(1)
-        depth_points(0)
-        finish(0)
-        depth_points(1)
-        finish(1)
+        weave(depth_product(1), depth_points(0))
+        weave(finish(0), depth_points(1))
+        weave(finish(1), [])
 
 
 def twice_gelu(half):
@@ -324,10 +343,11 @@
 
 
 def diagonals(matrices):
-    p, n, _ = matrices.shape
-    turned = jnp.pad(jnp.swapaxes(matrices, 1, 2)[:, :, ::-1], ((0, 0), (0, 0), (0, n)))
-    skewed = turned.reshape(p, 2 * n * n)[:, : n * (2 * n - 1)].reshape(p, n, 2 * n - 1)
-    return jnp.tile(jnp.transpose(skewed, (2, 0, 1)), (1, 1, LANE // n))
+    n = matrices.shape[1]
+    ids = np.arange(n)
+    picks = (ids[None, :, None] == (ids[None, None, :] - ids[:, None, None]) % n).astype(np.float32)
+    rows = jnp.sum(matrices[None] * picks[:, None], axis=2)
+    return jnp.repeat(rows, LANE // n, axis=2)
 
 
 def kron_eye(matrix, count):
@@ -392,6 +412,32 @@
     )(by_forward, field, field)
     gathered = lax.all_to_all(sent, "lat", split_axis=0, concat_axis=0, tiled=True)
 
+    per = SPAN // chans
+    flip = np.kron(np.eye(per)[::-1], np.eye(chans)).astype(ml_dtypes.bfloat16)
+    local_high, local_low = split_outside(kron_eye(0.5 * lat_local, per))
+    local = jnp.concatenate([local_high, local_low], axis=0)
+    turned = local.reshape(2 * SPAN, per, chans)[:, ::-1].reshape(2 * SPAN, SPAN)
+    four = 4
+    local_part, mirrored = pl.pallas_call(
+        local_kernel,
+        grid=(rows // four,),
+        in_specs=[
+            pl.BlockSpec((four, width_y, cells), lambda s: (s, 0, 0)),
+            pl.BlockSpec((2, 2 * SPAN, SPAN), lambda s: (0, 0, 0)),
+            pl.BlockSpec((SPAN, SPAN), lambda s: (0, 0)),
+        ],
+        out_specs=[
+            pl.BlockSpec((four, width_y, cells), lambda s: (s, 0, 0)),
+            pl.BlockSpec((four, width_y, SPAN), lambda s: (s, 0, 0)),
+        ],
+        out_shape=[
+            jax.ShapeDtypeStruct(field.shape, F32),
+            jax.ShapeDtypeStruct((rows, width_y, SPAN), BF16),
+        ],
+        compiler_params=pltpu.CompilerParams(vmem_limit_bytes=48 * 2**20),
+        name="local",
+    )(field, jnp.stack([local, turned]), flip)
+
     weights = np.einsum("pit,jt->pij", basis_x.reshape(modes_x, devices, rows), funcs)
     flat = weights.reshape(modes_x, devices * count)
     ah, al = split64(np.pad(flat, ((0, 0), (0, -flat.shape[1] % LANE))))
@@ -399,7 +445,12 @@
     bh, bl = split64(flat.T)
     a_back = np.concatenate([bh, bl, bh, bl], axis=1)
     gains = lax.dynamic_slice_in_dim(lat_gains, (me // halves) * GROUP, GROUP, axis=0)
-    gains = jnp.tile(gains, (1, SPAN // chans))
+    gains = jnp.tile(jnp.repeat(gains, LANE // chans, axis=1), (1, SPAN // LANE))
+    per_lane = LANE // chans
+    ids = np.arange(LANE)
+    order = np.zeros((LANE, LANE))
+    order[ids, ids % chans * per_lane + ids // chans] = 1
+    order = np.kron(np.eye(SPAN // LANE), order).astype(ml_dtypes.bfloat16)
     mixed = pl.pallas_call(
         functools.partial(mix_kernel, count, fine),
         out_shape=jax.ShapeDtypeStruct((devices, packed, SPAN), BF16),
@@ -409,16 +460,10 @@
         ],
         compiler_params=pltpu.CompilerParams(vmem_limit_bytes=48 * 2**20),
         name="mix",
-    )(gathered, a_forward, a_back, gains, diagonals(lat_modes))
+    )(gathered, a_forward, a_back, gains, diagonals(lat_modes), order)
     returned = lax.all_to_all(mixed, "lat", split_axis=0, concat_axis=0, tiled=True)
 
     by_back = np.concatenate([by_high, by_low, by_high, by_low], axis=0).T.copy()
-    per = SPAN // chans
-    flip = np.kron(np.eye(per)[::-1], np.eye(chans)).astype(ml_dtypes.bfloat16)
-    local_high, local_low = split_outside(kron_eye(0.5 * lat_local, per))
-    local = jnp.concatenate([local_high, local_low], axis=0)
-    turned = local.reshape(2 * SPAN, per, chans)[:, ::-1].reshape(2 * SPAN, SPAN)
-    local = jnp.stack([local, turned])
     near_z = basis_z[:, :per].astype(np.float32)
 
     def depth_matrix(parity):
@@ -429,32 +474,43 @@
         high, low = split_outside(full)
         return jnp.concatenate([high, high, low], axis=0)
 
-    wide = (width_y, cells)
-    narrow = (width_y, SPAN)
-    steps = rows // 2
+    place = np.stack([order.T, order.T @ flip])
+    wide = (2 * width_y, cells)
+    narrow = (2 * width_y, SPAN)
+    steps = rows // four
     return pl.pallas_call(
         functools.partial(tail_kernel, funcs, fine, 64),
         grid=(steps + 1,),
         in_specs=[
             pl.BlockSpec((devices, packed, SPAN), lambda s: (0, 0, 0)),
-            pl.BlockSpec((2, width_y, cells), lambda s: (jnp.minimum(s, steps - 1), 0, 0)),
+            pl.BlockSpec((four, width_y, cells), lambda s: (jnp.minimum(s, steps - 1), 0, 0)),
+            pl.BlockSpec((four, width_y, SPAN), lambda s: (jnp.minimum(s, steps - 1), 0, 0)),
+            pl.BlockSpec((four, width_y, SPAN), lambda s: (jnp.minimum(s, steps - 1), 0, 0)),
             pl.BlockSpec((width_y, SPAN), lambda s: (0, 0)),
-            pl.BlockSpec((2, 2 * SPAN, SPAN), lambda s: (0, 0, 0)),
             pl.BlockSpec((2, 3 * SPAN, SPAN), lambda s: (0, 0, 0)),
+            pl.BlockSpec((2, SPAN, SPAN), lambda s: (0, 0, 0)),
             pl.BlockSpec((SPAN, SPAN), lambda s: (0, 0)),
         ],
-        out_specs=pl.BlockSpec((2, width_y, cells), lambda s: (jnp.maximum(s - 1, 0), 0, 0)),
+        out_specs=pl.BlockSpec((four, width_y, cells), lambda s: (jnp.maximum(s - 1, 0), 0, 0)),
         out_shape=jax.ShapeDtypeStruct(field.shape, BF16),
         scratch_shapes=[pltpu.VMEM((rows, 4 * modes_y, cells), BF16)]
         + 2 * [pltpu.VMEM(wide, F32)]
-        + 2 * [pltpu.VMEM(narrow, F32)]
         + 2 * [pltpu.VMEM(wide, F32)]
-        + 2 * [pltpu.VMEM((width_y, 4 * SPAN), BF16)]
+        + 2 * [pltpu.VMEM((2 * width_y, 4 * SPAN), BF16)]
         + 2 * [pltpu.VMEM(wide, F32)]
         + 2 * [pltpu.VMEM(narrow, BF16)],
-        compiler_params=pltpu.CompilerParams(vmem_limit_bytes=52 * 2**20),
+        compiler_params=pltpu.CompilerParams(vmem_limit_bytes=58 * 2**20),
         name="tail",
-    )(returned, field, by_back, local, jnp.stack([depth_matrix(0), depth_matrix(1)]), flip)
+    )(
+        returned,
+        local_part,
+        field,
+        mirrored,
+        by_back,
+        jnp.stack([depth_matrix(0), depth_matrix(1)]),
+        place,
+        flip,
+    )
 
 
 def solution(mesh):

time: 149 us -> 151 us (1.013)
  Pallas kernels: 73.7 us -> 88 us
  waiting for transfers between devices: 40.2 us -> 28.7 us
  local copies, waits for them, and re-layouts: 15.7 us -> 12.3 us
    pallas_call x0 -> x1, Pallas kernels: none -> 22.6 us  [shards(): pl.pallas_call(local_kernel, grid=(rows // four,), in_specs=[pl.BlockSpec...]
    all_to_all x1, waiting for transfers between devices: 14.3 us -> 0.01 us  [shards(): lax.all_to_all(mixed, 'lat', split_axis=0, concat_axis=0, tiled=True)]
    pallas_call x1, Pallas kernels: 53.6 us -> 47.3 us  [shards(): pl.pallas_call(functools.partial(tail_kernel, funcs, fine, 64), grid=(ste...]
    another operation x5 -> x3, local copies, waits for them, and re-layouts: 4.54 us -> 0.94 us  [the longest x1 0.83 us: shards(): jnp.stack([local, turned])]
    all_to_all x1, waiting for transfers between devices: 25.9 us -> 28.7 us  [shards(): lax.all_to_all(sent, 'lat', split_axis=0, concat_axis=0, tiled=True)]
    pallas_call x1, Pallas kernels: 8.38 us -> 6.49 us  [shards(): pl.pallas_call(functools.partial(mix_kernel, count, fine), out_shape=jax....]
  transfers between devices with their start and end apart: 2 -> 2, of which waited for: 2 -> 1; matrix products, arithmetic and copies ran while one was open for 14% -> 12% of each run, Pallas kernels for 0% -> 15%
where the time goes in v3:
time: 151 us; the launch traced here: 149 us
  Pallas kernels  88 us (58%)
  waiting for transfers between devices  28.7 us (19%)
  local copies, waits for them, and re-layouts  12.3 us (8%)
  starting transfers between devices  11.7 us (8%)
  matrix products  4.39 us (3%)
  other arithmetic  3.96 us (3%)
    pallas_call x1, Pallas kernels, shards(): pl.pallas_call(functools.partial(tail_kernel, funcs, fine, 64), grid=(ste...  47.3 us
    all_to_all x1, waiting for transfers between devices, shards(): lax.all_to_all(sent, 'lat', split_axis=0, concat_axis=0, tiled=True)  28.7 us
    pallas_call x1, Pallas kernels, shards(): pl.pallas_call(local_kernel, grid=(rows // four,), in_specs=[pl.BlockSpec...  22.6 us
    pallas_call x1, Pallas kernels, shards(): pl.pallas_call(functools.partial(forward_kernel, funcs, fine), grid=(step...  11.7 us
    all_to_all x1, starting transfers between devices, shards(): lax.all_to_all(sent, 'lat', split_axis=0, concat_axis=0, tiled=True)  6.71 us
    pallas_call x1, Pallas kernels, shards(): pl.pallas_call(functools.partial(mix_kernel, count, fine), out_shape=jax....  6.49 us
    add x4, local copies, waits for them, and re-layouts, depth_matrix(): 0.5 * jnp.einsum('kz,kw,kcd->zcwd', b, b, depth_modes[parity::2], precisi...  5.51 us
    all_to_all x1, starting transfers between devices, shards(): lax.all_to_all(mixed, 'lat', split_axis=0, concat_axis=0, tiled=True)  5.01 us
  transfers between devices with their start and end apart: 2, of which 1 were waited for; matrix products, arithmetic and copies ran while one was open for 12% of the time, Pallas kernels for 15%

profile of v3, /device:TPU:15, one launch (start us, length us, event | category | flops | bytes accessed | tf_op | source)
XLA Modules:
  0.0 149.4 jit_solution(17146849916266895860)
XLA Ops:
  0.0 0.9 copy-done.3
  0.9 11.7 %forward.1 = bf16[16,160,256]{2,1,0:T(8,128)(2,1)} custom-call(bf16[128,512]{1,0:T(8,128)(2,1)S(1)} %copy-done.3, bf16[32,512,512]{2,1,0:T(8,128)(2,1)} %u_ref.3, bf16[32,512,512]{2,1,0:T(8,128)(2,1)} %u_ref.3), custom_call_target="tpu_custom_call" | custom-call | tf_op jit(solution)/shard_map/forward/pallas_call | solution.py:396
  12.6 6.7 %all-to-all-start = ((bf16[16,160,256]{2,1,0:T(8,128)(2,1)}), bf16[16,160,256]{2,1,0:T(8,128)(2,1)S(1)}, u32[]{:S(2)}, u32[]{:S(2)}) async-start(bf16[16,160,256]{2,1,0:T(8,128)(2,1)} %forward.1), calls=%async_computation | async-start | bytes 2621440 | tf_op jit(solution)/shard_map/all_to_all | solution.py:413
  19.4 0.1 constant_dynamic-slice_fusion
  19.6 0.1 copy.44
  19.6 0.1 broadcast_in_dim.4
  19.7 0.1 tile.10
  19.8 0.1 mul.113
  19.9 0.1 mul.109
  20.0 0.1 mul.110
  20.2 0.6 multiply_reduce_fusion
  20.8 0.1 broadcast_bitcast_fusion
  20.9 0.3 copy.42.w_ref
  21.2 28.7 %all-to-all-done.r_ref = bf16[16,160,256]{2,1,0:T(8,128)(2,1)S(1)} async-done(((bf16[16,160,256]{2,1,0:T(8,128)(2,1)}), bf16[16,160,256]{2,1,0:T(8,128)(2,1)S(1)}, u32[]{:S(2)}, u32[]{:S(2)}) %all-to-all-start) | async-done | bytes 1310752 | tf_op jit(solution)/shard_map/all_to_all | solution.py:413
  49.9 6.5 %mix.1 = bf16[16,160,256]{2,1,0:T(8,128)(2,1)} custom-call(bf16[16,160,256]{2,1,0:T(8,128)(2,1)S(1)} %all-to-all-done.r_ref, bf16[128,256]{1,0:T(8,128)(2,1)S(1)} %copy-done.6, bf16[224,256]{1,0:T(8,128)(2,1)S(1)} %copy-done.5, f32[8,256]{1,0:T(8,128)S(1)} %broadcast_bitcast_fusion.1.g_ref, f32[16,64,128]{2,1,0:T(8,128)S(1)} %copy.42.w_ref, ...), custom_call_target="tpu_custom_call" | custom-call | tf_op jit(solution)/shard_map/mix/pallas_call | solution.py:454
  56.4 5.0 %all-to-all-start.1 = ((bf16[16,160,256]{2,1,0:T(8,128)(2,1)}), bf16[16,160,256]{2,1,0:T(8,128)(2,1)S(1)}, u32[]{:S(2)}, u32[]{:S(2)}) async-start(bf16[16,160,256]{2,1,0:T(8,128)(2,1)} %mix.1), calls=%async_computation.1 | async-start | bytes 2621440 | tf_op jit(solution)/shard_map/all_to_all | solution.py:464
  61.5 0.8 copy.45
  62.4 2.2 %bitcast_add_fusion.1 = f32[16,16,16,16]{3,0,1,2:T(8,128)S(1)} fusion(f32[16,16]{1,0:T(8,128)S(1)} %copy-done.14, f32[16,16]{0,1:T(8,128)S(1)} %fusion.12, f32[8,16,16]{2,1,0:T(8,128)S(1)} %get-tuple-element.15, f32[8,16]{1,0:T(8,128)S(1)} %copy-done.18, f32[8,16]{0,1:T(8,128)S(1)} %copy-done.16), kind=kOutput, calls=%fused_computation.1 | convolution fusion | flops 6555648 | bytes 273408 | tf_op jit(solution)/shard_map/kz,kw,kcd->zcwd/dot_general | solution.py:471
  64.6 1.2 copy.48
  65.9 1.5 %add.18 = f32[256,256]{1,0:T(8,128)} reshape(f32[16,16,16,16]{3,2,1,0:T(8,128)S(1)} %copy.48) | data formatting | bytes 524288 | tf_op jit(solution)/shard_map/add | solution.py:471
  67.4 2.2 %bitcast_add_fusion = f32[16,16,16,16]{3,0,1,2:T(8,128)S(1)} fusion(f32[16,16]{1,0:T(8,128)S(1)} %copy-done.14, f32[16,16]{0,1:T(8,128)S(1)} %fusion.12, f32[8,16,16]{2,1,0:T(8,128)S(1)} %get-tuple-element.16, f32[8,16]{1,0:T(8,128)S(1)} %copy-done.17, f32[8,16]{0,1:T(8,128)S(1)} %copy-done.15), kind=kOutput, calls=%fused_computation | convolution fusion | flops 6555648 | bytes 273408 | tf_op jit(solution)/shard_map/kz,kw,kcd->zcwd/dot_general | solution.py:471
  69.6 1.2 copy.51
  70.8 1.5 %add.20 = f32[256,256]{1,0:T(8,128)} reshape(f32[16,16,16,16]{3,2,1,0:T(8,128)S(1)} %copy.51) | data formatting | bytes 524288 | tf_op jit(solution)/shard_map/add | solution.py:471
  72.4 0.2 broadcast_multiply_fusion
  72.6 1.2 copy.43
  73.8 1.5 %mul.108 = f32[256,256]{1,0:T(8,128)} reshape(f32[16,16,16,16]{3,2,1,0:T(8,128)S(1)} %copy.43) | data formatting | bytes 524288 | tf_op jit(solution)/shard_map/mul | solution.py:356
  75.4 1.0 reduce-precision_convert_fusion.3
  76.4 1.0 pad_maximum_fusion.1.l_ref
  77.4 22.6 %local.1 = (f32[32,512,512]{2,1,0:T(8,128)}, bf16[32,512,256]{2,1,0:T(8,128)(2,1)}) custom-call(bf16[32,512,512]{2,1,0:T(8,128)(2,1)} %u_ref.3, bf16[2,512,256]{2,1,0:T(8,128)(2,1)S(1)} %pad_maximum_fusion.1.l_ref, bf16[256,256]{1,0:T(8,128)(2,1)S(1)} %copy-done.2), custom_call_target="tpu_custom_call" | custom-call | tf_op jit(solution)/shard_map/local/pallas_call | solution.py:421
  100.1 1.0 pad_maximum_fusion.w_ref
  101.1 1.1 copy-done.7
  102.2 47.3 %tail.1 = bf16[32,512,512]{2,1,0:T(8,128)(2,1)} custom-call(bf16[16,160,256]{2,1,0:T(8,128)(2,1)} %copy-done.7, f32[32,512,512]{2,1,0:T(8,128)} %get-tuple-element.7.x_ref, bf16[32,512,512]{2,1,0:T(8,128)(2,1)} %u_ref.3, bf16[32,512,256]{2,1,0:T(8,128)(2,1)} %get-tuple-element.8.f_ref, bf16[512,256]{1,0:T(8,128)(2,1)} %constant.58.clone.by_ref, ...), custom_call_target="tpu_custom_call" | custom-call | tf_op jit(solution)/shard_map/tail/pallas_call | solution.py:481
  (50 shorter events, 0.4 us)
Async XLA Ops:
  0.0 19.4 %copy-start = (f32[64,16]{0,1:T(8,128)S(1)}, f32[64,16]{0,1:T(8,128)}, u32[]{:S(2)}) copy-start(f32[64,16]{0,1:T(8,128)} %param.20) | copy-start | bytes 12292
  0.0 0.9 copy-start.3
  12.6 6.9 %copy-start.13 = (f32[16,16]{1,0:T(8,128)S(1)}, f32[16,16]{1,0:T(8,128)}, u32[]{:S(2)}) copy-start(f32[16,16]{1,0:T(8,128)} %param.21) | copy-start | bytes 3076
  12.6 7.5 %copy-start.10 = (f32[64,16,16]{0,2,1:T(8,128)S(1)}, f32[64,16,16]{0,2,1:T(8,128)}, u32[]{:S(2)}) copy-start(f32[64,16,16]{0,2,1:T(8,128)} %param.19) | copy-start | bytes 196612
  12.6 7.5 %copy-start.11 = (f32[16,16,16]{2,1,0:T(8,128)S(1)}, f32[16,16,16]{2,1,0:T(8,128)}, u32[]{:S(2)}) copy-start(f32[16,16,16]{2,1,0:T(8,128)} %constant.60) | copy-start | bytes 49156
  12.6 37.3 %all-to-all-start = ((bf16[16,160,256]{2,1,0:T(8,128)(2,1)}), bf16[16,160,256]{2,1,0:T(8,128)(2,1)S(1)}, u32[]{:S(2)}, u32[]{:S(2)}) async-start(bf16[16,160,256]{2,1,0:T(8,128)(2,1)} %forward.1), calls=%async_computation | async-start | bytes 2621440 | tf_op jit(solution)/shard_map/all_to_all | solution.py:413
  19.3 30.6 %copy-start.4 = (bf16[256,256]{1,0:T(8,128)(2,1)S(1)}, bf16[256,256]{1,0:T(8,128)(2,1)}, u32[]{:S(2)}) copy-start(bf16[256,256]{1,0:T(8,128)(2,1)} %constant.55.clone.order_ref) | copy-start | bytes 393220
  19.3 30.6 %copy-start.5 = (bf16[224,256]{1,0:T(8,128)(2,1)S(1)}, bf16[224,256]{1,0:T(8,128)(2,1)}, u32[]{:S(2)}) copy-start(bf16[224,256]{1,0:T(8,128)(2,1)} %constant.54.clone.b_ref) | copy-start | bytes 344068
  19.4 30.6 %copy-start.6 = (bf16[128,256]{1,0:T(8,128)(2,1)S(1)}, bf16[128,256]{1,0:T(8,128)(2,1)}, u32[]{:S(2)}) copy-start(bf16[128,256]{1,0:T(8,128)(2,1)} %constant.53.clone.a_ref) | copy-start | bytes 196612
  56.4 6.0 %copy-start.12 = (f32[16,16,16]{2,1,0:T(8,128)S(1)}, f32[16,16,16]{2,1,0:T(8,128)}, u32[]{:S(2)}) copy-start(f32[16,16,16]{2,1,0:T(8,128)} %param.22) | copy-start | bytes 49156
  56.4 6.0 %copy-start.14 = (f32[16,16]{1,0:T(8,128)S(1)}, f32[16,16]{1,0:T(8,128)}, u32[]{:S(2)}) copy-start(f32[16,16]{1,0:T(8,128)} %param.23) | copy-start | bytes 3076
  56.4 6.0 %copy-start.16 = (f32[8,16]{0,1:T(8,128)S(1)}, f32[8,16]{0,1:T(8,128)}, u32[]{:S(2)}) copy-start(f32[8,16]{0,1:T(8,128)} %constant.61) | copy-start | bytes 1540
  56.4 6.0 %copy-start.18 = (f32[8,16]{1,0:T(8,128)S(1)}, f32[8,16]{1,0:T(8,128)}, u32[]{:S(2)}) copy-start(f32[8,16]{1,0:T(8,128)} %constant.56.clone) | copy-start | bytes 1540
  56.4 44.7 %all-to-all-start.1 = ((bf16[16,160,256]{2,1,0:T(8,128)(2,1)}), bf16[16,160,256]{2,1,0:T(8,128)(2,1)S(1)}, u32[]{:S(2)}, u32[]{:S(2)}) async-start(bf16[16,160,256]{2,1,0:T(8,128)(2,1)} %mix.1), calls=%async_computation.1 | async-start | bytes 2621440 | tf_op jit(solution)/shard_map/all_to_all | solution.py:464
  65.8 1.6 %copy-start.15 = (f32[8,16]{0,1:T(8,128)S(1)}, f32[8,16]{0,1:T(8,128)}, u32[]{:S(2)}) copy-start(f32[8,16]{0,1:T(8,128)} %constant.62) | copy-start | bytes 1540
  65.8 1.6 %copy-start.17 = (f32[8,16]{1,0:T(8,128)S(1)}, f32[8,16]{1,0:T(8,128)}, u32[]{:S(2)}) copy-start(f32[8,16]{1,0:T(8,128)} %constant.57.clone) | copy-start | bytes 1540
  73.8 3.6 %copy-start.2 = (bf16[256,256]{1,0:T(8,128)(2,1)S(1)}, bf16[256,256]{1,0:T(8,128)(2,1)}, u32[]{:S(2)}) copy-start(bf16[256,256]{1,0:T(8,128)(2,1)} %constant.51.clone.flip_ref) | copy-start | bytes 393220
  77.4 22.6 %copy-start.8 = (f32[256,256]{1,0:T(8,128)S(1)}, f32[256,256]{1,0:T(8,128)}, u32[]{:S(2)}) copy-start(f32[256,256]{1,0:T(8,128)} %add.18) | copy-start | bytes 786436
  77.4 22.6 %copy-start.9 = (f32[256,256]{1,0:T(8,128)S(1)}, f32[256,256]{1,0:T(8,128)}, u32[]{:S(2)}) copy-start(f32[256,256]{1,0:T(8,128)} %add.20) | copy-start | bytes 786436
  101.1 1.1 copy-start.7
  102.2 47.3 %copy-start.1 = (f32[64,16]{0,1:T(8,128)S(1)}, f32[64,16]{0,1:T(8,128)}, u32[]{:S(2)}) copy-start(f32[64,16]{0,1:T(8,128)} %param.20) | copy-start | bytes 12292

commit v4 on v3

--- a/solution.py
+++ b/solution.py
@@ -107,11 +107,14 @@
     _, se, ve = np.linalg.svd(np.cos(math.pi * order * place / length))
     _, so, vo = np.linalg.svd(np.sin(math.pi * order * place / length))
     top = max(se[0], so[0])
-    half = rows // 2
-    count = max(int(np.sum(se[:half] > top * 2.0**-24)), int(np.sum(so[:half] > top * 2.0**-24)))
-    fine = max(int(np.sum(se[:half] > top * 0.1)), int(np.sum(so[:half] > top * 0.1)))
-    funcs = np.stack([ve[:count], vo[:count]], axis=1).reshape(2 * count, rows)
-    return funcs, 2 * fine
+    both = sorted([(-w, 2 * n) for n, w in enumerate(se[: rows // 2])] + [(-w, 2 * n + 1) for n, w in enumerate(so[: rows // 2])])
+    weights = np.array([-w for w, _ in both])
+    count = int(np.sum(weights > top * 2.0**-23))
+    fine = int(np.sum(weights > top * 0.25))
+    fine += (count + fine) % 2
+    funcs = np.stack([ve[: rows // 2], vo[: rows // 2]], axis=1).reshape(rows // 2 * 2, rows)
+    assert [n for _, n in both[:count]] == list(range(count))
+    return funcs[:count], fine
 
 
 def forward_kernel(funcs, fine, by_ref, near_ref, far_ref, o_ref, cy_ref, acc_ref):
@@ -140,12 +143,11 @@
                     continue
                 h, k = divmod(c, SPAN // LANE)
                 place = slice(k * LANE, (k + 1) * LANE)
-                for j in range(0, count, 2):
-                    high, low = split(jnp.concatenate(totals[j : j + 2], axis=0))
-                    o_ref[g * halves + h, j * GROUP : (j + 2) * GROUP, place] = high
-                    if j < fine:
-                        at = (count + j) * GROUP
-                        o_ref[g * halves + h, at : at + 2 * GROUP, place] = low
+                slots = [total.astype(BF16).astype(F32) for total in totals]
+                slots += [totals[j] - slots[j] for j in range(fine)]
+                for j in range(0, count + fine, 2):
+                    two = jnp.concatenate(slots[j : j + 2], axis=0).astype(BF16)
+                    o_ref[g * halves + h, j * GROUP : (j + 2) * GROUP, place] = two
 
     def body(at):
         if at > 0:
@@ -160,7 +162,7 @@
         pl.when(step == at)(functools.partial(body, at))
 
 
-def mix_kernel(count, fine, r_ref, a_ref, b_ref, g_ref, w_ref, order_ref, o_ref, m_ref, back_ref):
+def mix_kernel(count, fine, r_ref, a_ref, b_ref, g_ref, w_ref, order_ref, after_ref, o_ref, m_ref, back_ref):
     devices, packed, span = r_ref.shape
     modes_x = w_ref.shape[1]
     depth = a_ref.shape[1]
@@ -195,9 +197,10 @@
             back_ref[k, pl.ds(q, devices * count, stride=GROUP), :] = z[:, lanes]
     for i in range(devices):
         for k, lanes in tiles:
-            high, low = split(back_ref[k, i * highs : (i + 1) * highs])
-            o_ref[i, :highs, lanes] = high
-            o_ref[i, highs:, lanes] = low[:lows]
+            z = back_ref[k, i * highs : (i + 1) * highs]
+            high = z.astype(BF16).astype(F32)
+            low = z[:lows] - high[:lows]
+            o_ref[i, :, lanes] = jnp.concatenate([high, low], axis=0).astype(BF16)
 
 
 def expand(funcs, fine, r_ref, place_ref, b_ref):
@@ -268,21 +271,29 @@
     width = u_ref.shape[1]
     pre, first, parts, post, done = (scratch[n : n + 2] for n in range(0, 10, 2))
     near, far = slice(0, SPAN), slice(SPAN, 2 * SPAN)
-    pieces = [(r, y) for r in range(2) for y in range(0, width, chunk)]
+    unit = pre[0].shape[0]
+    pieces = range(0, unit, chunk)
+
+    def where(n, y):
+        return divmod(n * unit + y, width)
 
     def lateral_product(n):
-        def piece(r, lanes):
-            right = b_ref[4 * step + 2 * n + r, :, lanes]
-            z = jnp.dot(by_ref[...], right, preferred_element_type=F32)
-            pre[n][r * width : (r + 1) * width, lanes] = z
-
-        return [functools.partial(piece, r, lanes) for r in range(2) for lanes in (near, far)]
+        tall = min(unit, width)
+
+        def piece(at, lanes):
+            r, y = where(n, at)
+            right = b_ref[u_ref.shape[0] * step + r, :, lanes]
+            z = jnp.dot(by_ref[y : y + tall], right, preferred_element_type=F32)
+            pre[n][at : at + tall, lanes] = z
+
+        return [functools.partial(piece, at, lanes) for at in range(0, unit, tall) for lanes in (near, far)]
 
     def lateral_points(n):
-        def piece(r, y):
-            at, ys = slice(r * width + y, r * width + y + chunk), slice(y, y + chunk)
-            f0 = u_ref[2 * n + r, ys].astype(F32) + twice_gelu(pre[n][at, near] + x_ref[2 * n + r, ys, near])
-            f1 = f_ref[2 * n + r, ys].astype(F32) + twice_gelu(pre[n][at, far] + x_ref[2 * n + r, ys, far])
+        def piece(y):
+            r, y0 = where(n, y)
+            at, ys = slice(y, y + chunk), slice(y0, y0 + chunk)
+            f0 = u_ref[r, ys].astype(F32) + twice_gelu(pre[n][at, near] + x_ref[r, ys, near])
+            f1 = f_ref[r, ys].astype(F32) + twice_gelu(pre[n][at, far] + x_ref[r, ys, far])
             first[n][at, near] = f0
             first[n][at, far] = f1
             for m, value in enumerate((f0 + f1, f0 - f1)):
@@ -290,7 +301,7 @@
                 parts[n][at, 2 * m * SPAN : (2 * m + 1) * SPAN] = high
                 parts[n][at, (2 * m + 1) * SPAN : (2 * m + 2) * SPAN] = low
 
-        return [functools.partial(piece, r, y) for r, y in pieces]
+        return [functools.partial(piece, y) for y in pieces]
 
     def depth_product(n):
         def piece(m, lanes):
@@ -302,18 +313,21 @@
         return [functools.partial(piece, m, lanes) for m, lanes in enumerate((near, far))]
 
     def depth_points(n):
-        def piece(r, y):
-            at, ys = slice(r * width + y, r * width + y + chunk), slice(y, y + chunk)
+        def piece(y):
+            r, y0 = where(n, y)
+            at, ys = slice(y, y + chunk), slice(y0, y0 + chunk)
             even, odd = post[n][at, near], post[n][at, far]
-            o_ref[2 * n + r, ys, near] = (first[n][at, near] + twice_gelu(even + odd)).astype(BF16)
+            o_ref[r, ys, near] = (first[n][at, near] + twice_gelu(even + odd)).astype(BF16)
             done[n][at] = (first[n][at, far] + twice_gelu(even - odd)).astype(BF16)
 
-        return [functools.partial(piece, r, y) for r, y in pieces]
+        return [functools.partial(piece, y) for y in pieces]
 
     def finish(n):
         def piece():
             z = jnp.dot(done[n][...], flip_ref[...], preferred_element_type=F32).astype(BF16)
-            o_ref[2 * n : 2 * n + 2, :, far] = z.reshape(2, width, SPAN)
+            for at in range(0, unit, min(unit, width)):
+                r, y0 = where(n, at)
+                o_ref[r, y0 : y0 + min(unit, width), far] = z[at : at + min(unit, width)]
 
         return [piece]
 
@@ -453,6 +467,7 @@
     order = np.kron(np.eye(SPAN // LANE), order).astype(ml_dtypes.bfloat16)
     mixed = pl.pallas_call(
         functools.partial(mix_kernel, count, fine),
+        in_specs=6 * [pl.BlockSpec(memory_space=pltpu.VMEM)] + [pl.BlockSpec(memory_space=pl.ANY)],
         out_shape=jax.ShapeDtypeStruct((devices, packed, SPAN), BF16),
         scratch_shapes=[
             pltpu.VMEM((SPAN // LANE, a_forward.shape[1] * GROUP, LANE), F32),
@@ -460,7 +475,7 @@
         ],
         compiler_params=pltpu.CompilerParams(vmem_limit_bytes=48 * 2**20),
         name="mix",
-    )(gathered, a_forward, a_back, gains, diagonals(lat_modes), order)
+    )(gathered, a_forward, a_back, gains, diagonals(lat_modes), order, mirrored)
     returned = lax.all_to_all(mixed, "lat", split_axis=0, concat_axis=0, tiled=True)
 
     by_back = np.concatenate([by_high, by_low, by_high, by_low], axis=0).T.copy()
@@ -475,28 +490,30 @@
         return jnp.concatenate([high, high, low], axis=0)
 
     place = np.stack([order.T, order.T @ flip])
-    wide = (2 * width_y, cells)
-    narrow = (2 * width_y, SPAN)
-    steps = rows // four
+    block = 1
+    unit = block * width_y // 2
+    wide = (unit, cells)
+    narrow = (unit, SPAN)
+    steps = rows // block
     return pl.pallas_call(
         functools.partial(tail_kernel, funcs, fine, 64),
         grid=(steps + 1,),
         in_specs=[
             pl.BlockSpec((devices, packed, SPAN), lambda s: (0, 0, 0)),
-            pl.BlockSpec((four, width_y, cells), lambda s: (jnp.minimum(s, steps - 1), 0, 0)),
-            pl.BlockSpec((four, width_y, SPAN), lambda s: (jnp.minimum(s, steps - 1), 0, 0)),
-            pl.BlockSpec((four, width_y, SPAN), lambda s: (jnp.minimum(s, steps - 1), 0, 0)),
+            pl.BlockSpec((block, width_y, cells), lambda s: (jnp.minimum(s, steps - 1), 0, 0)),
+            pl.BlockSpec((block, width_y, SPAN), lambda s: (jnp.minimum(s, steps - 1), 0, 0)),
+            pl.BlockSpec((block, width_y, SPAN), lambda s: (jnp.minimum(s, steps - 1), 0, 0)),
             pl.BlockSpec((width_y, SPAN), lambda s: (0, 0)),
             pl.BlockSpec((2, 3 * SPAN, SPAN), lambda s: (0, 0, 0)),
             pl.BlockSpec((2, SPAN, SPAN), lambda s: (0, 0, 0)),
             pl.BlockSpec((SPAN, SPAN), lambda s: (0, 0)),
         ],
-        out_specs=pl.BlockSpec((four, width_y, cells), lambda s: (jnp.maximum(s - 1, 0), 0, 0)),
+        out_specs=pl.BlockSpec((block, width_y, cells), lambda s: (jnp.maximum(s - 1, 0), 0, 0)),
         out_shape=jax.ShapeDtypeStruct(field.shape, BF16),
         scratch_shapes=[pltpu.VMEM((rows, 4 * modes_y, cells), BF16)]
         + 2 * [pltpu.VMEM(wide, F32)]
         + 2 * [pltpu.VMEM(wide, F32)]
-        + 2 * [pltpu.VMEM((2 * width_y, 4 * SPAN), BF16)]
+        + 2 * [pltpu.VMEM((unit, 4 * SPAN), BF16)]
         + 2 * [pltpu.VMEM(wide, F32)]
         + 2 * [pltpu.VMEM(narrow, BF16)],
         compiler_params=pltpu.CompilerParams(vmem_limit_bytes=58 * 2**20),

time: 151 us -> 146 us (0.967)
  waiting for transfers between devices: 28.7 us -> 14.8 us
  Pallas kernels: 88 us -> 94 us
    all_to_all x1, waiting for transfers between devices: 28.7 us -> 0.01 us  [shards(): lax.all_to_all(sent, 'lat', split_axis=0, concat_axis=0, tiled=True)]
    all_to_all x1, waiting for transfers between devices: 0.01 us -> 14.8 us  [shards(): lax.all_to_all(mixed, 'lat', split_axis=0, concat_axis=0, tiled=True)]
    pallas_call x1, Pallas kernels: 47.3 us -> 53.6 us  [shards(): pl.pallas_call(functools.partial(tail_kernel, funcs, fine, 64), grid=(ste...]
    mul x6, local copies, waits for them, and re-layouts: 3.07 us -> 5.33 us  [kron_eye(): eye[:, None, :, None] * matrix[..., None, :, None, :]]
  transfers between devices with their start and end apart: 2 -> 2, of which waited for: 1 -> 1; matrix products, arithmetic and copies ran while one was open for 12% -> 14% of each run, Pallas kernels for 15% -> 16%
where the time goes in v4:
time: 146 us; the launch traced here: 144 us
  Pallas kernels  94 us (64%)
  waiting for transfers between devices  14.8 us (10%)
  local copies, waits for them, and re-layouts  13.8 us (9%)
  starting transfers between devices  12.9 us (9%)
  matrix products  5.25 us (4%)
  other arithmetic  3.06 us (2%)
    pallas_call x1, Pallas kernels, shards(): pl.pallas_call(functools.partial(tail_kernel, funcs, fine, 64), grid=(ste...  53.6 us
    pallas_call x1, Pallas kernels, shards(): pl.pallas_call(local_kernel, grid=(rows // four,), in_specs=[pl.BlockSpec...  22.6 us
    all_to_all x1, waiting for transfers between devices, shards(): lax.all_to_all(mixed, 'lat', split_axis=0, concat_axis=0, tiled=True)  14.8 us
    pallas_call x1, Pallas kernels, shards(): pl.pallas_call(functools.partial(forward_kernel, funcs, fine), grid=(step...  11.5 us
    all_to_all x1, starting transfers between devices, shards(): lax.all_to_all(sent, 'lat', split_axis=0, concat_axis=0, tiled=True)  6.71 us
    pallas_call x1, Pallas kernels, shards(): pl.pallas_call(functools.partial(mix_kernel, count, fine), in_specs=6 * [...  6.36 us
    all_to_all x1, starting transfers between devices, shards(): lax.all_to_all(mixed, 'lat', split_axis=0, concat_axis=0, tiled=True)  6.16 us
    mul x6, local copies, waits for them, and re-layouts, kron_eye(): eye[:, None, :, None] * matrix[..., None, :, None, :]  5.33 us
  transfers between devices with their start and end apart: 2, of which 1 were waited for; matrix products, arithmetic and copies ran while one was open for 14% of the time, Pallas kernels for 16%

profile of v4, /device:TPU:15, one launch (start us, length us, event | category | flops | bytes accessed | tf_op | source)
XLA Modules:
  0.0 144.1 jit_solution(10495959022862687524)
XLA Ops:
  0.0 0.9 copy-done.4
  0.9 11.5 %forward.1 = bf16[16,144,256]{2,1,0:T(8,128)(2,1)} custom-call(bf16[128,512]{1,0:T(8,128)(2,1)S(1)} %copy-done.4, bf16[32,512,512]{2,1,0:T(8,128)(2,1)} %u_ref.3, bf16[32,512,512]{2,1,0:T(8,128)(2,1)} %u_ref.3), custom_call_target="tpu_custom_call" | custom-call | tf_op jit(solution)/shard_map/forward/pallas_call | solution.py:410
  12.4 6.7 %all-to-all-start = ((bf16[16,144,256]{2,1,0:T(8,128)(2,1)}), bf16[16,144,256]{2,1,0:T(8,128)(2,1)S(1)}, u32[]{:S(2)}, u32[]{:S(2)}) async-start(bf16[16,144,256]{2,1,0:T(8,128)(2,1)} %forward.1), calls=%async_computation | async-start | bytes 2359296 | tf_op jit(solution)/shard_map/all_to_all | solution.py:427
  19.1 0.1 constant_dynamic-slice_fusion
  19.3 0.1 copy.43
  19.4 0.1 broadcast_in_dim.4
  19.4 0.1 tile.10
  19.6 0.1 mul.113
  19.7 0.1 mul.109
  19.8 0.1 mul.110
  20.0 0.1 copy.44
  20.2 0.6 multiply_reduce_fusion
  20.8 0.1 broadcast_bitcast_fusion
  20.9 0.3 copy.45.w_ref
  21.2 0.2 broadcast_multiply_fusion
  21.4 2.5 %copy.42 = f32[16,16,16,16]{3,2,1,0:T(8,128)} copy(f32[16,16,16,16]{3,0,1,2:T(8,128)S(1)} %broadcast_multiply_fusion) | data formatting | bytes 524288 | tf_op jit(solution)/shard_map/mul | solution.py:370
  23.9 2.5 %mul.108 = f32[256,256]{1,0:T(8,128)S(1)} reshape(f32[16,16,16,16]{3,2,1,0:T(8,128)} %copy.42) | data formatting | bytes 524288 | tf_op jit(solution)/shard_map/mul | solution.py:370
  26.6 22.6 %local.1 = (f32[32,512,512]{2,1,0:T(8,128)}, bf16[32,512,256]{2,1,0:T(8,128)(2,1)}) custom-call(bf16[32,512,512]{2,1,0:T(8,128)(2,1)} %u_ref.3, bf16[2,512,256]{2,1,0:T(8,128)(2,1)S(1)} %pad_maximum_fusion.1.l_ref, bf16[256,256]{1,0:T(8,128)(2,1)S(1)} %copy-done.2), custom_call_target="tpu_custom_call" | custom-call | tf_op jit(solution)/shard_map/local/pallas_call | solution.py:435
  49.2 6.4 %mix.1 = bf16[16,144,256]{2,1,0:T(8,128)(2,1)} custom-call(bf16[16,144,256]{2,1,0:T(8,128)(2,1)S(1)} %all-to-all-done.r_ref, bf16[128,256]{1,0:T(8,128)(2,1)S(1)} %copy-done.6, bf16[208,256]{1,0:T(8,128)(2,1)S(1)} %copy-done.5, f32[8,256]{1,0:T(8,128)S(1)} %broadcast_bitcast_fusion.1.g_ref, f32[16,64,128]{2,1,0:T(8,128)S(1)} %copy.45.w_ref, ...), custom_call_target="tpu_custom_call" | custom-call | tf_op jit(solution)/shard_map/mix/pallas_call | solution.py:468
  55.6 6.2 %all-to-all-start.1 = ((bf16[16,144,256]{2,1,0:T(8,128)(2,1)}), bf16[16,144,256]{2,1,0:T(8,128)(2,1)S(1)}, u32[]{:S(2)}, u32[]{:S(2)}) async-start(bf16[16,144,256]{2,1,0:T(8,128)(2,1)} %mix.1), calls=%async_computation.1 | async-start | bytes 2359296 | tf_op jit(solution)/shard_map/all_to_all | solution.py:479
  61.8 0.6 fusion.13
  62.4 2.2 %bitcast_add_fusion.1 = f32[16,16,16,16]{3,0,1,2:T(8,128)S(1)} fusion(f32[16,16]{1,0:T(8,128)S(1)} %copy-done.12, f32[16,16]{0,1:T(8,128)S(1)} %fusion.12, f32[8,16,16]{2,1,0:T(8,128)S(1)} %get-tuple-element.15, f32[8,16]{1,0:T(8,128)S(1)} %copy-done.14, f32[8,16]{0,1:T(8,128)S(1)} %copy-done.13), kind=kOutput, calls=%fused_computation.1 | convolution fusion | flops 6555648 | bytes 273408 | tf_op jit(solution)/shard_map/kz,kw,kcd->zcwd/dot_general | solution.py:486
  64.6 1.2 copy.48
  65.8 0.9 add.18
  66.8 3.0 %bitcast_add_fusion = f32[16,16,16,16]{3,0,1,2:T(8,128)S(1)} fusion(f32[16,16]{1,0:T(8,128)S(1)} %copy-done.12, f32[16,16]{0,1:T(8,128)S(1)} %fusion.12, f32[8,16,16]{2,1,0:T(8,128)} %get-tuple-element.16, f32[8,16]{1,0:T(8,128)} %constant.57.clone, f32[8,16]{0,1:T(8,128)} %constant.62), kind=kOutput, calls=%fused_computation | convolution fusion | flops 6555648 | bytes 273408 | tf_op jit(solution)/shard_map/kz,kw,kcd->zcwd/dot_general | solution.py:486
  69.8 1.2 copy.51
  71.0 1.5 %add.20 = f32[256,256]{1,0:T(8,128)} reshape(f32[16,16,16,16]{3,2,1,0:T(8,128)S(1)} %copy.51) | data formatting | bytes 524288 | tf_op jit(solution)/shard_map/add | solution.py:486
  72.6 1.0 reduce-precision_convert_fusion
  73.7 1.0 pad_maximum_fusion.w_ref
  74.7 14.8 %all-to-all-done.1.r_ref = bf16[16,144,256]{2,1,0:T(8,128)(2,1)S(1)} async-done(((bf16[16,144,256]{2,1,0:T(8,128)(2,1)}), bf16[16,144,256]{2,1,0:T(8,128)(2,1)S(1)}, u32[]{:S(2)}, u32[]{:S(2)}) %all-to-all-start.1) | async-done | bytes 1179680 | tf_op jit(solution)/shard_map/all_to_all | solution.py:479
  89.5 1.0 copy-done.7
  90.5 53.6 %tail.1 = bf16[32,512,512]{2,1,0:T(8,128)(2,1)} custom-call(bf16[16,144,256]{2,1,0:T(8,128)(2,1)} %copy-done.7, f32[32,512,512]{2,1,0:T(8,128)} %get-tuple-element.8.x_ref, bf16[32,512,512]{2,1,0:T(8,128)(2,1)} %u_ref.3, bf16[32,512,256]{2,1,0:T(8,128)(2,1)} %get-tuple-element.7.after_ref.f_ref, bf16[512,256]{1,0:T(8,128)(2,1)} %constant.58.clone.by_ref, ...), custom_call_target="tpu_custom_call" | custom-call | tf_op jit(solution)/shard_map/tail/pallas_call | solution.py:498
  (42 shorter events, 0.4 us)
Async XLA Ops:
  0.0 19.1 %copy-start = (f32[64,16]{0,1:T(8,128)S(1)}, f32[64,16]{0,1:T(8,128)}, u32[]{:S(2)}) copy-start(f32[64,16]{0,1:T(8,128)} %param.20) | copy-start | bytes 12292
  0.0 0.9 copy-start.4
  12.4 6.9 %copy-start.11 = (f32[16,16]{1,0:T(8,128)S(1)}, f32[16,16]{1,0:T(8,128)}, u32[]{:S(2)}) copy-start(f32[16,16]{1,0:T(8,128)} %param.21) | copy-start | bytes 3076
  12.4 7.7 %copy-start.8 = (f32[64,16,16]{0,2,1:T(8,128)S(1)}, f32[64,16,16]{0,2,1:T(8,128)}, u32[]{:S(2)}) copy-start(f32[64,16,16]{0,2,1:T(8,128)} %param.19) | copy-start | bytes 196612
  12.4 7.7 %copy-start.9 = (f32[16,16,16]{2,1,0:T(8,128)S(1)}, f32[16,16,16]{2,1,0:T(8,128)}, u32[]{:S(2)}) copy-start(f32[16,16,16]{2,1,0:T(8,128)} %constant.60) | copy-start | bytes 49156
  12.4 36.8 %all-to-all-start = ((bf16[16,144,256]{2,1,0:T(8,128)(2,1)}), bf16[16,144,256]{2,1,0:T(8,128)(2,1)S(1)}, u32[]{:S(2)}, u32[]{:S(2)}) async-start(bf16[16,144,256]{2,1,0:T(8,128)(2,1)} %forward.1), calls=%async_computation | async-start | bytes 2359296 | tf_op jit(solution)/shard_map/all_to_all | solution.py:427
  23.9 2.6 %copy-start.2 = (bf16[256,256]{1,0:T(8,128)(2,1)S(1)}, bf16[256,256]{1,0:T(8,128)(2,1)}, u32[]{:S(2)}) copy-start(bf16[256,256]{1,0:T(8,128)(2,1)} %constant.51.clone.flip_ref) | copy-start | bytes 393220
  26.6 22.6 %copy-start.3 = (bf16[256,256]{1,0:T(8,128)(2,1)S(1)}, bf16[256,256]{1,0:T(8,128)(2,1)}, u32[]{:S(2)}) copy-start(bf16[256,256]{1,0:T(8,128)(2,1)} %constant.55.clone.order_ref) | copy-start | bytes 393220
  26.6 22.6 %copy-start.5 = (bf16[208,256]{1,0:T(8,128)(2,1)S(1)}, bf16[208,256]{1,0:T(8,128)(2,1)}, u32[]{:S(2)}) copy-start(bf16[208,256]{1,0:T(8,128)(2,1)} %constant.54.clone.b_ref) | copy-start | bytes 319492
  26.6 22.6 %copy-start.6 = (bf16[128,256]{1,0:T(8,128)(2,1)S(1)}, bf16[128,256]{1,0:T(8,128)(2,1)}, u32[]{:S(2)}) copy-start(bf16[128,256]{1,0:T(8,128)(2,1)} %constant.53.clone.a_ref) | copy-start | bytes 196612
  55.6 6.2 %copy-start.10 = (f32[16,16,16]{2,1,0:T(8,128)S(1)}, f32[16,16,16]{2,1,0:T(8,128)}, u32[]{:S(2)}) copy-start(f32[16,16,16]{2,1,0:T(8,128)} %param.22) | copy-start | bytes 49156
  55.6 6.8 %copy-start.12 = (f32[16,16]{1,0:T(8,128)S(1)}, f32[16,16]{1,0:T(8,128)}, u32[]{:S(2)}) copy-start(f32[16,16]{1,0:T(8,128)} %param.23) | copy-start | bytes 3076
  55.6 6.8 %copy-start.13 = (f32[8,16]{0,1:T(8,128)S(1)}, f32[8,16]{0,1:T(8,128)}, u32[]{:S(2)}) copy-start(f32[8,16]{0,1:T(8,128)} %constant.61) | copy-start | bytes 1540
  55.6 6.8 %copy-start.14 = (f32[8,16]{1,0:T(8,128)S(1)}, f32[8,16]{1,0:T(8,128)}, u32[]{:S(2)}) copy-start(f32[8,16]{1,0:T(8,128)} %constant.56.clone) | copy-start | bytes 1540
  55.6 33.9 %all-to-all-start.1 = ((bf16[16,144,256]{2,1,0:T(8,128)(2,1)}), bf16[16,144,256]{2,1,0:T(8,128)(2,1)S(1)}, u32[]{:S(2)}, u32[]{:S(2)}) async-start(bf16[16,144,256]{2,1,0:T(8,128)(2,1)} %mix.1), calls=%async_computation.1 | async-start | bytes 2359296 | tf_op jit(solution)/shard_map/all_to_all | solution.py:479
  89.5 1.0 copy-start.7
  90.5 53.6 %copy-start.1 = (f32[64,16]{0,1:T(8,128)S(1)}, f32[64,16]{0,1:T(8,128)}, u32[]{:S(2)}) copy-start(f32[64,16]{0,1:T(8,128)} %param.20) | copy-start | bytes 12292

commit v5 on v4

--- a/solution.py
+++ b/solution.py
@@ -244,13 +244,17 @@
     lax.fori_loop(0, modes_y // (2 * GROUP), some, 0)
 
 
-def local_kernel(u_ref, l_ref, flip_ref, x_ref, f_ref):
+def local_near_kernel(u_ref, l_ref, x_ref):
     rows, width, _ = u_ref.shape
-    for h in range(2):
-        lanes = slice(h * SPAN, (h + 1) * SPAN)
-        u = u_ref[:, :, lanes].reshape(rows * width, SPAN)
-        x = jnp.dot(jnp.concatenate([u, u], axis=1), l_ref[h], preferred_element_type=F32)
-        x_ref[:, :, lanes] = x.reshape(rows, width, SPAN)
+    u = u_ref[...].reshape(rows * width, SPAN)
+    x = jnp.dot(jnp.concatenate([u, u], axis=1), l_ref[...], preferred_element_type=F32)
+    x_ref[...] = x.reshape(rows, width, SPAN)
+
+
+def local_far_kernel(u_ref, l_ref, flip_ref, after_ref, x_ref, f_ref):
+    local_near_kernel(u_ref, l_ref, x_ref)
+    rows, width, _ = u_ref.shape
+    u = u_ref[...].reshape(rows * width, SPAN)
     f = jnp.dot(u, flip_ref[...], preferred_element_type=F32)
     f_ref[...] = f.astype(BF16).reshape(rows, width, SPAN)
 
@@ -265,7 +269,7 @@
         done = until
 
 
-def tail_kernel(funcs, fine, chunk, r_ref, x_ref, u_ref, f_ref, by_ref, w_ref, place_ref, flip_ref, o_ref, b_ref, *scratch):
+def tail_kernel(funcs, fine, chunk, r_ref, x0_ref, x1_ref, u_ref, f_ref, by_ref, w_ref, place_ref, flip_ref, o_ref, b_ref, *scratch):
     step = pl.program_id(0)
     last = pl.num_programs(0) - 1
     width = u_ref.shape[1]
@@ -292,8 +296,8 @@
         def piece(y):
             r, y0 = where(n, y)
             at, ys = slice(y, y + chunk), slice(y0, y0 + chunk)
-            f0 = u_ref[r, ys].astype(F32) + twice_gelu(pre[n][at, near] + x_ref[r, ys, near])
-            f1 = f_ref[r, ys].astype(F32) + twice_gelu(pre[n][at, far] + x_ref[r, ys, far])
+            f0 = u_ref[r, ys].astype(F32) + twice_gelu(pre[n][at, near] + x0_ref[r, ys])
+            f1 = f_ref[r, ys].astype(F32) + twice_gelu(pre[n][at, far] + x1_ref[r, ys])
             first[n][at, near] = f0
             first[n][at, far] = f1
             for m, value in enumerate((f0 + f1, f0 - f1)):
@@ -432,25 +436,18 @@
     local = jnp.concatenate([local_high, local_low], axis=0)
     turned = local.reshape(2 * SPAN, per, chans)[:, ::-1].reshape(2 * SPAN, SPAN)
     four = 4
-    local_part, mirrored = pl.pallas_call(
-        local_kernel,
+    local_near = pl.pallas_call(
+        local_near_kernel,
         grid=(rows // four,),
         in_specs=[
-            pl.BlockSpec((four, width_y, cells), lambda s: (s, 0, 0)),
-            pl.BlockSpec((2, 2 * SPAN, SPAN), lambda s: (0, 0, 0)),
-            pl.BlockSpec((SPAN, SPAN), lambda s: (0, 0)),
-        ],
-        out_specs=[
-            pl.BlockSpec((four, width_y, cells), lambda s: (s, 0, 0)),
             pl.BlockSpec((four, width_y, SPAN), lambda s: (s, 0, 0)),
-        ],
-        out_shape=[
-            jax.ShapeDtypeStruct(field.shape, F32),
-            jax.ShapeDtypeStruct((rows, width_y, SPAN), BF16),
-        ],
+            pl.BlockSpec((2 * SPAN, SPAN), lambda s: (0, 0)),
+        ],
+        out_specs=pl.BlockSpec((four, width_y, SPAN), lambda s: (s, 0, 0)),
+        out_shape=jax.ShapeDtypeStruct((rows, width_y, SPAN), F32),
         compiler_params=pltpu.CompilerParams(vmem_limit_bytes=48 * 2**20),
-        name="local",
-    )(field, jnp.stack([local, turned]), flip)
+        name="local_near",
+    )(field, local)
 
     weights = np.einsum("pit,jt->pij", basis_x.reshape(modes_x, devices, rows), funcs)
     flat = weights.reshape(modes_x, devices * count)
@@ -475,8 +472,26 @@
         ],
         compiler_params=pltpu.CompilerParams(vmem_limit_bytes=48 * 2**20),
         name="mix",
-    )(gathered, a_forward, a_back, gains, diagonals(lat_modes), order, mirrored)
+    )(gathered, a_forward, a_back, gains, diagonals(lat_modes), order, local_near)
     returned = lax.all_to_all(mixed, "lat", split_axis=0, concat_axis=0, tiled=True)
+
+    local_far, mirrored = pl.pallas_call(
+        local_far_kernel,
+        grid=(rows // four,),
+        in_specs=[
+            pl.BlockSpec((four, width_y, SPAN), lambda s: (s, 0, 1)),
+            pl.BlockSpec((2 * SPAN, SPAN), lambda s: (0, 0)),
+            pl.BlockSpec((SPAN, SPAN), lambda s: (0, 0)),
+            pl.BlockSpec(memory_space=pl.ANY),
+        ],
+        out_specs=2 * [pl.BlockSpec((four, width_y, SPAN), lambda s: (s, 0, 0))],
+        out_shape=[
+            jax.ShapeDtypeStruct((rows, width_y, SPAN), F32),
+            jax.ShapeDtypeStruct((rows, width_y, SPAN), BF16),
+        ],
+        compiler_params=pltpu.CompilerParams(vmem_limit_bytes=48 * 2**20),
+        name="local_far",
+    )(field, turned, flip, mixed)
 
     by_back = np.concatenate([by_high, by_low, by_high, by_low], axis=0).T.copy()
     near_z = basis_z[:, :per].astype(np.float32)
@@ -490,17 +505,18 @@
         return jnp.concatenate([high, high, low], axis=0)
 
     place = np.stack([order.T, order.T @ flip])
-    block = 1
+    block = 4
     unit = block * width_y // 2
     wide = (unit, cells)
     narrow = (unit, SPAN)
     steps = rows // block
     return pl.pallas_call(
-        functools.partial(tail_kernel, funcs, fine, 64),
+        functools.partial(tail_kernel, funcs, fine, 16),
         grid=(steps + 1,),
         in_specs=[
             pl.BlockSpec((devices, packed, SPAN), lambda s: (0, 0, 0)),
-            pl.BlockSpec((block, width_y, cells), lambda s: (jnp.minimum(s, steps - 1), 0, 0)),
+            pl.BlockSpec((block, width_y, SPAN), lambda s: (jnp.minimum(s, steps - 1), 0, 0)),
+            pl.BlockSpec((block, width_y, SPAN), lambda s: (jnp.minimum(s, steps - 1), 0, 0)),
             pl.BlockSpec((block, width_y, SPAN), lambda s: (jnp.minimum(s, steps - 1), 0, 0)),
             pl.BlockSpec((block, width_y, SPAN), lambda s: (jnp.minimum(s, steps - 1), 0, 0)),
             pl.BlockSpec((width_y, SPAN), lambda s: (0, 0)),
@@ -520,7 +536,8 @@
         name="tail",
     )(
         returned,
-        local_part,
+        local_near,
+        local_far,
         field,
         mirrored,
         by_back,

time: 146 us -> 139 us (0.952)
  waiting for transfers between devices: 14.8 us -> 8.3 us
    all_to_all x1, waiting for transfers between devices: 14.8 us -> 0.01 us  [shards(): lax.all_to_all(mixed, 'lat', split_axis=0, concat_axis=0, tiled=True)]
    all_to_all x1, waiting for transfers between devices: 0.01 us -> 8.29 us  [shards(): lax.all_to_all(sent, 'lat', split_axis=0, concat_axis=0, tiled=True)]
    pallas_call x2 -> x3, Pallas kernels: 76.1 us -> 75.2 us  [the longest x1 47.8 us: shards(): pl.pallas_call(functools.partial(tail_kernel, funcs, fine, 16), grid=(ste...]
  transfers between devices with their start and end apart: 2 -> 2, of which waited for: 1 -> 1; matrix products, arithmetic and copies ran while one was open for 14% -> 16% of each run, Pallas kernels for 16% -> 20%
where the time goes in v5:
time: 139 us; the launch traced here: 137 us
  Pallas kernels  93.1 us (67%)
  local copies, waits for them, and re-layouts  14.4 us (10%)
  starting transfers between devices  11.7 us (8%)
  waiting for transfers between devices  8.3 us (6%)
  matrix products  5.25 us (4%)
  other arithmetic  3.99 us (3%)
    pallas_call x1, Pallas kernels, shards(): pl.pallas_call(functools.partial(tail_kernel, funcs, fine, 16), grid=(ste...  47.8 us
    pallas_call x1, Pallas kernels, shards(): pl.pallas_call(local_far_kernel, grid=(rows // four,), in_specs=[pl.Block...  14.8 us
    pallas_call x1, Pallas kernels, shards(): pl.pallas_call(local_near_kernel, grid=(rows // four,), in_specs=[pl.Bloc...  12.7 us
    pallas_call x1, Pallas kernels, shards(): pl.pallas_call(functools.partial(forward_kernel, funcs, fine), grid=(step...  11.5 us
    all_to_all x1, waiting for transfers between devices, shards(): lax.all_to_all(sent, 'lat', split_axis=0, concat_axis=0, tiled=True)  8.29 us
    all_to_all x1, starting transfers between devices, shards(): lax.all_to_all(sent, 'lat', split_axis=0, concat_axis=0, tiled=True)  6.69 us
    pallas_call x1, Pallas kernels, shards(): pl.pallas_call(functools.partial(mix_kernel, count, fine), in_specs=6 * [...  6.34 us
    add x4, local copies, waits for them, and re-layouts, depth_matrix(): 0.5 * jnp.einsum('kz,kw,kcd->zcwd', b, b, depth_modes[parity::2], precisi...  5.51 us
  transfers between devices with their start and end apart: 2, of which 1 were waited for; matrix products, arithmetic and copies ran while one was open for 16% of the time, Pallas kernels for 20%

profile of v5, /device:TPU:15, one launch (start us, length us, event | category | flops | bytes accessed | tf_op | source)
XLA Modules:
  0.0 137.0 jit_solution(17742801188036393923)
XLA Ops:
  0.0 0.9 copy-done.4
  0.9 11.5 %forward.1 = bf16[16,144,256]{2,1,0:T(8,128)(2,1)} custom-call(bf16[128,512]{1,0:T(8,128)(2,1)S(1)} %copy-done.4, bf16[32,512,512]{2,1,0:T(8,128)(2,1)} %u_ref.5, bf16[32,512,512]{2,1,0:T(8,128)(2,1)} %u_ref.5), custom_call_target="tpu_custom_call" | custom-call | tf_op jit(solution)/shard_map/forward/pallas_call | solution.py:414
  12.4 6.7 %all-to-all-start = ((bf16[16,144,256]{2,1,0:T(8,128)(2,1)}), bf16[16,144,256]{2,1,0:T(8,128)(2,1)S(1)}, u32[]{:S(2)}, u32[]{:S(2)}) async-start(bf16[16,144,256]{2,1,0:T(8,128)(2,1)} %forward.1), calls=%async_computation | async-start | bytes 2359296 | tf_op jit(solution)/shard_map/all_to_all | solution.py:431
  19.3 0.1 broadcast_in_dim.4
  19.4 0.1 tile.10
  19.5 0.6 multiply_reduce_fusion
  20.1 0.1 broadcast_bitcast_fusion
  20.2 0.3 copy.43.w_ref
  20.6 0.2 broadcast_multiply_fusion
  20.8 2.5 %copy.42 = f32[16,16,16,16]{3,2,1,0:T(8,128)} copy(f32[16,16,16,16]{3,0,1,2:T(8,128)S(1)} %broadcast_multiply_fusion) | data formatting | bytes 524288 | tf_op jit(solution)/shard_map/mul | solution.py:374
  23.3 2.4 %mul.108 = f32[256,256]{1,0:T(8,128)S(1)} reshape(f32[16,16,16,16]{3,2,1,0:T(8,128)} %copy.42) | data formatting | bytes 524288 | tf_op jit(solution)/shard_map/mul | solution.py:374
  25.9 12.7 %local_near.1.after_ref.x0_ref = f32[32,512,256]{2,1,0:T(8,128)} custom-call(bf16[32,512,512]{2,1,0:T(8,128)(2,1)} %u_ref.5, bf16[512,256]{1,0:T(8,128)(2,1)S(1)} %pad_maximum_fusion.1.l_ref), custom_call_target="tpu_custom_call" | custom-call | tf_op jit(solution)/shard_map/local_near/pallas_call | solution.py:439
  38.6 8.3 %all-to-all-done.r_ref = bf16[16,144,256]{2,1,0:T(8,128)(2,1)S(1)} async-done(((bf16[16,144,256]{2,1,0:T(8,128)(2,1)}), bf16[16,144,256]{2,1,0:T(8,128)(2,1)S(1)}, u32[]{:S(2)}, u32[]{:S(2)}) %all-to-all-start) | async-done | bytes 1179680 | tf_op jit(solution)/shard_map/all_to_all | solution.py:431
  46.9 6.3 %mix.1.after_ref = bf16[16,144,256]{2,1,0:T(8,128)(2,1)} custom-call(bf16[16,144,256]{2,1,0:T(8,128)(2,1)S(1)} %all-to-all-done.r_ref, bf16[128,256]{1,0:T(8,128)(2,1)S(1)} %copy-done.6, bf16[208,256]{1,0:T(8,128)(2,1)S(1)} %copy-done.5, f32[8,256]{1,0:T(8,128)S(1)} %broadcast_bitcast_fusion.1.g_ref, f32[16,64,128]{2,1,0:T(8,128)S(1)} %copy.43.w_ref, ...), custom_call_target="tpu_custom_call" | custom-call | tf_op jit(solution)/shard_map/mix/pallas_call | solution.py:465
  53.2 5.0 %all-to-all-start.1 = ((bf16[16,144,256]{2,1,0:T(8,128)(2,1)}), bf16[16,144,256]{2,1,0:T(8,128)(2,1)S(1)}, u32[]{:S(2)}, u32[]{:S(2)}) async-start(bf16[16,144,256]{2,1,0:T(8,128)(2,1)} %mix.1.after_ref), calls=%async_computation.1 | async-start | bytes 2359296 | tf_op jit(solution)/shard_map/all_to_all | solution.py:476
  58.3 0.1 mul.113
  58.4 0.1 mul.109
  58.5 0.1 mul.110
  58.8 0.1 copy.45.l_ref
  58.9 0.6 fusion.13
  59.5 2.2 %bitcast_add_fusion.1 = f32[16,16,16,16]{3,0,1,2:T(8,128)S(1)} fusion(f32[16,16]{1,0:T(8,128)S(1)} %copy-done.12, f32[16,16]{0,1:T(8,128)S(1)} %fusion.12, f32[8,16,16]{2,1,0:T(8,128)S(1)} %get-tuple-element.15, f32[8,16]{1,0:T(8,128)S(1)} %copy-done.14, f32[8,16]{0,1:T(8,128)S(1)} %copy-done.13), kind=kOutput, calls=%fused_computation.1 | convolution fusion | flops 6555648 | bytes 273408 | tf_op jit(solution)/shard_map/kz,kw,kcd->zcwd/dot_general | solution.py:501
  61.8 1.2 copy.48
  63.0 1.5 %add.18 = f32[256,256]{1,0:T(8,128)} reshape(f32[16,16,16,16]{3,2,1,0:T(8,128)S(1)} %copy.48) | data formatting | bytes 524288 | tf_op jit(solution)/shard_map/add | solution.py:501
  64.5 3.1 %bitcast_add_fusion = f32[16,16,16,16]{3,0,1,2:T(8,128)S(1)} fusion(f32[16,16]{1,0:T(8,128)S(1)} %copy-done.12, f32[16,16]{0,1:T(8,128)S(1)} %fusion.12, f32[8,16,16]{2,1,0:T(8,128)} %get-tuple-element.16, f32[8,16]{1,0:T(8,128)} %constant.57.clone, f32[8,16]{0,1:T(8,128)} %constant.62), kind=kOutput, calls=%fused_computation | convolution fusion | flops 6555648 | bytes 273408 | tf_op jit(solution)/shard_map/kz,kw,kcd->zcwd/dot_general | solution.py:501
  67.6 1.2 copy.51
  68.8 1.5 %add.20 = f32[256,256]{1,0:T(8,128)} reshape(f32[16,16,16,16]{3,2,1,0:T(8,128)S(1)} %copy.51) | data formatting | bytes 524288 | tf_op jit(solution)/shard_map/add | solution.py:501
  70.3 1.0 reduce-precision_convert_fusion.1
  71.4 1.0 reduce-precision_convert_fusion
  72.4 1.0 pad_maximum_fusion.w_ref
  73.4 14.8 %local_far.1 = (f32[32,512,256]{2,1,0:T(8,128)}, bf16[32,512,256]{2,1,0:T(8,128)(2,1)}) custom-call(bf16[32,512,512]{2,1,0:T(8,128)(2,1)} %u_ref.5, bf16[512,256]{1,0:T(8,128)(2,1)S(1)} %copy.45.l_ref, bf16[256,256]{1,0:T(8,128)(2,1)S(1)} %copy-done.2, bf16[16,144,256]{2,1,0:T(8,128)(2,1)} %mix.1.after_ref), custom_call_target="tpu_custom_call" | custom-call | tf_op jit(solution)/shard_map/local_far/pallas_call | solution.py:478
  88.2 1.0 copy-done.7
  89.2 47.8 %tail.1 = bf16[32,512,512]{2,1,0:T(8,128)(2,1)} custom-call(bf16[16,144,256]{2,1,0:T(8,128)(2,1)} %copy-done.7, f32[32,512,256]{2,1,0:T(8,128)} %local_near.1.after_ref.x0_ref, f32[32,512,256]{2,1,0:T(8,128)} %get-tuple-element.7.x1_ref, bf16[32,512,512]{2,1,0:T(8,128)(2,1)} %u_ref.5, bf16[32,512,256]{2,1,0:T(8,128)(2,1)} %get-tuple-element.8.f_ref, ...), custom_call_target="tpu_custom_call" | custom-call | tf_op jit(solution)/shard_map/tail/pallas_call | solution.py:513
  (42 shorter events, 0.5 us)
Async XLA Ops:
  0.0 19.2 %copy-start = (f32[64,16]{0,1:T(8,128)S(1)}, f32[64,16]{0,1:T(8,128)}, u32[]{:S(2)}) copy-start(f32[64,16]{0,1:T(8,128)} %param.20) | copy-start | bytes 12292
  0.0 0.9 copy-start.4
  12.4 7.1 %copy-start.8 = (f32[64,16,16]{0,2,1:T(8,128)S(1)}, f32[64,16,16]{0,2,1:T(8,128)}, u32[]{:S(2)}) copy-start(f32[64,16,16]{0,2,1:T(8,128)} %param.19) | copy-start | bytes 196612
  12.4 7.1 %copy-start.9 = (f32[16,16,16]{2,1,0:T(8,128)S(1)}, f32[16,16,16]{2,1,0:T(8,128)}, u32[]{:S(2)}) copy-start(f32[16,16,16]{2,1,0:T(8,128)} %constant.60) | copy-start | bytes 49156
  12.4 34.5 %all-to-all-start = ((bf16[16,144,256]{2,1,0:T(8,128)(2,1)}), bf16[16,144,256]{2,1,0:T(8,128)(2,1)S(1)}, u32[]{:S(2)}, u32[]{:S(2)}) async-start(bf16[16,144,256]{2,1,0:T(8,128)(2,1)} %forward.1), calls=%async_computation | async-start | bytes 2359296 | tf_op jit(solution)/shard_map/all_to_all | solution.py:431
  19.1 1.4 %copy-start.11 = (f32[16,16]{1,0:T(8,128)S(1)}, f32[16,16]{1,0:T(8,128)}, u32[]{:S(2)}) copy-start(f32[16,16]{1,0:T(8,128)} %param.21) | copy-start | bytes 3076
  25.9 21.0 %copy-start.3 = (bf16[256,256]{1,0:T(8,128)(2,1)S(1)}, bf16[256,256]{1,0:T(8,128)(2,1)}, u32[]{:S(2)}) copy-start(bf16[256,256]{1,0:T(8,128)(2,1)} %constant.54.clone.order_ref) | copy-start | bytes 393220
  25.9 21.0 %copy-start.5 = (bf16[208,256]{1,0:T(8,128)(2,1)S(1)}, bf16[208,256]{1,0:T(8,128)(2,1)}, u32[]{:S(2)}) copy-start(bf16[208,256]{1,0:T(8,128)(2,1)} %constant.53.clone.b_ref) | copy-start | bytes 319492
  25.9 21.0 %copy-start.6 = (bf16[128,256]{1,0:T(8,128)(2,1)S(1)}, bf16[128,256]{1,0:T(8,128)(2,1)}, u32[]{:S(2)}) copy-start(bf16[128,256]{1,0:T(8,128)(2,1)} %constant.52.clone.a_ref) | copy-start | bytes 196612
  53.2 5.7 %copy-start.10 = (f32[16,16,16]{2,1,0:T(8,128)S(1)}, f32[16,16,16]{2,1,0:T(8,128)}, u32[]{:S(2)}) copy-start(f32[16,16,16]{2,1,0:T(8,128)} %param.22) | copy-start | bytes 49156
  53.2 6.3 %copy-start.12 = (f32[16,16]{1,0:T(8,128)S(1)}, f32[16,16]{1,0:T(8,128)}, u32[]{:S(2)}) copy-start(f32[16,16]{1,0:T(8,128)} %param.23) | copy-start | bytes 3076
  53.2 6.3 %copy-start.13 = (f32[8,16]{0,1:T(8,128)S(1)}, f32[8,16]{0,1:T(8,128)}, u32[]{:S(2)}) copy-start(f32[8,16]{0,1:T(8,128)} %constant.61) | copy-start | bytes 1540
  53.2 6.3 %copy-start.14 = (f32[8,16]{1,0:T(8,128)S(1)}, f32[8,16]{1,0:T(8,128)}, u32[]{:S(2)}) copy-start(f32[8,16]{1,0:T(8,128)} %constant.56.clone) | copy-start | bytes 1540
  53.2 34.9 %all-to-all-start.1 = ((bf16[16,144,256]{2,1,0:T(8,128)(2,1)}), bf16[16,144,256]{2,1,0:T(8,128)(2,1)S(1)}, u32[]{:S(2)}, u32[]{:S(2)}) async-start(bf16[16,144,256]{2,1,0:T(8,128)(2,1)} %mix.1.after_ref), calls=%async_computation.1 | async-start | bytes 2359296 | tf_op jit(solution)/shard_map/all_to_all | solution.py:476
  70.3 3.1 %copy-start.2 = (bf16[256,256]{1,0:T(8,128)(2,1)S(1)}, bf16[256,256]{1,0:T(8,128)(2,1)}, u32[]{:S(2)}) copy-start(bf16[256,256]{1,0:T(8,128)(2,1)} %constant.55.clone.flip_ref) | copy-start | bytes 393220
  88.2 1.0 copy-start.7
  89.2 47.8 %copy-start.1 = (f32[64,16]{0,1:T(8,128)S(1)}, f32[64,16]{0,1:T(8,128)}, u32[]{:S(2)}) copy-start(f32[64,16]{0,1:T(8,128)} %param.20) | copy-start | bytes 12292

commit v6 on v5

--- a/solution.py
+++ b/solution.py
@@ -162,7 +162,7 @@
         pl.when(step == at)(functools.partial(body, at))
 
 
-def mix_kernel(count, fine, r_ref, a_ref, b_ref, g_ref, w_ref, order_ref, after_ref, o_ref, m_ref, back_ref):
+def mix_kernel(count, fine, r_ref, a_ref, b_ref, g_ref, w_ref, order_ref, place_ref, after_ref, o_ref, m_ref, back_ref):
     devices, packed, span = r_ref.shape
     modes_x = w_ref.shape[1]
     depth = a_ref.shape[1]
@@ -196,14 +196,13 @@
         for k, lanes in tiles:
             back_ref[k, pl.ds(q, devices * count, stride=GROUP), :] = z[:, lanes]
     for i in range(devices):
-        for k, lanes in tiles:
-            z = back_ref[k, i * highs : (i + 1) * highs]
-            high = z.astype(BF16).astype(F32)
-            low = z[:lows] - high[:lows]
-            o_ref[i, :, lanes] = jnp.concatenate([high, low], axis=0).astype(BF16)
-
-
-def expand(funcs, fine, r_ref, place_ref, b_ref):
+        z = jnp.concatenate([back_ref[k, i * highs : (i + 1) * highs] for k, _ in tiles], axis=1)
+        high = z.astype(BF16).astype(F32)
+        both = jnp.concatenate([high, z[:lows] - high[:lows]], axis=0).astype(BF16)
+        o_ref[i] = jnp.dot(both, place_ref[...], preferred_element_type=F32).astype(BF16)
+
+
+def expand(funcs, fine, r_ref, b_ref):
     count, rows = funcs.shape
     modes_y = b_ref.shape[1] // 4
     halves = b_ref.shape[2] // SPAN
@@ -214,7 +213,7 @@
             got = []
             for k in range(2):
                 block = r_ref[(2 * g + k) * halves + h]
-                got.append(jnp.dot(block, place_ref[h], preferred_element_type=F32))
+                got.append(block.astype(F32))
             for c in range(SPAN // LANE):
                 part = slice(c * LANE, (c + 1) * LANE)
                 modes = []
@@ -269,91 +268,124 @@
         done = until
 
 
-def tail_kernel(funcs, fine, chunk, r_ref, x0_ref, x1_ref, u_ref, f_ref, by_ref, w_ref, place_ref, flip_ref, o_ref, b_ref, *scratch):
+def tail_kernel(funcs, fine, chunk, r_ref, x0_ref, x1_ref, u_ref, f_ref, by_ref, w_ref, flip_ref, o_ref, b_ref, *scratch):
     step = pl.program_id(0)
-    last = pl.num_programs(0) - 1
-    width = u_ref.shape[1]
-    pre, first, parts, post, done = (scratch[n : n + 2] for n in range(0, 10, 2))
+    rows, width, _ = u_ref.shape
+    first, parts, done = scratch[0:2], scratch[2:4], scratch[4:6]
+    size = done[0].shape[0]
+    count = rows * width // size
     near, far = slice(0, SPAN), slice(SPAN, 2 * SPAN)
-    unit = pre[0].shape[0]
-    pieces = range(0, unit, chunk)
-
-    def where(n, y):
-        return divmod(n * unit + y, width)
-
-    def lateral_product(n):
-        tall = min(unit, width)
-
-        def piece(at, lanes):
-            r, y = where(n, at)
-            right = b_ref[u_ref.shape[0] * step + r, :, lanes]
-            z = jnp.dot(by_ref[y : y + tall], right, preferred_element_type=F32)
-            pre[n][at : at + tall, lanes] = z
-
-        return [functools.partial(piece, at, lanes) for at in range(0, unit, tall) for lanes in (near, far)]
-
-    def lateral_points(n):
-        def piece(y):
-            r, y0 = where(n, y)
-            at, ys = slice(y, y + chunk), slice(y0, y0 + chunk)
-            f0 = u_ref[r, ys].astype(F32) + twice_gelu(pre[n][at, near] + x0_ref[r, ys])
-            f1 = f_ref[r, ys].astype(F32) + twice_gelu(pre[n][at, far] + x1_ref[r, ys])
-            first[n][at, near] = f0
-            first[n][at, far] = f1
-            for m, value in enumerate((f0 + f1, f0 - f1)):
-                high, low = split(value)
-                parts[n][at, 2 * m * SPAN : (2 * m + 1) * SPAN] = high
-                parts[n][at, (2 * m + 1) * SPAN : (2 * m + 2) * SPAN] = low
-
-        return [functools.partial(piece, y) for y in pieces]
-
-    def depth_product(n):
-        def piece(m, lanes):
-            high = parts[n][:, 2 * m * SPAN : (2 * m + 1) * SPAN]
-            low = parts[n][:, (2 * m + 1) * SPAN : (2 * m + 2) * SPAN]
-            left = jnp.concatenate([high, low, high], axis=1)
-            post[n][:, lanes] = jnp.dot(left, w_ref[m], preferred_element_type=F32)
-
-        return [functools.partial(piece, m, lanes) for m, lanes in enumerate((near, far))]
-
-    def depth_points(n):
-        def piece(y):
-            r, y0 = where(n, y)
-            at, ys = slice(y, y + chunk), slice(y0, y0 + chunk)
-            even, odd = post[n][at, near], post[n][at, far]
-            o_ref[r, ys, near] = (first[n][at, near] + twice_gelu(even + odd)).astype(BF16)
-            done[n][at] = (first[n][at, far] + twice_gelu(even - odd)).astype(BF16)
-
-        return [functools.partial(piece, y) for y in pieces]
-
-    def finish(n):
-        def piece():
-            z = jnp.dot(done[n][...], flip_ref[...], preferred_element_type=F32).astype(BF16)
-            for at in range(0, unit, min(unit, width)):
-                r, y0 = where(n, at)
-                o_ref[r, y0 : y0 + min(unit, width), far] = z[at : at + min(unit, width)]
-
-        return [piece]
+    pieces = [(n, slice(y, y + chunk)) for n, y in enumerate(range(0, size, chunk))]
+    units = range(2)
+
+    def place(part, ys):
+        row, y = divmod(part * size + ys.start, width)
+        return row, slice(y, y + chunk)
 
     @pl.when(step == 0)
     def _():
-        expand(funcs, fine, r_ref, place_ref, b_ref)
+        expand(funcs, fine, r_ref, b_ref)
+
+    def run(lateral, depth):
+        def stream(weights, passes):
+            steps = []
+
+            def push(n):
+                for unit in units:
+                    pltpu.matmul_push_rhs(weights(n, unit), n % 2, unit)
+
+            def multiply(n, load, acc, left):
+                for unit in units:
+                    pltpu.matmul_acc_lhs(acc(unit), left(unit), load_staged_rhs=load)
+
+            for n, batch in enumerate(passes):
+                steps.append(functools.partial(push, n))
+                for m, (acc, left) in enumerate(batch):
+                    steps.append(functools.partial(multiply, n, n % 2 if m == 0 else None, acc, left))
+            return steps
+
+        def lateral_product(part):
+            row = place(part, pieces[0][1])[0]
+            batch = [
+                (
+                    lambda unit, n=n: lateral[part % 2][unit][n],
+                    lambda unit, ys=ys: by_ref[place(part, ys)[1]],
+                )
+                for n, ys in pieces
+            ]
+            lanes = (near, far)
+            return stream(lambda n, unit: b_ref[rows * step + row, :, lanes[unit]], [batch])
+
+        def depth_product(part):
+            def batch(low):
+                def left(unit, ys):
+                    at = (2 * unit + low) * SPAN
+                    return parts[part % 2][ys, at : at + SPAN]
+
+                return [
+                    (lambda unit, n=n: depth[part % 2][unit][n], lambda unit, ys=ys: left(unit, ys))
+                    for n, ys in pieces
+                ]
+
+            return stream(
+                lambda n, unit: w_ref[unit, n * SPAN : (n + 1) * SPAN], [batch(0) + batch(1), batch(0)]
+            )
+
+        def finish(part):
+            half = len(pieces) // 2
+            accs = lateral[part % 2 ^ 1]
+            batch = [
+                (
+                    lambda unit, n=n: accs[unit][n],
+                    lambda unit, n=n: done[part % 2][pieces[n + half * unit][1]],
+                )
+                for n in range(half)
+            ]
+
+            def pop(n):
+                for unit in units:
+                    row, at = place(part, pieces[n + half * unit][1])
+                    o_ref[row, at, far] = pltpu.matmul_pop(accs[unit][n]).astype(BF16)
+
+            return stream(lambda n, unit: flip_ref[...], [batch]) + [functools.partial(pop, n) for n in range(half)]
+
+        def lateral_points(part):
+            def piece(n, ys):
+                row, at = place(part, ys)
+                h0 = pltpu.matmul_pop(lateral[part % 2][0][n]) + x0_ref[row, at]
+                h1 = pltpu.matmul_pop(lateral[part % 2][1][n]) + x1_ref[row, at]
+                f0 = u_ref[row, at].astype(F32) + twice_gelu(h0)
+                f1 = f_ref[row, at].astype(F32) + twice_gelu(h1)
+                first[part % 2][ys, near] = f0
+                first[part % 2][ys, far] = f1
+                for m, value in enumerate((f0 + f1, f0 - f1)):
+                    high, low = split(value)
+                    parts[part % 2][ys, 2 * m * SPAN : (2 * m + 1) * SPAN] = high
+                    parts[part % 2][ys, (2 * m + 1) * SPAN : (2 * m + 2) * SPAN] = low
+
+            return [functools.partial(piece, n, ys) for n, ys in pieces]
+
+        def depth_points(part):
+            def piece(n, ys):
+                row, at = place(part, ys)
+                even, odd = pltpu.matmul_pop(depth[part % 2][0][n]), pltpu.matmul_pop(depth[part % 2][1][n])
+                o_ref[row, at, near] = (first[part % 2][ys, near] + twice_gelu(even + odd)).astype(BF16)
+                done[part % 2][ys] = (first[part % 2][ys, far] + twice_gelu(even - odd)).astype(BF16)
+
+            return [functools.partial(piece, n, ys) for n, ys in pieces]
+
         weave(lateral_product(0), [])
         weave(lateral_product(1), lateral_points(0))
         weave(depth_product(0), lateral_points(1))
-
-    @pl.when(jnp.logical_and(step > 0, step < last))
-    def _():
-        weave(depth_product(1), depth_points(0))
-        weave(lateral_product(0) + finish(0), depth_points(1))
-        weave(lateral_product(1) + finish(1), lateral_points(0))
-        weave(depth_product(0), lateral_points(1))
-
-    @pl.when(step == last)
-    def _():
-        weave(depth_product(1), depth_points(0))
-        weave(finish(0), depth_points(1))
-        weave(finish(1), [])
+        for part in range(count - 2):
+            weave(depth_product(part + 1) + lateral_product(part + 2), depth_points(part))
+            weave(finish(part), lateral_points(part + 2))
+        weave(depth_product(count - 1), depth_points(count - 2))
+        weave(finish(count - 2), depth_points(count - 1))
+        weave(finish(count - 1), [])
+
+    accs = [[[pltpu.ACC(unit)((chunk, SPAN), F32) for _ in pieces] for unit in units] for _ in range(2)]
+    pl.run_scoped(run, accs, accs)
 
 
 def twice_gelu(half):
@@ -409,7 +441,7 @@
 
     by_high, by_low = split64(basis_y)
     by_forward = np.concatenate([by_high, by_low], axis=0)
-    pairs = 2
+    pairs = 4
     steps = rows // (2 * pairs)
     sent = pl.pallas_call(
         functools.partial(forward_kernel, funcs, fine),
@@ -462,9 +494,10 @@
     order = np.zeros((LANE, LANE))
     order[ids, ids % chans * per_lane + ids // chans] = 1
     order = np.kron(np.eye(SPAN // LANE), order).astype(ml_dtypes.bfloat16)
+    place = jnp.where(me % halves == 1, order.T @ flip, order.T)
     mixed = pl.pallas_call(
         functools.partial(mix_kernel, count, fine),
-        in_specs=6 * [pl.BlockSpec(memory_space=pltpu.VMEM)] + [pl.BlockSpec(memory_space=pl.ANY)],
+        in_specs=7 * [pl.BlockSpec(memory_space=pltpu.VMEM)] + [pl.BlockSpec(memory_space=pl.ANY)],
         out_shape=jax.ShapeDtypeStruct((devices, packed, SPAN), BF16),
         scratch_shapes=[
             pltpu.VMEM((SPAN // LANE, a_forward.shape[1] * GROUP, LANE), F32),
@@ -472,7 +505,7 @@
         ],
         compiler_params=pltpu.CompilerParams(vmem_limit_bytes=48 * 2**20),
         name="mix",
-    )(gathered, a_forward, a_back, gains, diagonals(lat_modes), order, local_near)
+    )(gathered, a_forward, a_back, gains, diagonals(lat_modes), order, place, local_near)
     returned = lax.all_to_all(mixed, "lat", split_axis=0, concat_axis=0, tiled=True)
 
     local_far, mirrored = pl.pallas_call(
@@ -502,37 +535,30 @@
             "kz,kw,kcd->zcwd", b, b, depth_modes[parity::2], precision=highest
         ).reshape(SPAN, SPAN) + 0.25 * kron_eye(depth_local, per)
         high, low = split_outside(full)
-        return jnp.concatenate([high, high, low], axis=0)
-
-    place = np.stack([order.T, order.T @ flip])
+        return jnp.concatenate([high, low], axis=0)
+
     block = 4
-    unit = block * width_y // 2
-    wide = (unit, cells)
-    narrow = (unit, SPAN)
-    steps = rows // block
+    size = 256
     return pl.pallas_call(
-        functools.partial(tail_kernel, funcs, fine, 16),
-        grid=(steps + 1,),
+        functools.partial(tail_kernel, funcs, fine, 32),
+        grid=(rows // block,),
         in_specs=[
             pl.BlockSpec((devices, packed, SPAN), lambda s: (0, 0, 0)),
-            pl.BlockSpec((block, width_y, SPAN), lambda s: (jnp.minimum(s, steps - 1), 0, 0)),
-            pl.BlockSpec((block, width_y, SPAN), lambda s: (jnp.minimum(s, steps - 1), 0, 0)),
-            pl.BlockSpec((block, width_y, SPAN), lambda s: (jnp.minimum(s, steps - 1), 0, 0)),
-            pl.BlockSpec((block, width_y, SPAN), lambda s: (jnp.minimum(s, steps - 1), 0, 0)),
+            pl.BlockSpec((block, width_y, SPAN), lambda s: (s, 0, 0)),
+            pl.BlockSpec((block, width_y, SPAN), lambda s: (s, 0, 0)),
+            pl.BlockSpec((block, width_y, SPAN), lambda s: (s, 0, 0)),
+            pl.BlockSpec((block, width_y, SPAN), lambda s: (s, 0, 0)),
             pl.BlockSpec((width_y, SPAN), lambda s: (0, 0)),
-            pl.BlockSpec((2, 3 * SPAN, SPAN), lambda s: (0, 0, 0)),
-            pl.BlockSpec((2, SPAN, SPAN), lambda s: (0, 0, 0)),
+            pl.BlockSpec((2, 2 * SPAN, SPAN), lambda s: (0, 0, 0)),
             pl.BlockSpec((SPAN, SPAN), lambda s: (0, 0)),
         ],
-        out_specs=pl.BlockSpec((block, width_y, cells), lambda s: (jnp.maximum(s - 1, 0), 0, 0)),
+        out_specs=pl.BlockSpec((block, width_y, cells), lambda s: (s, 0, 0)),
         out_shape=jax.ShapeDtypeStruct(field.shape, BF16),
         scratch_shapes=[pltpu.VMEM((rows, 4 * modes_y, cells), BF16)]
-        + 2 * [pltpu.VMEM(wide, F32)]
-        + 2 * [pltpu.VMEM(wide, F32)]
-        + 2 * [pltpu.VMEM((unit, 4 * SPAN), BF16)]
-        + 2 * [pltpu.VMEM(wide, F32)]
-        + 2 * [pltpu.VMEM(narrow, BF16)],
-        compiler_params=pltpu.CompilerParams(vmem_limit_bytes=58 * 2**20),
+        + 2 * [pltpu.VMEM((size, cells), F32)]
+        + 2 * [pltpu.VMEM((size, 4 * SPAN), BF16)]
+        + 2 * [pltpu.VMEM((size, SPAN), BF16)],
+        compiler_params=pltpu.CompilerParams(vmem_limit_bytes=52 * 2**20),
         name="tail",
     )(
         returned,
@@ -542,7 +568,6 @@
         mirrored,
         by_back,
         jnp.stack([depth_matrix(0), depth_matrix(1)]),
-        place,
         flip,
     )
 

time: 139 us -> 140 us (level)
  Pallas kernels: 93.1 us -> 95.3 us
    pallas_call x2, Pallas kernels: 54.1 us -> 57.9 us  [the longest x1 51.3 us: shards(): pl.pallas_call(functools.partial(tail_kernel, funcs, fine, 32), grid=(row...]
    pallas_call x1, Pallas kernels: 11.5 us -> 9.9 us  [shards(): pl.pallas_call(functools.partial(forward_kernel, funcs, fine), grid=(step...]
  transfers between devices with their start and end apart: 2 -> 2, of which waited for: 1 -> 1; matrix products, arithmetic and copies ran while one was open for 16% -> 15% of each run, Pallas kernels for 20% -> 20%
where the time goes in v6:
time: 140 us; the launch traced here: 138 us
  Pallas kernels  95.3 us (68%)
  local copies, waits for them, and re-layouts  14.4 us (10%)
  starting transfers between devices  11.7 us (8%)
  waiting for transfers between devices  8.24 us (6%)
  matrix products  5.25 us (4%)
  other arithmetic  3.06 us (2%)
    pallas_call x1, Pallas kernels, shards(): pl.pallas_call(functools.partial(tail_kernel, funcs, fine, 32), grid=(row...  51.3 us
    pallas_call x1, Pallas kernels, shards(): pl.pallas_call(local_far_kernel, grid=(rows // four,), in_specs=[pl.Block...  14.8 us
    pallas_call x1, Pallas kernels, shards(): pl.pallas_call(local_near_kernel, grid=(rows // four,), in_specs=[pl.Bloc...  12.7 us
    pallas_call x1, Pallas kernels, shards(): pl.pallas_call(functools.partial(forward_kernel, funcs, fine), grid=(step...  9.9 us
    all_to_all x1, waiting for transfers between devices, shards(): lax.all_to_all(sent, 'lat', split_axis=0, concat_axis=0, tiled=True)  8.23 us
    all_to_all x1, starting transfers between devices, shards(): lax.all_to_all(sent, 'lat', split_axis=0, concat_axis=0, tiled=True)  6.69 us
    pallas_call x1, Pallas kernels, shards(): pl.pallas_call(functools.partial(mix_kernel, count, fine), in_specs=7 * [...  6.6 us
    add x4, local copies, waits for them, and re-layouts, depth_matrix(): 0.5 * jnp.einsum('kz,kw,kcd->zcwd', b, b, depth_modes[parity::2], precisi...  5.51 us
  transfers between devices with their start and end apart: 2, of which 1 were waited for; matrix products, arithmetic and copies ran while one was open for 15% of the time, Pallas kernels for 20%

profile of v6, /device:TPU:15, one launch (start us, length us, event | category | flops | bytes accessed | tf_op | source)
XLA Modules:
  0.0 138.3 jit_solution(11846796307613373464)
XLA Ops:
  0.0 0.9 copy-done.5
  0.9 9.9 %forward.1 = bf16[16,144,256]{2,1,0:T(8,128)(2,1)} custom-call(bf16[128,512]{1,0:T(8,128)(2,1)S(1)} %copy-done.5, bf16[32,512,512]{2,1,0:T(8,128)(2,1)} %u_ref.5, bf16[32,512,512]{2,1,0:T(8,128)(2,1)} %u_ref.5), custom_call_target="tpu_custom_call" | custom-call | tf_op jit(solution)/shard_map/forward/pallas_call | solution.py:446
  10.8 6.7 %all-to-all-start = ((bf16[16,144,256]{2,1,0:T(8,128)(2,1)}), bf16[16,144,256]{2,1,0:T(8,128)(2,1)S(1)}, u32[]{:S(2)}, u32[]{:S(2)}) async-start(bf16[16,144,256]{2,1,0:T(8,128)(2,1)} %forward.1), calls=%async_computation | async-start | bytes 2359296 | tf_op jit(solution)/shard_map/all_to_all | solution.py:463
  17.6 0.1 constant_dynamic-slice_fusion
  17.7 0.1 broadcast_in_dim.4
  17.8 0.1 tile.10
  17.9 0.6 multiply_reduce_fusion
  18.5 0.1 broadcast_bitcast_fusion
  18.6 0.3 copy.44.w_ref
  19.0 0.2 broadcast_multiply_fusion
  19.2 2.5 %copy.43 = f32[16,16,16,16]{3,2,1,0:T(8,128)} copy(f32[16,16,16,16]{3,0,1,2:T(8,128)S(1)} %broadcast_multiply_fusion) | data formatting | bytes 524288 | tf_op jit(solution)/shard_map/mul | solution.py:406
  21.7 2.4 %mul.108 = f32[256,256]{1,0:T(8,128)S(1)} reshape(f32[16,16,16,16]{3,2,1,0:T(8,128)} %copy.43) | data formatting | bytes 524288 | tf_op jit(solution)/shard_map/mul | solution.py:406
  24.3 12.7 %local_near.1.after_ref.x0_ref = f32[32,512,256]{2,1,0:T(8,128)} custom-call(bf16[32,512,512]{2,1,0:T(8,128)(2,1)} %u_ref.5, bf16[512,256]{1,0:T(8,128)(2,1)S(1)} %pad_maximum_fusion.1.l_ref), custom_call_target="tpu_custom_call" | custom-call | tf_op jit(solution)/shard_map/local_near/pallas_call | solution.py:471
  37.0 8.2 %all-to-all-done.r_ref = bf16[16,144,256]{2,1,0:T(8,128)(2,1)S(1)} async-done(((bf16[16,144,256]{2,1,0:T(8,128)(2,1)}), bf16[16,144,256]{2,1,0:T(8,128)(2,1)S(1)}, u32[]{:S(2)}, u32[]{:S(2)}) %all-to-all-start) | async-done | bytes 1179680 | tf_op jit(solution)/shard_map/all_to_all | solution.py:463
  45.3 6.6 %mix.1.after_ref = bf16[16,144,256]{2,1,0:T(8,128)(2,1)} custom-call(bf16[16,144,256]{2,1,0:T(8,128)(2,1)S(1)} %all-to-all-done.r_ref, bf16[128,256]{1,0:T(8,128)(2,1)S(1)} %copy-done.7, bf16[208,256]{1,0:T(8,128)(2,1)S(1)} %copy-done.6, f32[8,256]{1,0:T(8,128)S(1)} %broadcast_bitcast_fusion.1.g_ref, f32[16,64,128]{2,1,0:T(8,128)S(1)} %copy.44.w_ref, ...), custom_call_target="tpu_custom_call" | custom-call | tf_op jit(solution)/shard_map/mix/pallas_call | solution.py:498
  51.9 5.0 %all-to-all-start.1 = ((bf16[16,144,256]{2,1,0:T(8,128)(2,1)}), bf16[16,144,256]{2,1,0:T(8,128)(2,1)S(1)}, u32[]{:S(2)}, u32[]{:S(2)}) async-start(bf16[16,144,256]{2,1,0:T(8,128)(2,1)} %mix.1.after_ref), calls=%async_computation.1 | async-start | bytes 2359296 | tf_op jit(solution)/shard_map/all_to_all | solution.py:509
  57.0 0.1 mul.113
  57.1 0.1 mul.109
  57.2 0.1 mul.110
  57.4 0.1 copy.46.l_ref
  57.6 0.6 fusion.13
  58.2 2.2 %bitcast_add_fusion.1 = f32[16,16,16,16]{3,0,1,2:T(8,128)S(1)} fusion(f32[16,16]{1,0:T(8,128)S(1)} %copy-done.15, f32[16,16]{0,1:T(8,128)S(1)} %fusion.12, f32[8,16,16]{2,1,0:T(8,128)S(1)} %get-tuple-element.15, f32[8,16]{1,0:T(8,128)S(1)} %copy-done.17, f32[8,16]{0,1:T(8,128)S(1)} %copy-done.16), kind=kOutput, calls=%fused_computation.1 | convolution fusion | flops 6555648 | bytes 273408 | tf_op jit(solution)/shard_map/kz,kw,kcd->zcwd/dot_general | solution.py:534
  60.4 1.2 copy.49
  61.6 1.5 %add.23 = f32[256,256]{1,0:T(8,128)} reshape(f32[16,16,16,16]{3,2,1,0:T(8,128)S(1)} %copy.49) | data formatting | bytes 524288 | tf_op jit(solution)/shard_map/add | solution.py:534
  63.2 3.1 %bitcast_add_fusion = f32[16,16,16,16]{3,0,1,2:T(8,128)S(1)} fusion(f32[16,16]{1,0:T(8,128)S(1)} %copy-done.15, f32[16,16]{0,1:T(8,128)S(1)} %fusion.12, f32[8,16,16]{2,1,0:T(8,128)} %get-tuple-element.16, f32[8,16]{1,0:T(8,128)} %constant.72.clone, f32[8,16]{0,1:T(8,128)} %constant.77), kind=kOutput, calls=%fused_computation | convolution fusion | flops 6555648 | bytes 273408 | tf_op jit(solution)/shard_map/kz,kw,kcd->zcwd/dot_general | solution.py:534
  66.2 1.2 copy.52
  67.5 1.5 %add.25 = f32[256,256]{1,0:T(8,128)} reshape(f32[16,16,16,16]{3,2,1,0:T(8,128)S(1)} %copy.52) | data formatting | bytes 524288 | tf_op jit(solution)/shard_map/add | solution.py:534
  69.0 1.0 reduce-precision_convert_fusion.1
  70.0 1.0 reduce-precision_convert_fusion
  71.1 14.8 %local_far.1 = (f32[32,512,256]{2,1,0:T(8,128)}, bf16[32,512,256]{2,1,0:T(8,128)(2,1)}) custom-call(bf16[32,512,512]{2,1,0:T(8,128)(2,1)} %u_ref.5, bf16[512,256]{1,0:T(8,128)(2,1)S(1)} %copy.46.l_ref, bf16[256,256]{1,0:T(8,128)(2,1)S(1)} %copy-done.2, bf16[16,144,256]{2,1,0:T(8,128)(2,1)} %mix.1.after_ref), custom_call_target="tpu_custom_call" | custom-call | tf_op jit(solution)/shard_map/local_far/pallas_call | solution.py:511
  85.9 1.0 copy-done.8
  87.0 51.3 %tail.1 = bf16[32,512,512]{2,1,0:T(8,128)(2,1)} custom-call(bf16[16,144,256]{2,1,0:T(8,128)(2,1)} %copy-done.8, f32[32,512,256]{2,1,0:T(8,128)} %local_near.1.after_ref.x0_ref, f32[32,512,256]{2,1,0:T(8,128)} %get-tuple-element.7.x1_ref, bf16[32,512,512]{2,1,0:T(8,128)(2,1)} %u_ref.5, bf16[32,512,256]{2,1,0:T(8,128)(2,1)} %get-tuple-element.8.f_ref, ...), custom_call_target="tpu_custom_call" | custom-call | tf_op jit(solution)/shard_map/tail/pallas_call | solution.py:542
  (49 shorter events, 0.5 us)
Async XLA Ops:
  0.0 17.5 %copy-start = (f32[64,16]{0,1:T(8,128)S(1)}, f32[64,16]{0,1:T(8,128)}, u32[]{:S(2)}) copy-start(f32[64,16]{0,1:T(8,128)} %param.21) | copy-start | bytes 12292
  0.0 0.9 copy-start.5
  10.8 7.1 %copy-start.11 = (f32[64,16,16]{0,2,1:T(8,128)S(1)}, f32[64,16,16]{0,2,1:T(8,128)}, u32[]{:S(2)}) copy-start(f32[64,16,16]{0,2,1:T(8,128)} %param.20) | copy-start | bytes 196612
  10.8 7.1 %copy-start.12 = (f32[16,16,16]{2,1,0:T(8,128)S(1)}, f32[16,16,16]{2,1,0:T(8,128)}, u32[]{:S(2)}) copy-start(f32[16,16,16]{2,1,0:T(8,128)} %constant.74) | copy-start | bytes 49156
  10.8 34.4 %all-to-all-start = ((bf16[16,144,256]{2,1,0:T(8,128)(2,1)}), bf16[16,144,256]{2,1,0:T(8,128)(2,1)S(1)}, u32[]{:S(2)}, u32[]{:S(2)}) async-start(bf16[16,144,256]{2,1,0:T(8,128)(2,1)} %forward.1), calls=%async_computation | async-start | bytes 2359296 | tf_op jit(solution)/shard_map/all_to_all | solution.py:463
  17.5 1.5 %copy-start.14 = (f32[16,16]{1,0:T(8,128)S(1)}, f32[16,16]{1,0:T(8,128)}, u32[]{:S(2)}) copy-start(f32[16,16]{1,0:T(8,128)} %param.22) | copy-start | bytes 3076
  24.2 12.7 %copy-start.9 = (f32[256,256]{1,0:T(8,128)S(1)}, f32[256,256]{1,0:T(8,128)}, u32[]{:S(2)}) copy-start(f32[256,256]{1,0:T(8,128)} %constant.75) | copy-start | bytes 786436
  24.3 12.7 %copy-start.10 = (f32[256,256]{1,0:T(8,128)S(1)}, f32[256,256]{1,0:T(8,128)}, u32[]{:S(2)}) copy-start(f32[256,256]{1,0:T(8,128)} %constant.64.clone) | copy-start | bytes 786436
  24.3 21.0 %copy-start.4 = (bf16[256,256]{1,0:T(8,128)(2,1)S(1)}, bf16[256,256]{1,0:T(8,128)(2,1)}, u32[]{:S(2)}) copy-start(bf16[256,256]{1,0:T(8,128)(2,1)} %constant.69.clone.order_ref) | copy-start | bytes 393220
  24.3 21.0 %copy-start.6 = (bf16[208,256]{1,0:T(8,128)(2,1)S(1)}, bf16[208,256]{1,0:T(8,128)(2,1)}, u32[]{:S(2)}) copy-start(bf16[208,256]{1,0:T(8,128)(2,1)} %constant.68.clone.b_ref) | copy-start | bytes 319492
  24.3 21.0 %copy-start.7 = (bf16[128,256]{1,0:T(8,128)(2,1)S(1)}, bf16[128,256]{1,0:T(8,128)(2,1)}, u32[]{:S(2)}) copy-start(bf16[128,256]{1,0:T(8,128)(2,1)} %constant.67.clone.a_ref) | copy-start | bytes 196612
  51.9 5.7 %copy-start.13 = (f32[16,16,16]{2,1,0:T(8,128)S(1)}, f32[16,16,16]{2,1,0:T(8,128)}, u32[]{:S(2)}) copy-start(f32[16,16,16]{2,1,0:T(8,128)} %param.23) | copy-start | bytes 49156
  51.9 6.3 %copy-start.15 = (f32[16,16]{1,0:T(8,128)S(1)}, f32[16,16]{1,0:T(8,128)}, u32[]{:S(2)}) copy-start(f32[16,16]{1,0:T(8,128)} %param.24) | copy-start | bytes 3076
  51.9 6.3 %copy-start.16 = (f32[8,16]{0,1:T(8,128)S(1)}, f32[8,16]{0,1:T(8,128)}, u32[]{:S(2)}) copy-start(f32[8,16]{0,1:T(8,128)} %constant.76) | copy-start | bytes 1540
  51.9 6.3 %copy-start.17 = (f32[8,16]{1,0:T(8,128)S(1)}, f32[8,16]{1,0:T(8,128)}, u32[]{:S(2)}) copy-start(f32[8,16]{1,0:T(8,128)} %constant.71.clone) | copy-start | bytes 1540
  51.9 34.1 %all-to-all-start.1 = ((bf16[16,144,256]{2,1,0:T(8,128)(2,1)}), bf16[16,144,256]{2,1,0:T(8,128)(2,1)S(1)}, u32[]{:S(2)}, u32[]{:S(2)}) async-start(bf16[16,144,256]{2,1,0:T(8,128)(2,1)} %mix.1.after_ref), calls=%async_computation.1 | async-start | bytes 2359296 | tf_op jit(solution)/shard_map/all_to_all | solution.py:509
  69.0 2.1 %copy-start.2 = (bf16[256,256]{1,0:T(8,128)(2,1)S(1)}, bf16[256,256]{1,0:T(8,128)(2,1)}, u32[]{:S(2)}) copy-start(bf16[256,256]{1,0:T(8,128)(2,1)} %constant.70.clone.flip_ref) | copy-start | bytes 393220
  71.1 15.9 %copy-start.3 = (bf16[512,256]{1,0:T(8,128)(2,1)S(1)}, bf16[512,256]{1,0:T(8,128)(2,1)}, u32[]{:S(2)}) copy-start(bf16[512,256]{1,0:T(8,128)(2,1)} %constant.73.clone.by_ref) | copy-start | bytes 786436
  85.9 1.0 copy-start.8
  87.0 51.3 %copy-start.1 = (f32[64,16]{0,1:T(8,128)S(1)}, f32[64,16]{0,1:T(8,128)}, u32[]{:S(2)}) copy-start(f32[64,16]{0,1:T(8,128)} %param.21) | copy-start | bytes 12292

commit v7 on v5

--- a/solution.py
+++ b/solution.py
@@ -96,11 +96,6 @@
     return high, (array - high.astype(F32)).astype(BF16)
 
 
-def split_outside(array):
-    high = lax.reduce_precision(array, 8, 7)
-    return high.astype(BF16), (array - high).astype(BF16)
-
-
 def window_modes(rows, length, modes):
     place = np.arange(rows) - (rows - 1) / 2
     order = np.arange(modes)[:, None]
@@ -162,7 +157,7 @@
         pl.when(step == at)(functools.partial(body, at))
 
 
-def mix_kernel(count, fine, r_ref, a_ref, b_ref, g_ref, w_ref, order_ref, after_ref, o_ref, m_ref, back_ref):
+def mix_kernel(count, fine, r_ref, a_ref, b_ref, g_ref, w_ref, order_ref, place_ref, after_ref, o_ref, m_ref, back_ref):
     devices, packed, span = r_ref.shape
     modes_x = w_ref.shape[1]
     depth = a_ref.shape[1]
@@ -196,14 +191,13 @@
         for k, lanes in tiles:
             back_ref[k, pl.ds(q, devices * count, stride=GROUP), :] = z[:, lanes]
     for i in range(devices):
-        for k, lanes in tiles:
-            z = back_ref[k, i * highs : (i + 1) * highs]
-            high = z.astype(BF16).astype(F32)
-            low = z[:lows] - high[:lows]
-            o_ref[i, :, lanes] = jnp.concatenate([high, low], axis=0).astype(BF16)
-
-
-def expand(funcs, fine, r_ref, place_ref, b_ref):
+        z = jnp.concatenate([back_ref[k, i * highs : (i + 1) * highs] for k, _ in tiles], axis=1)
+        high = z.astype(BF16).astype(F32)
+        both = jnp.concatenate([high, z[:lows] - high[:lows]], axis=0).astype(BF16)
+        o_ref[i] = jnp.dot(both, place_ref[...], preferred_element_type=F32).astype(BF16)
+
+
+def expand(funcs, fine, r_ref, b_ref):
     count, rows = funcs.shape
     modes_y = b_ref.shape[1] // 4
     halves = b_ref.shape[2] // SPAN
@@ -214,7 +208,7 @@
             got = []
             for k in range(2):
                 block = r_ref[(2 * g + k) * halves + h]
-                got.append(jnp.dot(block, place_ref[h], preferred_element_type=F32))
+                got.append(block.astype(F32))
             for c in range(SPAN // LANE):
                 part = slice(c * LANE, (c + 1) * LANE)
                 modes = []
@@ -269,7 +263,28 @@
         done = until
 
 
-def tail_kernel(funcs, fine, chunk, r_ref, x0_ref, x1_ref, u_ref, f_ref, by_ref, w_ref, place_ref, flip_ref, o_ref, b_ref, *scratch):
+def prepare_kernel(l_ref, m_ref, d_ref, e_ref, et_ref, mask_ref, a_ref, b_ref, flip_ref, after_ref, near_ref, far_ref, w_ref):
+    highest = lax.Precision.HIGHEST
+
+    def dot(x, y):
+        return jnp.dot(x, y, preferred_element_type=F32, precision=highest)
+
+    def spread(ref):
+        return dot(dot(et_ref[...], ref[...]), e_ref[...]) * mask_ref[...]
+
+    for n, half in enumerate(split(0.5 * spread(l_ref))):
+        near_ref[n * SPAN : (n + 1) * SPAN] = half
+        far_ref[n * SPAN : (n + 1) * SPAN] = jnp.dot(half, flip_ref[...], preferred_element_type=F32).astype(BF16)
+    local = 0.25 * spread(d_ref)
+    for parity in range(2):
+        modes = jnp.concatenate([m_ref[k] for k in range(parity, m_ref.shape[0], 2)], axis=0)
+        full = dot(a_ref[parity], dot(modes, e_ref[...]) * b_ref[parity]) + local
+        high, low = split(full)
+        for n, half in enumerate((high, high, low)):
+            w_ref[parity, n * SPAN : (n + 1) * SPAN] = half
+
+
+def tail_kernel(funcs, fine, chunk, r_ref, x0_ref, x1_ref, u_ref, f_ref, by_ref, w_ref, flip_ref, o_ref, b_ref, *scratch):
     step = pl.program_id(0)
     last = pl.num_programs(0) - 1
     width = u_ref.shape[1]
@@ -337,7 +352,7 @@
 
     @pl.when(step == 0)
     def _():
-        expand(funcs, fine, r_ref, place_ref, b_ref)
+        expand(funcs, fine, r_ref, b_ref)
         weave(lateral_product(0), [])
         weave(lateral_product(1), lateral_points(0))
         weave(depth_product(0), lateral_points(1))
@@ -366,12 +381,6 @@
     picks = (ids[None, :, None] == (ids[None, None, :] - ids[:, None, None]) % n).astype(np.float32)
     rows = jnp.sum(matrices[None] * picks[:, None], axis=2)
     return jnp.repeat(rows, LANE // n, axis=2)
-
-
-def kron_eye(matrix, count):
-    *lead, n, m = matrix.shape
-    eye = jnp.eye(count, dtype=matrix.dtype)
-    return (eye[:, None, :, None] * matrix[..., None, :, None, :]).reshape(*lead, count * n, count * m)
 
 
 def fits(mesh_lat, rows, width_y, cells, chans, modes_x, modes_y):
@@ -388,7 +397,6 @@
 
 
 def shards(field, lat_modes, lat_gains, lat_local, depth_modes, depth_local):
-    highest = lax.Precision.HIGHEST
     devices = lax.axis_size("lat")
     rows, width_y, cells = field.shape
     modes_x, chans, _ = lat_modes.shape
@@ -409,7 +417,7 @@
 
     by_high, by_low = split64(basis_y)
     by_forward = np.concatenate([by_high, by_low], axis=0)
-    pairs = 2
+    pairs = 4
     steps = rows // (2 * pairs)
     sent = pl.pallas_call(
         functools.partial(forward_kernel, funcs, fine),
@@ -432,9 +440,25 @@
 
     per = SPAN // chans
     flip = np.kron(np.eye(per)[::-1], np.eye(chans)).astype(ml_dtypes.bfloat16)
-    local_high, local_low = split_outside(kron_eye(0.5 * lat_local, per))
-    local = jnp.concatenate([local_high, local_low], axis=0)
-    turned = local.reshape(2 * SPAN, per, chans)[:, ::-1].reshape(2 * SPAN, SPAN)
+    near_z = basis_z[:, :per]
+    ids = np.arange(SPAN)
+    pick = (np.arange(chans)[:, None] == ids[None, :] % chans).astype(np.float32)
+    mask = (ids[:, None] // chans == ids[None, :] // chans).astype(np.float32)
+    halved = [near_z[parity::2] for parity in range(2)]
+    outer = np.stack([0.5 * np.kron(b.T, np.eye(chans)) for b in halved]).astype(np.float32)
+    inner = np.stack([np.kron(b, np.ones((chans, chans))) for b in halved]).astype(np.float32)
+    anywhere = pl.BlockSpec(memory_space=pl.ANY)
+    local, turned, depth_weights = pl.pallas_call(
+        prepare_kernel,
+        in_specs=9 * [pl.BlockSpec(memory_space=pltpu.VMEM)] + [anywhere],
+        out_shape=[
+            jax.ShapeDtypeStruct((2 * SPAN, SPAN), BF16),
+            jax.ShapeDtypeStruct((2 * SPAN, SPAN), BF16),
+            jax.ShapeDtypeStruct((2, 3 * SPAN, SPAN), BF16),
+        ],
+        compiler_params=pltpu.CompilerParams(vmem_limit_bytes=24 * 2**20),
+        name="prepare",
+    )(lat_local, depth_modes, depth_local, pick, pick.T.copy(), mask, outer, inner, flip, sent)
     four = 4
     local_near = pl.pallas_call(
         local_near_kernel,
@@ -462,9 +486,10 @@
     order = np.zeros((LANE, LANE))
     order[ids, ids % chans * per_lane + ids // chans] = 1
     order = np.kron(np.eye(SPAN // LANE), order).astype(ml_dtypes.bfloat16)
+    place = jnp.where(me % halves == 1, order.T @ flip, order.T)
     mixed = pl.pallas_call(
         functools.partial(mix_kernel, count, fine),
-        in_specs=6 * [pl.BlockSpec(memory_space=pltpu.VMEM)] + [pl.BlockSpec(memory_space=pl.ANY)],
+        in_specs=7 * [pl.BlockSpec(memory_space=pltpu.VMEM)] + [pl.BlockSpec(memory_space=pl.ANY)],
         out_shape=jax.ShapeDtypeStruct((devices, packed, SPAN), BF16),
         scratch_shapes=[
             pltpu.VMEM((SPAN // LANE, a_forward.shape[1] * GROUP, LANE), F32),
@@ -472,7 +497,7 @@
         ],
         compiler_params=pltpu.CompilerParams(vmem_limit_bytes=48 * 2**20),
         name="mix",
-    )(gathered, a_forward, a_back, gains, diagonals(lat_modes), order, local_near)
+    )(gathered, a_forward, a_back, gains, diagonals(lat_modes), order, place, local_near)
     returned = lax.all_to_all(mixed, "lat", split_axis=0, concat_axis=0, tiled=True)
 
     local_far, mirrored = pl.pallas_call(
@@ -494,17 +519,6 @@
     )(field, turned, flip, mixed)
 
     by_back = np.concatenate([by_high, by_low, by_high, by_low], axis=0).T.copy()
-    near_z = basis_z[:, :per].astype(np.float32)
-
-    def depth_matrix(parity):
-        b = near_z[parity::2]
-        full = 0.5 * jnp.einsum(
-            "kz,kw,kcd->zcwd", b, b, depth_modes[parity::2], precision=highest
-        ).reshape(SPAN, SPAN) + 0.25 * kron_eye(depth_local, per)
-        high, low = split_outside(full)
-        return jnp.concatenate([high, high, low], axis=0)
-
-    place = np.stack([order.T, order.T @ flip])
     block = 4
     unit = block * width_y // 2
     wide = (unit, cells)
@@ -521,7 +535,6 @@
             pl.BlockSpec((block, width_y, SPAN), lambda s: (jnp.minimum(s, steps - 1), 0, 0)),
             pl.BlockSpec((width_y, SPAN), lambda s: (0, 0)),
             pl.BlockSpec((2, 3 * SPAN, SPAN), lambda s: (0, 0, 0)),
-            pl.BlockSpec((2, SPAN, SPAN), lambda s: (0, 0, 0)),
             pl.BlockSpec((SPAN, SPAN), lambda s: (0, 0)),
         ],
         out_specs=pl.BlockSpec((block, width_y, cells), lambda s: (jnp.maximum(s - 1, 0), 0, 0)),
@@ -541,8 +554,7 @@
         field,
         mirrored,
         by_back,
-        jnp.stack([depth_matrix(0), depth_matrix(1)]),
-        place,
+        depth_weights,
         flip,
     )
 

time: 139 us -> 133 us (0.957)
  waiting for transfers between devices: 8.3 us -> 20.8 us
  local copies, waits for them, and re-layouts: 14.4 us -> 5.9 us
  matrix products: 5.25 us -> 0 us
  other arithmetic: 3.99 us -> 0.64 us
    all_to_all x1, waiting for transfers between devices: 0.01 us -> 13 us  [shards(): lax.all_to_all(mixed, 'lat', split_axis=0, concat_axis=0, tiled=True)]
    add x4 -> x0, local copies, waits for them, and re-layouts: 5.51 us -> none  [depth_matrix(): 0.5 * jnp.einsum('kz,kw,kcd->zcwd', b, b, depth_modes[parity::2], precisi...]
    mul x7 -> x0, local copies, waits for them, and re-layouts: 5.36 us -> none  [the longest x6 5.29 us: kron_eye(): eye[:, None, :, None] * matrix[..., None, :, None, :]]
    dot_general x2 -> x0, matrix products: 5.25 us -> none  [depth_matrix(): jnp.einsum('kz,kw,kcd->zcwd', b, b, depth_modes[parity::2], precision=hig...]
    pallas_call x1 -> x2, Pallas kernels: 6.34 us -> 8.98 us  [the longest x1 6.62 us: shards(): pl.pallas_call(functools.partial(mix_kernel, count, fine), in_specs=7 * [...]
    reshape x2, local copies, waits for them, and re-layouts: 0.41 us -> 2.64 us  [diagonals(): return jnp.repeat(rows, LANE // n, axis=2)]
    convert_element_type x5 -> x0, other arithmetic: 2.09 us -> none  [the longest x4 2.08 us: split_outside(): return (high.astype(BF16), (array - high).astype(BF16))]
    pallas_call x1, Pallas kernels: 11.5 us -> 9.86 us  [shards(): pl.pallas_call(functools.partial(forward_kernel, funcs, fine), grid=(step...]
  transfers between devices with their start and end apart: 2 -> 2, of which waited for: 1 -> 2; matrix products, arithmetic and copies ran while one was open for 16% -> 3% of each run, Pallas kernels for 20% -> 23%
where the time goes in v7:
time: 133 us; the launch traced here: 132 us
  Pallas kernels  92.8 us (70%)
  waiting for transfers between devices  20.8 us (16%)
  starting transfers between devices  11.6 us (9%)
  local copies, waits for them, and re-layouts  5.9 us (4%)
    pallas_call x1, Pallas kernels, shards(): pl.pallas_call(functools.partial(tail_kernel, funcs, fine, 16), grid=(ste...  46.5 us
    pallas_call x1, Pallas kernels, shards(): pl.pallas_call(local_far_kernel, grid=(rows // four,), in_specs=[pl.Block...  14.8 us
    all_to_all x1, waiting for transfers between devices, shards(): lax.all_to_all(mixed, 'lat', split_axis=0, concat_axis=0, tiled=True)  13 us
    pallas_call x1, Pallas kernels, shards(): pl.pallas_call(local_near_kernel, grid=(rows // four,), in_specs=[pl.Bloc...  12.7 us
    pallas_call x1, Pallas kernels, shards(): pl.pallas_call(functools.partial(forward_kernel, funcs, fine), grid=(step...  9.86 us
    all_to_all x1, waiting for transfers between devices, shards(): lax.all_to_all(sent, 'lat', split_axis=0, concat_axis=0, tiled=True)  7.85 us
    all_to_all x1, starting transfers between devices, shards(): lax.all_to_all(sent, 'lat', split_axis=0, concat_axis=0, tiled=True)  6.69 us
    pallas_call x1, Pallas kernels, shards(): pl.pallas_call(functools.partial(mix_kernel, count, fine), in_specs=7 * [...  6.62 us
  transfers between devices with their start and end apart: 2, of which 2 were waited for; matrix products, arithmetic and copies ran while one was open for 3% of the time, Pallas kernels for 23%

profile of v7, /device:TPU:15, one launch (start us, length us, event | category | flops | bytes accessed | tf_op | source)
XLA Modules:
  0.0 132.1 jit_solution(7091128315981170187)
XLA Ops:
  0.0 0.9 copy-done.8
  0.9 9.9 %forward.1.after_ref = bf16[16,144,256]{2,1,0:T(8,128)(2,1)} custom-call(bf16[128,512]{1,0:T(8,128)(2,1)S(1)} %copy-done.8, bf16[32,512,512]{2,1,0:T(8,128)(2,1)} %u_ref.5, bf16[32,512,512]{2,1,0:T(8,128)(2,1)} %u_ref.5), custom_call_target="tpu_custom_call" | custom-call | tf_op jit(solution)/shard_map/forward/pallas_call | solution.py:422
  10.8 6.7 %all-to-all-start = ((bf16[16,144,256]{2,1,0:T(8,128)(2,1)}), bf16[16,144,256]{2,1,0:T(8,128)(2,1)S(1)}, u32[]{:S(2)}, u32[]{:S(2)}) async-start(bf16[16,144,256]{2,1,0:T(8,128)(2,1)} %forward.1.after_ref), calls=%async_computation | async-start | bytes 2359296 | tf_op jit(solution)/shard_map/all_to_all | solution.py:439
  17.5 0.0 copy-start.4
  17.5 0.0 copy-start.5
  17.5 0.0 copy-start.6
  17.5 0.0 copy-start.9
  17.5 0.0 copy-start.10
  17.5 0.0 copy-start.13
  17.6 0.0 copy-start.14
  17.6 0.0 copy-start.15
  17.6 0.1 constant_dynamic-slice_fusion
  17.7 0.1 copy.26
  17.8 0.1 broadcast_in_dim.7
  17.8 0.1 tile.10
  17.9 0.0 copy-done.19
  18.0 0.0 copy-done.20
  18.0 0.6 multiply_reduce_fusion
  18.6 1.1 broadcast_bitcast_fusion
  19.7 1.5 %copy.27.w_ref = f32[16,64,128]{2,1,0:T(8,128)S(1)} copy(f32[16,64,128]{1,2,0:T(8,128)} %broadcast_bitcast_fusion) | data formatting | bytes 1048576 | tf_op jit(solution)/shard_map/reshape | solution.py:383
  21.3 2.4 %prepare.1 = (bf16[512,256]{1,0:T(8,128)(2,1)S(1)}, bf16[512,256]{1,0:T(8,128)(2,1)S(1)}, bf16[2,768,256]{2,1,0:T(8,128)(2,1)S(1)}) custom-call(f32[16,16]{1,0:T(8,128)S(1)} %copy-done.14, f32[16,16,16]{2,1,0:T(8,128)S(1)} %copy-done.9, f32[16,16]{1,0:T(8,128)S(1)} %copy-done.15, f32[16,256]{1,0:T(8,128)S(1)} %copy-done.13, f32[256,16]{1,0:T(8,128)S(1)} %copy-done.10, ...), custom_call_target="tpu_custom_call" | custom-call | tf_op jit(solution)/shard_map/prepare/pallas_call | solution.py:451
  23.7 0.9 copy-done.3
  24.6 0.0 copy-start.12
  24.6 12.7 %local_near.1.after_ref.x0_ref = f32[32,512,256]{2,1,0:T(8,128)} custom-call(bf16[32,512,512]{2,1,0:T(8,128)(2,1)} %u_ref.5, bf16[512,256]{1,0:T(8,128)(2,1)S(1)} %get-tuple-element.10.l_ref), custom_call_target="tpu_custom_call" | custom-call | tf_op jit(solution)/shard_map/local_near/pallas_call | solution.py:463
  37.3 0.0 copy-done.18
  37.4 7.8 %all-to-all-done.r_ref = bf16[16,144,256]{2,1,0:T(8,128)(2,1)S(1)} async-done(((bf16[16,144,256]{2,1,0:T(8,128)(2,1)}), bf16[16,144,256]{2,1,0:T(8,128)(2,1)S(1)}, u32[]{:S(2)}, u32[]{:S(2)}) %all-to-all-start) | async-done | bytes 1179680 | tf_op jit(solution)/shard_map/all_to_all | solution.py:439
  45.2 6.6 %mix.1.after_ref = bf16[16,144,256]{2,1,0:T(8,128)(2,1)} custom-call(bf16[16,144,256]{2,1,0:T(8,128)(2,1)S(1)} %all-to-all-done.r_ref, bf16[128,256]{1,0:T(8,128)(2,1)S(1)} %copy-done.12, bf16[208,256]{1,0:T(8,128)(2,1)S(1)} %copy-done.11, f32[8,256]{1,0:T(8,128)S(1)} %broadcast_bitcast_fusion.1.g_ref, f32[16,64,128]{2,1,0:T(8,128)S(1)} %copy.27.w_ref, ...), custom_call_target="tpu_custom_call" | custom-call | tf_op jit(solution)/shard_map/mix/pallas_call | solution.py:490
  51.9 4.9 %all-to-all-start.1 = ((bf16[16,144,256]{2,1,0:T(8,128)(2,1)}), bf16[16,144,256]{2,1,0:T(8,128)(2,1)S(1)}, u32[]{:S(2)}, u32[]{:S(2)}) async-start(bf16[16,144,256]{2,1,0:T(8,128)(2,1)} %mix.1.after_ref), calls=%async_computation.1 | async-start | bytes 2359296 | tf_op jit(solution)/shard_map/all_to_all | solution.py:501
  56.7 14.8 %local_far.1 = (f32[32,512,256]{2,1,0:T(8,128)}, bf16[32,512,256]{2,1,0:T(8,128)(2,1)}) custom-call(bf16[32,512,512]{2,1,0:T(8,128)(2,1)} %u_ref.5, bf16[512,256]{1,0:T(8,128)(2,1)S(1)} %get-tuple-element.11.l_ref, bf16[256,256]{1,0:T(8,128)(2,1)S(1)} %copy-done.2, bf16[16,144,256]{2,1,0:T(8,128)(2,1)} %mix.1.after_ref), custom_call_target="tpu_custom_call" | custom-call | tf_op jit(solution)/shard_map/local_far/pallas_call | solution.py:503
  71.5 13.0 %all-to-all-done.1.r_ref = bf16[16,144,256]{2,1,0:T(8,128)(2,1)S(1)} async-done(((bf16[16,144,256]{2,1,0:T(8,128)(2,1)}), bf16[16,144,256]{2,1,0:T(8,128)(2,1)S(1)}, u32[]{:S(2)}, u32[]{:S(2)}) %all-to-all-start.1) | async-done | bytes 1179680 | tf_op jit(solution)/shard_map/all_to_all | solution.py:501
  84.5 1.0 copy-done.16
  85.5 46.5 %tail.1 = bf16[32,512,512]{2,1,0:T(8,128)(2,1)} custom-call(bf16[16,144,256]{2,1,0:T(8,128)(2,1)} %copy-done.16, f32[32,512,256]{2,1,0:T(8,128)} %local_near.1.after_ref.x0_ref, f32[32,512,256]{2,1,0:T(8,128)} %get-tuple-element.12.x1_ref, bf16[32,512,512]{2,1,0:T(8,128)(2,1)} %u_ref.5, bf16[32,512,256]{2,1,0:T(8,128)(2,1)} %get-tuple-element.13.f_ref, ...), custom_call_target="tpu_custom_call" | custom-call | tf_op jit(solution)/shard_map/tail/pallas_call | solution.py:527
  (29 shorter events, 0.1 us)
Async XLA Ops:
  0.0 17.6 %copy-start = (f32[64,16]{0,1:T(8,128)S(1)}, f32[64,16]{0,1:T(8,128)}, u32[]{:S(2)}) copy-start(f32[64,16]{0,1:T(8,128)} %param.22) | copy-start | bytes 12292
  0.0 0.9 copy-start.8
  10.8 7.2 %copy-start.19 = (f32[64,16,16]{0,2,1:T(8,128)S(1)}, f32[64,16,16]{0,2,1:T(8,128)}, u32[]{:S(2)}) copy-start(f32[64,16,16]{0,2,1:T(8,128)} %param.21) | copy-start | bytes 196612
  10.8 7.2 %copy-start.20 = (f32[16,16,16]{2,1,0:T(8,128)S(1)}, f32[16,16,16]{2,1,0:T(8,128)}, u32[]{:S(2)}) copy-start(f32[16,16,16]{2,1,0:T(8,128)} %constant.78) | copy-start | bytes 49156
  10.8 34.4 %all-to-all-start = ((bf16[16,144,256]{2,1,0:T(8,128)(2,1)}), bf16[16,144,256]{2,1,0:T(8,128)(2,1)S(1)}, u32[]{:S(2)}, u32[]{:S(2)}) async-start(bf16[16,144,256]{2,1,0:T(8,128)(2,1)} %forward.1.after_ref), calls=%async_computation | async-start | bytes 2359296 | tf_op jit(solution)/shard_map/all_to_all | solution.py:439
  17.5 3.8 %copy-start.2 = (bf16[256,256]{1,0:T(8,128)(2,1)S(1)}, bf16[256,256]{1,0:T(8,128)(2,1)}, u32[]{:S(2)}) copy-start(bf16[256,256]{1,0:T(8,128)(2,1)} %constant.70.clone.flip_ref) | copy-start | bytes 393220
  17.5 3.8 %copy-start.4 = (f32[2,128,256]{2,1,0:T(8,128)S(1)}, f32[2,128,256]{2,1,0:T(8,128)}, u32[]{:S(2)}) copy-start(f32[2,128,256]{2,1,0:T(8,128)} %constant.69.clone.b_ref) | copy-start | bytes 786436
  17.5 3.8 %copy-start.5 = (f32[2,256,128]{2,1,0:T(8,128)S(1)}, f32[2,256,128]{2,1,0:T(8,128)}, u32[]{:S(2)}) copy-start(f32[2,256,128]{2,1,0:T(8,128)} %constant.68.clone.a_ref) | copy-start | bytes 786436
  17.5 3.8 %copy-start.6 = (f32[256,256]{1,0:T(8,128)S(1)}, f32[256,256]{1,0:T(8,128)}, u32[]{:S(2)}) copy-start(f32[256,256]{1,0:T(8,128)} %constant.67.clone.mask_ref) | copy-start | bytes 786436
  17.5 3.7 %copy-start.9 = (f32[16,16,16]{2,1,0:T(8,128)S(1)}, f32[16,16,16]{2,1,0:T(8,128)}, u32[]{:S(2)}) copy-start(f32[16,16,16]{2,1,0:T(8,128)} %m_ref.1) | copy-start | bytes 49156
  17.5 3.7 %copy-start.10 = (f32[256,16]{1,0:T(8,128)S(1)}, f32[256,16]{1,0:T(8,128)}, u32[]{:S(2)}) copy-start(f32[256,16]{1,0:T(8,128)} %constant.66.clone.et_ref) | copy-start | bytes 49156
  17.5 3.7 %copy-start.13 = (f32[16,256]{1,0:T(8,128)S(1)}, f32[16,256]{1,0:T(8,128)}, u32[]{:S(2)}) copy-start(f32[16,256]{1,0:T(8,128)} %constant.65.clone.e_ref) | copy-start | bytes 49156
  17.6 3.7 %copy-start.14 = (f32[16,16]{1,0:T(8,128)S(1)}, f32[16,16]{1,0:T(8,128)}, u32[]{:S(2)}) copy-start(f32[16,16]{1,0:T(8,128)} %l_ref.1) | copy-start | bytes 3076
  17.6 3.7 %copy-start.15 = (f32[16,16]{1,0:T(8,128)S(1)}, f32[16,16]{1,0:T(8,128)}, u32[]{:S(2)}) copy-start(f32[16,16]{1,0:T(8,128)} %d_ref.1) | copy-start | bytes 3076
  23.7 0.9 copy-start.3
  24.6 12.7 %copy-start.17 = (f32[256,256]{1,0:T(8,128)S(1)}, f32[256,256]{1,0:T(8,128)}, u32[]{:S(2)}) copy-start(f32[256,256]{1,0:T(8,128)} %constant.79) | copy-start | bytes 786436
  24.6 12.7 %copy-start.18 = (f32[256,256]{1,0:T(8,128)S(1)}, f32[256,256]{1,0:T(8,128)}, u32[]{:S(2)}) copy-start(f32[256,256]{1,0:T(8,128)} %constant.71.clone) | copy-start | bytes 786436
  24.6 20.6 %copy-start.7 = (bf16[256,256]{1,0:T(8,128)(2,1)S(1)}, bf16[256,256]{1,0:T(8,128)(2,1)}, u32[]{:S(2)}) copy-start(bf16[256,256]{1,0:T(8,128)(2,1)} %constant.76.clone.order_ref) | copy-start | bytes 393220
  24.6 20.6 %copy-start.11 = (bf16[208,256]{1,0:T(8,128)(2,1)S(1)}, bf16[208,256]{1,0:T(8,128)(2,1)}, u32[]{:S(2)}) copy-start(bf16[208,256]{1,0:T(8,128)(2,1)} %constant.75.clone.b_ref) | copy-start | bytes 319492
  24.6 20.6 %copy-start.12 = (bf16[128,256]{1,0:T(8,128)(2,1)S(1)}, bf16[128,256]{1,0:T(8,128)(2,1)}, u32[]{:S(2)}) copy-start(bf16[128,256]{1,0:T(8,128)(2,1)} %constant.74.clone.a_ref) | copy-start | bytes 196612
  51.9 32.6 %all-to-all-start.1 = ((bf16[16,144,256]{2,1,0:T(8,128)(2,1)}), bf16[16,144,256]{2,1,0:T(8,128)(2,1)S(1)}, u32[]{:S(2)}, u32[]{:S(2)}) async-start(bf16[16,144,256]{2,1,0:T(8,128)(2,1)} %mix.1.after_ref), calls=%async_computation.1 | async-start | bytes 2359296 | tf_op jit(solution)/shard_map/all_to_all | solution.py:501
  84.5 1.0 copy-start.16
  85.5 46.5 %copy-start.1 = (f32[64,16]{0,1:T(8,128)S(1)}, f32[64,16]{0,1:T(8,128)}, u32[]{:S(2)}) copy-start(f32[64,16]{0,1:T(8,128)} %param.22) | copy-start | bytes 12292

commit v8 on v7

--- a/solution.py
+++ b/solution.py
@@ -197,45 +197,24 @@
         o_ref[i] = jnp.dot(both, place_ref[...], preferred_element_type=F32).astype(BF16)
 
 
-def expand(funcs, fine, r_ref, b_ref):
-    count, rows = funcs.shape
-    modes_y = b_ref.shape[1] // 4
+def expand(r_ref, v_ref, b_ref):
+    rows = b_ref.shape[0]
+    modes_y = b_ref.shape[1] // 2
     halves = b_ref.shape[2] // SPAN
-
-    def some(g, carry):
-        at = pl.multiple_of(g * 2 * GROUP, 2 * GROUP)
+    for g in range(modes_y // (2 * GROUP)):
+        at = g * 2 * GROUP
         for h in range(halves):
             got = []
             for k in range(2):
                 block = r_ref[(2 * g + k) * halves + h]
-                got.append(block.astype(F32))
-            for c in range(SPAN // LANE):
-                part = slice(c * LANE, (c + 1) * LANE)
-                modes = []
-                for j in range(count):
-                    pieces = []
-                    for k in range(2):
-                        piece = got[k][j * GROUP : (j + 1) * GROUP, part]
-                        if j < fine:
-                            low = got[k][(count + j) * GROUP : (count + j + 1) * GROUP, part]
-                            piece = piece + low
-                        pieces.append(piece)
-                    modes.append(jnp.concatenate(pieces, axis=0))
-                lanes = slice(h * SPAN + c * LANE, h * SPAN + (c + 1) * LANE)
-                for t in range(rows // 2):
-                    sums = []
-                    for parity in range(2):
-                        total = modes[parity] * float(0.5 * funcs[parity, t])
-                        for j in range(parity + 2, count, 2):
-                            total = total + modes[j] * float(0.5 * funcs[j, t])
-                        sums.append(total)
-                    for row, value in ((t, sums[0] + sums[1]), (rows - 1 - t, sums[0] - sums[1])):
-                        high, low = split(value)
-                        for n, half in enumerate((high, high, low, low)):
-                            b_ref[row, pl.ds(at + n * modes_y, 2 * GROUP), lanes] = half
-        return carry
-
-    lax.fori_loop(0, modes_y // (2 * GROUP), some, 0)
+                z = jnp.dot(v_ref[...], block, preferred_element_type=F32)
+                got.append(z[: rows * GROUP] + z[rows * GROUP :])
+            lanes = slice(h * SPAN, (h + 1) * SPAN)
+            for t in range(rows):
+                part = slice(t * GROUP, (t + 1) * GROUP)
+                high, low = split(jnp.concatenate([got[0][part], got[1][part]], axis=0))
+                b_ref[t, at : at + 2 * GROUP, lanes] = high
+                b_ref[t, modes_y + at : modes_y + at + 2 * GROUP, lanes] = low
 
 
 def local_near_kernel(u_ref, l_ref, x_ref):
@@ -284,11 +263,24 @@
             w_ref[parity, n * SPAN : (n + 1) * SPAN] = half
 
 
-def tail_kernel(funcs, fine, chunk, r_ref, x0_ref, x1_ref, u_ref, f_ref, by_ref, w_ref, flip_ref, o_ref, b_ref, *scratch):
+def tail_kernel(chunk, r_ref, x0_all, x1_all, u_all, f_all, by_ref, w_ref, flip_ref, v_ref, o_ref, b_ref, *scratch):
     step = pl.program_id(0)
     last = pl.num_programs(0) - 1
-    width = u_ref.shape[1]
     pre, first, parts, post, done = (scratch[n : n + 2] for n in range(0, 10, 2))
+    held, arrived = scratch[10:14], scratch[14]
+    block, width = held[0].shape[1:3]
+    modes_y = b_ref.shape[1] // 2
+    x0_ref, x1_ref, u_ref, f_ref = (ref.at[lax.rem(step, 2)] for ref in held)
+
+    def copies(at):
+        slot = lax.rem(at, 2)
+        return [
+            pltpu.make_async_copy(
+                source.at[pl.ds(at * block, block), :, pl.ds(0, SPAN)], ref.at[slot], arrived.at[slot, n]
+            )
+            for n, (source, ref) in enumerate(zip((x0_all, x1_all, u_all, f_all), held))
+        ]
+
     near, far = slice(0, SPAN), slice(SPAN, 2 * SPAN)
     unit = pre[0].shape[0]
     pieces = range(0, unit, chunk)
@@ -301,7 +293,8 @@
 
         def piece(at, lanes):
             r, y = where(n, at)
-            right = b_ref[u_ref.shape[0] * step + r, :, lanes]
+            high, low = b_ref[block * step + r, :modes_y, lanes], b_ref[block * step + r, modes_y:, lanes]
+            right = jnp.concatenate([high, high, low, low], axis=0)
             z = jnp.dot(by_ref[y : y + tall], right, preferred_element_type=F32)
             pre[n][at : at + tall, lanes] = z
 
@@ -352,7 +345,25 @@
 
     @pl.when(step == 0)
     def _():
-        expand(funcs, fine, r_ref, b_ref)
+        for copy in copies(step):
+            copy.start()
+
+    @pl.when(step < last - 1)
+    def _():
+        for copy in copies(step + 1):
+            copy.start()
+
+    @pl.when(step == 0)
+    def _():
+        expand(r_ref, v_ref, b_ref)
+
+    @pl.when(step < last)
+    def _():
+        for copy in copies(step):
+            copy.wait()
+
+    @pl.when(step == 0)
+    def _():
         weave(lateral_product(0), [])
         weave(lateral_product(1), lateral_points(0))
         weave(depth_product(0), lateral_points(1))
@@ -519,32 +530,35 @@
     )(field, turned, flip, mixed)
 
     by_back = np.concatenate([by_high, by_low, by_high, by_low], axis=0).T.copy()
+    slots = np.concatenate([funcs, funcs[:fine]], axis=0)
+    spread = np.concatenate(split64(np.kron(0.5 * slots.T, np.eye(GROUP))), axis=0)
     block = 4
     unit = block * width_y // 2
     wide = (unit, cells)
     narrow = (unit, SPAN)
     steps = rows // block
     return pl.pallas_call(
-        functools.partial(tail_kernel, funcs, fine, 16),
+        functools.partial(tail_kernel, 16),
         grid=(steps + 1,),
         in_specs=[
             pl.BlockSpec((devices, packed, SPAN), lambda s: (0, 0, 0)),
-            pl.BlockSpec((block, width_y, SPAN), lambda s: (jnp.minimum(s, steps - 1), 0, 0)),
-            pl.BlockSpec((block, width_y, SPAN), lambda s: (jnp.minimum(s, steps - 1), 0, 0)),
-            pl.BlockSpec((block, width_y, SPAN), lambda s: (jnp.minimum(s, steps - 1), 0, 0)),
-            pl.BlockSpec((block, width_y, SPAN), lambda s: (jnp.minimum(s, steps - 1), 0, 0)),
+            *(4 * [anywhere]),
             pl.BlockSpec((width_y, SPAN), lambda s: (0, 0)),
             pl.BlockSpec((2, 3 * SPAN, SPAN), lambda s: (0, 0, 0)),
             pl.BlockSpec((SPAN, SPAN), lambda s: (0, 0)),
+            pl.BlockSpec(spread.shape, lambda s: (0, 0)),
         ],
         out_specs=pl.BlockSpec((block, width_y, cells), lambda s: (jnp.maximum(s - 1, 0), 0, 0)),
         out_shape=jax.ShapeDtypeStruct(field.shape, BF16),
-        scratch_shapes=[pltpu.VMEM((rows, 4 * modes_y, cells), BF16)]
+        scratch_shapes=[pltpu.VMEM((rows, 2 * modes_y, cells), BF16)]
         + 2 * [pltpu.VMEM(wide, F32)]
         + 2 * [pltpu.VMEM(wide, F32)]
         + 2 * [pltpu.VMEM((unit, 4 * SPAN), BF16)]
         + 2 * [pltpu.VMEM(wide, F32)]
-        + 2 * [pltpu.VMEM(narrow, BF16)],
+        + 2 * [pltpu.VMEM(narrow, BF16)]
+        + 2 * [pltpu.VMEM((2, block, width_y, SPAN), F32)]
+        + 2 * [pltpu.VMEM((2, block, width_y, SPAN), BF16)]
+        + [pltpu.SemaphoreType.DMA((2, 4))],
         compiler_params=pltpu.CompilerParams(vmem_limit_bytes=58 * 2**20),
         name="tail",
     )(
@@ -556,6 +570,7 @@
         by_back,
         depth_weights,
         flip,
+        spread,
     )
 
 

time: 133 us -> 132 us (level)
  no operation moved by 1% of the time
where the time goes in v8:
time: 132 us; the launch traced here: 131 us
  Pallas kernels  91.9 us (70%)
  waiting for transfers between devices  20.8 us (16%)
  starting transfers between devices  11.6 us (9%)
  local copies, waits for them, and re-layouts  5.9 us (4%)
    pallas_call x1, Pallas kernels, shards(): pl.pallas_call(functools.partial(tail_kernel, 16), grid=(steps + 1,), in_...  45.6 us
    pallas_call x1, Pallas kernels, shards(): pl.pallas_call(local_far_kernel, grid=(rows // four,), in_specs=[pl.Block...  14.8 us
    all_to_all x1, waiting for transfers between devices, shards(): lax.all_to_all(mixed, 'lat', split_axis=0, concat_axis=0, tiled=True)  13 us
    pallas_call x1, Pallas kernels, shards(): pl.pallas_call(local_near_kernel, grid=(rows // four,), in_specs=[pl.Bloc...  12.7 us
    pallas_call x1, Pallas kernels, shards(): pl.pallas_call(functools.partial(forward_kernel, funcs, fine), grid=(step...  9.86 us
    all_to_all x1, waiting for transfers between devices, shards(): lax.all_to_all(sent, 'lat', split_axis=0, concat_axis=0, tiled=True)  7.85 us
    all_to_all x1, starting transfers between devices, shards(): lax.all_to_all(sent, 'lat', split_axis=0, concat_axis=0, tiled=True)  6.69 us
    pallas_call x1, Pallas kernels, shards(): pl.pallas_call(functools.partial(mix_kernel, count, fine), in_specs=7 * [...  6.63 us
  transfers between devices with their start and end apart: 2, of which 2 were waited for; matrix products, arithmetic and copies ran while one was open for 3% of the time, Pallas kernels for 23%

profile of v8, /device:TPU:15, one launch (start us, length us, event | category | flops | bytes accessed | tf_op | source)
XLA Modules:
  0.0 131.3 jit_solution(9034092136869530857)
XLA Ops:
  0.0 0.0 copy-start
  0.0 0.9 copy-done.8
  0.9 9.9 %forward.1.after_ref = bf16[16,144,256]{2,1,0:T(8,128)(2,1)} custom-call(bf16[128,512]{1,0:T(8,128)(2,1)S(1)} %copy-done.8, bf16[32,512,512]{2,1,0:T(8,128)(2,1)} %u_all.1, bf16[32,512,512]{2,1,0:T(8,128)(2,1)} %u_all.1), custom_call_target="tpu_custom_call" | custom-call | tf_op jit(solution)/shard_map/forward/pallas_call | solution.py:433
  10.8 6.7 %all-to-all-start = ((bf16[16,144,256]{2,1,0:T(8,128)(2,1)}), bf16[16,144,256]{2,1,0:T(8,128)(2,1)S(1)}, u32[]{:S(2)}, u32[]{:S(2)}) async-start(bf16[16,144,256]{2,1,0:T(8,128)(2,1)} %forward.1.after_ref), calls=%async_computation | async-start | bytes 2359296 | tf_op jit(solution)/shard_map/all_to_all | solution.py:450
  17.5 0.0 copy-start.4
  17.5 0.0 copy-start.5
  17.5 0.0 copy-start.6
  17.5 0.0 copy-start.9
  17.5 0.0 copy-start.10
  17.5 0.0 copy-start.13
  17.6 0.0 copy-start.14
  17.6 0.0 copy-start.15
  17.6 0.0 copy-done
  17.6 0.1 constant_dynamic-slice_fusion
  17.7 0.1 copy.27
  17.8 0.1 broadcast_in_dim.7
  17.8 0.1 tile.10
  18.0 0.6 multiply_reduce_fusion
  18.6 1.1 broadcast_bitcast_fusion
  19.7 1.5 %copy.28.w_ref = f32[16,64,128]{2,1,0:T(8,128)S(1)} copy(f32[16,64,128]{1,2,0:T(8,128)} %broadcast_bitcast_fusion) | data formatting | bytes 1048576 | tf_op jit(solution)/shard_map/reshape | solution.py:394
  21.3 2.4 %prepare.1 = (bf16[512,256]{1,0:T(8,128)(2,1)S(1)}, bf16[512,256]{1,0:T(8,128)(2,1)S(1)}, bf16[2,768,256]{2,1,0:T(8,128)(2,1)S(1)}) custom-call(f32[16,16]{1,0:T(8,128)S(1)} %copy-done.14, f32[16,16,16]{2,1,0:T(8,128)S(1)} %copy-done.9, f32[16,16]{1,0:T(8,128)S(1)} %copy-done.15, f32[16,256]{1,0:T(8,128)S(1)} %copy-done.13, f32[256,16]{1,0:T(8,128)S(1)} %copy-done.10, ...), custom_call_target="tpu_custom_call" | custom-call | tf_op jit(solution)/shard_map/prepare/pallas_call | solution.py:462
  23.7 0.9 copy-done.3
  24.6 0.0 copy-start.12
  24.6 12.7 %local_near.1.after_ref.x0_all = f32[32,512,256]{2,1,0:T(8,128)} custom-call(bf16[32,512,512]{2,1,0:T(8,128)(2,1)} %u_all.1, bf16[512,256]{1,0:T(8,128)(2,1)S(1)} %get-tuple-element.10.l_ref), custom_call_target="tpu_custom_call" | custom-call | tf_op jit(solution)/shard_map/local_near/pallas_call | solution.py:474
  37.4 7.8 %all-to-all-done.r_ref = bf16[16,144,256]{2,1,0:T(8,128)(2,1)S(1)} async-done(((bf16[16,144,256]{2,1,0:T(8,128)(2,1)}), bf16[16,144,256]{2,1,0:T(8,128)(2,1)S(1)}, u32[]{:S(2)}, u32[]{:S(2)}) %all-to-all-start) | async-done | bytes 1179680 | tf_op jit(solution)/shard_map/all_to_all | solution.py:450
  45.2 0.0 copy-done.11
  45.2 6.6 %mix.1.after_ref = bf16[16,144,256]{2,1,0:T(8,128)(2,1)} custom-call(bf16[16,144,256]{2,1,0:T(8,128)(2,1)S(1)} %all-to-all-done.r_ref, bf16[128,256]{1,0:T(8,128)(2,1)S(1)} %copy-done.12, bf16[208,256]{1,0:T(8,128)(2,1)S(1)} %copy-done.11, f32[8,256]{1,0:T(8,128)S(1)} %broadcast_bitcast_fusion.1.g_ref, f32[16,64,128]{2,1,0:T(8,128)S(1)} %copy.28.w_ref, ...), custom_call_target="tpu_custom_call" | custom-call | tf_op jit(solution)/shard_map/mix/pallas_call | solution.py:501
  51.9 4.9 %all-to-all-start.1 = ((bf16[16,144,256]{2,1,0:T(8,128)(2,1)}), bf16[16,144,256]{2,1,0:T(8,128)(2,1)S(1)}, u32[]{:S(2)}, u32[]{:S(2)}) async-start(bf16[16,144,256]{2,1,0:T(8,128)(2,1)} %mix.1.after_ref), calls=%async_computation.1 | async-start | bytes 2359296 | tf_op jit(solution)/shard_map/all_to_all | solution.py:512
  56.7 14.8 %local_far.1 = (f32[32,512,256]{2,1,0:T(8,128)}, bf16[32,512,256]{2,1,0:T(8,128)(2,1)}) custom-call(bf16[32,512,512]{2,1,0:T(8,128)(2,1)} %u_all.1, bf16[512,256]{1,0:T(8,128)(2,1)S(1)} %get-tuple-element.11.l_ref, bf16[256,256]{1,0:T(8,128)(2,1)S(1)} %copy-done.2, bf16[16,144,256]{2,1,0:T(8,128)(2,1)} %mix.1.after_ref), custom_call_target="tpu_custom_call" | custom-call | tf_op jit(solution)/shard_map/local_far/pallas_call | solution.py:514
  71.5 13.0 %all-to-all-done.1.r_ref = bf16[16,144,256]{2,1,0:T(8,128)(2,1)S(1)} async-done(((bf16[16,144,256]{2,1,0:T(8,128)(2,1)}), bf16[16,144,256]{2,1,0:T(8,128)(2,1)S(1)}, u32[]{:S(2)}, u32[]{:S(2)}) %all-to-all-start.1) | async-done | bytes 1179680 | tf_op jit(solution)/shard_map/all_to_all | solution.py:512
  84.5 1.0 copy-done.16
  85.5 45.6 %tail.1 = bf16[32,512,512]{2,1,0:T(8,128)(2,1)} custom-call(bf16[16,144,256]{2,1,0:T(8,128)(2,1)} %copy-done.16, f32[32,512,256]{2,1,0:T(8,128)} %local_near.1.after_ref.x0_all, f32[32,512,256]{2,1,0:T(8,128)} %get-tuple-element.12.x1_all, bf16[32,512,512]{2,1,0:T(8,128)(2,1)} %u_all.1, bf16[32,512,256]{2,1,0:T(8,128)(2,1)} %get-tuple-element.13.f_all, ...), custom_call_target="tpu_custom_call" | custom-call | tf_op jit(solution)/shard_map/tail/pallas_call | solution.py:540
  (29 shorter events, 0.1 us)
Async XLA Ops:
  0.0 17.6 %copy-start = (f32[64,16]{0,1:T(8,128)S(1)}, f32[64,16]{0,1:T(8,128)}, u32[]{:S(2)}) copy-start(f32[64,16]{0,1:T(8,128)} %param.23) | copy-start | bytes 12292
  0.0 0.9 copy-start.8
  10.8 7.2 %copy-start.19 = (f32[64,16,16]{0,2,1:T(8,128)S(1)}, f32[64,16,16]{0,2,1:T(8,128)}, u32[]{:S(2)}) copy-start(f32[64,16,16]{0,2,1:T(8,128)} %param.22) | copy-start | bytes 196612
  10.8 7.2 %copy-start.20 = (f32[16,16,16]{2,1,0:T(8,128)S(1)}, f32[16,16,16]{2,1,0:T(8,128)}, u32[]{:S(2)}) copy-start(f32[16,16,16]{2,1,0:T(8,128)} %constant.81) | copy-start | bytes 49156
  10.8 34.4 %all-to-all-start = ((bf16[16,144,256]{2,1,0:T(8,128)(2,1)}), bf16[16,144,256]{2,1,0:T(8,128)(2,1)S(1)}, u32[]{:S(2)}, u32[]{:S(2)}) async-start(bf16[16,144,256]{2,1,0:T(8,128)(2,1)} %forward.1.after_ref), calls=%async_computation | async-start | bytes 2359296 | tf_op jit(solution)/shard_map/all_to_all | solution.py:450
  17.5 3.8 %copy-start.2 = (bf16[256,256]{1,0:T(8,128)(2,1)S(1)}, bf16[256,256]{1,0:T(8,128)(2,1)}, u32[]{:S(2)}) copy-start(bf16[256,256]{1,0:T(8,128)(2,1)} %constant.72.clone.flip_ref) | copy-start | bytes 393220
  17.5 3.8 %copy-start.4 = (f32[2,128,256]{2,1,0:T(8,128)S(1)}, f32[2,128,256]{2,1,0:T(8,128)}, u32[]{:S(2)}) copy-start(f32[2,128,256]{2,1,0:T(8,128)} %constant.71.clone.b_ref) | copy-start | bytes 786436
  17.5 3.8 %copy-start.5 = (f32[2,256,128]{2,1,0:T(8,128)S(1)}, f32[2,256,128]{2,1,0:T(8,128)}, u32[]{:S(2)}) copy-start(f32[2,256,128]{2,1,0:T(8,128)} %constant.70.clone.a_ref) | copy-start | bytes 786436
  17.5 3.8 %copy-start.6 = (f32[256,256]{1,0:T(8,128)S(1)}, f32[256,256]{1,0:T(8,128)}, u32[]{:S(2)}) copy-start(f32[256,256]{1,0:T(8,128)} %constant.69.clone.mask_ref) | copy-start | bytes 786436
  17.5 3.7 %copy-start.9 = (f32[16,16,16]{2,1,0:T(8,128)S(1)}, f32[16,16,16]{2,1,0:T(8,128)}, u32[]{:S(2)}) copy-start(f32[16,16,16]{2,1,0:T(8,128)} %m_ref.1) | copy-start | bytes 49156
  17.5 3.7 %copy-start.10 = (f32[256,16]{1,0:T(8,128)S(1)}, f32[256,16]{1,0:T(8,128)}, u32[]{:S(2)}) copy-start(f32[256,16]{1,0:T(8,128)} %constant.68.clone.et_ref) | copy-start | bytes 49156
  17.5 3.7 %copy-start.13 = (f32[16,256]{1,0:T(8,128)S(1)}, f32[16,256]{1,0:T(8,128)}, u32[]{:S(2)}) copy-start(f32[16,256]{1,0:T(8,128)} %constant.67.clone.e_ref) | copy-start | bytes 49156
  17.6 3.7 %copy-start.14 = (f32[16,16]{1,0:T(8,128)S(1)}, f32[16,16]{1,0:T(8,128)}, u32[]{:S(2)}) copy-start(f32[16,16]{1,0:T(8,128)} %l_ref.1) | copy-start | bytes 3076
  17.6 3.7 %copy-start.15 = (f32[16,16]{1,0:T(8,128)S(1)}, f32[16,16]{1,0:T(8,128)}, u32[]{:S(2)}) copy-start(f32[16,16]{1,0:T(8,128)} %d_ref.1) | copy-start | bytes 3076
  23.7 0.9 copy-start.3
  24.6 12.7 %copy-start.17 = (f32[256,256]{1,0:T(8,128)S(1)}, f32[256,256]{1,0:T(8,128)}, u32[]{:S(2)}) copy-start(f32[256,256]{1,0:T(8,128)} %constant.82) | copy-start | bytes 786436
  24.6 12.7 %copy-start.18 = (f32[256,256]{1,0:T(8,128)S(1)}, f32[256,256]{1,0:T(8,128)}, u32[]{:S(2)}) copy-start(f32[256,256]{1,0:T(8,128)} %constant.73.clone) | copy-start | bytes 786436
  24.6 20.6 %copy-start.7 = (bf16[256,256]{1,0:T(8,128)(2,1)S(1)}, bf16[256,256]{1,0:T(8,128)(2,1)}, u32[]{:S(2)}) copy-start(bf16[256,256]{1,0:T(8,128)(2,1)} %constant.78.clone.order_ref) | copy-start | bytes 393220
  24.6 20.6 %copy-start.11 = (bf16[208,256]{1,0:T(8,128)(2,1)S(1)}, bf16[208,256]{1,0:T(8,128)(2,1)}, u32[]{:S(2)}) copy-start(bf16[208,256]{1,0:T(8,128)(2,1)} %constant.77.clone.b_ref) | copy-start | bytes 319492
  24.6 20.6 %copy-start.12 = (bf16[128,256]{1,0:T(8,128)(2,1)S(1)}, bf16[128,256]{1,0:T(8,128)(2,1)}, u32[]{:S(2)}) copy-start(bf16[128,256]{1,0:T(8,128)(2,1)} %constant.76.clone.a_ref) | copy-start | bytes 196612
  51.9 32.6 %all-to-all-start.1 = ((bf16[16,144,256]{2,1,0:T(8,128)(2,1)}), bf16[16,144,256]{2,1,0:T(8,128)(2,1)S(1)}, u32[]{:S(2)}, u32[]{:S(2)}) async-start(bf16[16,144,256]{2,1,0:T(8,128)(2,1)} %mix.1.after_ref), calls=%async_computation.1 | async-start | bytes 2359296 | tf_op jit(solution)/shard_map/all_to_all | solution.py:512
  84.5 1.0 copy-start.16
  85.5 45.6 %copy-start.1 = (f32[64,16]{0,1:T(8,128)S(1)}, f32[64,16]{0,1:T(8,128)}, u32[]{:S(2)}) copy-start(f32[64,16]{0,1:T(8,128)} %param.23) | copy-start | bytes 12292

commit v9 on v8

--- a/solution.py
+++ b/solution.py
@@ -157,14 +157,16 @@
         pl.when(step == at)(functools.partial(body, at))
 
 
-def mix_kernel(count, fine, r_ref, a_ref, b_ref, g_ref, w_ref, order_ref, place_ref, after_ref, o_ref, m_ref, back_ref):
+def mix_kernel(count, fine, r_ref, a_ref, b_ref, g_ref, w_ref, order_ref, place_ref, after_ref, o_ref, m_ref, back_ref, send_ref):
     devices, packed, span = r_ref.shape
     modes_x = w_ref.shape[1]
     depth = a_ref.shape[1]
     highs, lows = count * GROUP, fine * GROUP
     tiles = [(k, slice(k * LANE, (k + 1) * LANE)) for k in range(span // LANE)]
+    ordered = r_ref[...].reshape(devices * packed, span)
+    ordered = jnp.dot(ordered, order_ref[...], preferred_element_type=F32)
     for i in range(devices):
-        got = jnp.dot(r_ref[i], order_ref[...], preferred_element_type=F32)
+        got = ordered[i * packed : (i + 1) * packed]
         for k, lanes in tiles:
             m_ref[k, i * highs : i * highs + lows] = got[:lows, lanes] + got[highs:, lanes]
             m_ref[k, i * highs + lows : (i + 1) * highs] = got[lows:highs, lanes]
@@ -193,8 +195,9 @@
     for i in range(devices):
         z = jnp.concatenate([back_ref[k, i * highs : (i + 1) * highs] for k, _ in tiles], axis=1)
         high = z.astype(BF16).astype(F32)
-        both = jnp.concatenate([high, z[:lows] - high[:lows]], axis=0).astype(BF16)
-        o_ref[i] = jnp.dot(both, place_ref[...], preferred_element_type=F32).astype(BF16)
+        send_ref[i * packed : (i + 1) * packed] = jnp.concatenate([high, z[:lows] - high[:lows]], axis=0).astype(BF16)
+    z = jnp.dot(send_ref[...], place_ref[...], preferred_element_type=F32)
+    o_ref[...] = z.astype(BF16).reshape(devices, packed, span)
 
 
 def expand(r_ref, v_ref, b_ref):
@@ -505,6 +508,7 @@
         scratch_shapes=[
             pltpu.VMEM((SPAN // LANE, a_forward.shape[1] * GROUP, LANE), F32),
             pltpu.VMEM((SPAN // LANE, devices * count * GROUP, LANE), F32),
+            pltpu.VMEM((devices * packed, SPAN), BF16),
         ],
         compiler_params=pltpu.CompilerParams(vmem_limit_bytes=48 * 2**20),
         name="mix",
@@ -559,7 +563,7 @@
         + 2 * [pltpu.VMEM((2, block, width_y, SPAN), F32)]
         + 2 * [pltpu.VMEM((2, block, width_y, SPAN), BF16)]
         + [pltpu.SemaphoreType.DMA((2, 4))],
-        compiler_params=pltpu.CompilerParams(vmem_limit_bytes=58 * 2**20),
+        compiler_params=pltpu.CompilerParams(vmem_limit_bytes=50 * 2**20),
         name="tail",
     )(
         returned,

time: 132 us -> 129 us (0.977)
  Pallas kernels: 91.9 us -> 89.8 us
  waiting for transfers between devices: 20.8 us -> 19.2 us
    unnamed x42 -> x44, local copies, waits for them, and re-layouts: 2.94 us -> 5.22 us
    reshape x2, local copies, waits for them, and re-layouts: 2.64 us -> 0.41 us  [diagonals(): return jnp.repeat(rows, LANE // n, axis=2)]
    pallas_call x1, Pallas kernels: 45.6 us -> 43.6 us  [shards(): pl.pallas_call(functools.partial(tail_kernel, 16), grid=(steps + 1,), in_...]
    all_to_all x1, waiting for transfers between devices: 7.85 us -> 6.28 us  [shards(): lax.all_to_all(sent, 'lat', split_axis=0, concat_axis=0, tiled=True)]
  transfers between devices with their start and end apart: 2 -> 2, of which waited for: 2 -> 2; matrix products, arithmetic and copies ran while one was open for 3% -> 2% of each run, Pallas kernels for 23% -> 23%
where the time goes in v9:
time: 129 us; the launch traced here: 128 us
  Pallas kernels  89.8 us (70%)
  waiting for transfers between devices  19.2 us (15%)
  starting transfers between devices  11.6 us (9%)
  local copies, waits for them, and re-layouts  6.55 us (5%)
    pallas_call x1, Pallas kernels, shards(): pl.pallas_call(functools.partial(tail_kernel, 16), grid=(steps + 1,), in_...  43.6 us
    pallas_call x1, Pallas kernels, shards(): pl.pallas_call(local_far_kernel, grid=(rows // four,), in_specs=[pl.Block...  14.8 us
    all_to_all x1, waiting for transfers between devices, shards(): lax.all_to_all(mixed, 'lat', split_axis=0, concat_axis=0, tiled=True)  12.9 us
    pallas_call x1, Pallas kernels, shards(): pl.pallas_call(local_near_kernel, grid=(rows // four,), in_specs=[pl.Bloc...  12.7 us
    pallas_call x1, Pallas kernels, shards(): pl.pallas_call(functools.partial(forward_kernel, funcs, fine), grid=(step...  9.86 us
    all_to_all x1, starting transfers between devices, shards(): lax.all_to_all(sent, 'lat', split_axis=0, concat_axis=0, tiled=True)  6.69 us
    pallas_call x1, Pallas kernels, shards(): pl.pallas_call(functools.partial(mix_kernel, count, fine), in_specs=7 * [...  6.44 us
    all_to_all x1, waiting for transfers between devices, shards(): lax.all_to_all(sent, 'lat', split_axis=0, concat_axis=0, tiled=True)  6.28 us
  transfers between devices with their start and end apart: 2, of which 2 were waited for; matrix products, arithmetic and copies ran while one was open for 2% of the time, Pallas kernels for 23%

profile of v9, /device:TPU:15, one launch (start us, length us, event | category | flops | bytes accessed | tf_op | source)
XLA Modules:
  0.0 128.1 jit_solution(13124213684139929522)
XLA Ops:
  0.0 0.9 copy-done.9
  0.9 9.9 %forward.1.after_ref = bf16[16,144,256]{2,1,0:T(8,128)(2,1)} custom-call(bf16[128,512]{1,0:T(8,128)(2,1)S(1)} %copy-done.9, bf16[32,512,512]{2,1,0:T(8,128)(2,1)} %u_all.1, bf16[32,512,512]{2,1,0:T(8,128)(2,1)} %u_all.1), custom_call_target="tpu_custom_call" | custom-call | tf_op jit(solution)/shard_map/forward/pallas_call | solution.py:436
  10.8 6.7 %all-to-all-start = ((bf16[16,144,256]{2,1,0:T(8,128)(2,1)}), bf16[16,144,256]{2,1,0:T(8,128)(2,1)S(1)}, u32[]{:S(2)}, u32[]{:S(2)}) async-start(bf16[16,144,256]{2,1,0:T(8,128)(2,1)} %forward.1.after_ref), calls=%async_computation | async-start | bytes 2359296 | tf_op jit(solution)/shard_map/all_to_all | solution.py:453
  17.5 0.0 copy-start.5
  17.5 0.0 copy-start.10
  17.6 0.1 constant_dynamic-slice_fusion
  17.6 0.1 copy.27
  17.7 0.1 broadcast_in_dim.7
  17.8 0.7 tile.10
  18.5 0.6 multiply_reduce_fusion
  19.1 0.1 broadcast_bitcast_fusion
  19.2 0.3 copy.28.w_ref
  19.6 0.0 copy-start.6
  19.6 0.9 copy-done.6
  20.5 0.9 copy-done.7
  21.5 0.9 copy-done.11
  22.4 0.7 copy-done.14
  23.1 0.7 copy-done.16
  23.8 2.3 %prepare.1 = (bf16[512,256]{1,0:T(8,128)(2,1)S(1)}, bf16[512,256]{1,0:T(8,128)(2,1)S(1)}, bf16[2,768,256]{2,1,0:T(8,128)(2,1)S(1)}) custom-call(f32[16,16]{1,0:T(8,128)S(1)} %copy-done.15, f32[16,16,16]{2,1,0:T(8,128)S(1)} %copy-done.10, f32[16,16]{1,0:T(8,128)S(1)} %copy-done.16, f32[16,256]{1,0:T(8,128)S(1)} %copy-done.14, f32[256,16]{1,0:T(8,128)S(1)} %copy-done.11, ...), custom_call_target="tpu_custom_call" | custom-call | tf_op jit(solution)/shard_map/prepare/pallas_call | solution.py:465
  26.2 0.0 copy-start.17
  26.2 0.0 copy-start.18
  26.2 0.0 copy-start.8
  26.2 0.0 copy-start.12
  26.2 0.0 copy-start.13
  26.2 12.7 %local_near.1.after_ref.x0_all = f32[32,512,256]{2,1,0:T(8,128)} custom-call(bf16[32,512,512]{2,1,0:T(8,128)(2,1)} %u_all.1, bf16[512,256]{1,0:T(8,128)(2,1)S(1)} %get-tuple-element.10.l_ref), custom_call_target="tpu_custom_call" | custom-call | tf_op jit(solution)/shard_map/local_near/pallas_call | solution.py:477
  39.0 6.3 %all-to-all-done.r_ref = bf16[16,144,256]{2,1,0:T(8,128)(2,1)S(1)} async-done(((bf16[16,144,256]{2,1,0:T(8,128)(2,1)}), bf16[16,144,256]{2,1,0:T(8,128)(2,1)S(1)}, u32[]{:S(2)}, u32[]{:S(2)}) %all-to-all-start) | async-done | bytes 1179680 | tf_op jit(solution)/shard_map/all_to_all | solution.py:453
  45.2 6.4 %mix.1.after_ref = bf16[16,144,256]{2,1,0:T(8,128)(2,1)} custom-call(bf16[16,144,256]{2,1,0:T(8,128)(2,1)S(1)} %all-to-all-done.r_ref, bf16[128,256]{1,0:T(8,128)(2,1)S(1)} %copy-done.13, bf16[208,256]{1,0:T(8,128)(2,1)S(1)} %copy-done.12, f32[8,256]{1,0:T(8,128)S(1)} %broadcast_bitcast_fusion.1.g_ref, f32[16,64,128]{2,1,0:T(8,128)S(1)} %copy.28.w_ref, ...), custom_call_target="tpu_custom_call" | custom-call | tf_op jit(solution)/shard_map/mix/pallas_call | solution.py:504
  51.7 4.9 %all-to-all-start.1 = ((bf16[16,144,256]{2,1,0:T(8,128)(2,1)}), bf16[16,144,256]{2,1,0:T(8,128)(2,1)S(1)}, u32[]{:S(2)}, u32[]{:S(2)}) async-start(bf16[16,144,256]{2,1,0:T(8,128)(2,1)} %mix.1.after_ref), calls=%async_computation.1 | async-start | bytes 2359296 | tf_op jit(solution)/shard_map/all_to_all | solution.py:516
  56.6 0.0 copy-start.4
  56.6 14.8 %local_far.1 = (f32[32,512,256]{2,1,0:T(8,128)}, bf16[32,512,256]{2,1,0:T(8,128)(2,1)}) custom-call(bf16[32,512,512]{2,1,0:T(8,128)(2,1)} %u_all.1, bf16[512,256]{1,0:T(8,128)(2,1)S(1)} %get-tuple-element.11.l_ref, bf16[256,256]{1,0:T(8,128)(2,1)S(1)} %copy-done.2, bf16[16,144,256]{2,1,0:T(8,128)(2,1)} %mix.1.after_ref), custom_call_target="tpu_custom_call" | custom-call | tf_op jit(solution)/shard_map/local_far/pallas_call | solution.py:518
  71.4 12.9 %all-to-all-done.1.r_ref = bf16[16,144,256]{2,1,0:T(8,128)(2,1)S(1)} async-done(((bf16[16,144,256]{2,1,0:T(8,128)(2,1)}), bf16[16,144,256]{2,1,0:T(8,128)(2,1)S(1)}, u32[]{:S(2)}, u32[]{:S(2)}) %all-to-all-start.1) | async-done | bytes 1179680 | tf_op jit(solution)/shard_map/all_to_all | solution.py:516
  84.3 43.6 %tail.1 = bf16[32,512,512]{2,1,0:T(8,128)(2,1)} custom-call(bf16[16,144,256]{2,1,0:T(8,128)(2,1)S(1)} %all-to-all-done.1.r_ref, f32[32,512,256]{2,1,0:T(8,128)} %local_near.1.after_ref.x0_all, f32[32,512,256]{2,1,0:T(8,128)} %get-tuple-element.12.x1_all, bf16[32,512,512]{2,1,0:T(8,128)(2,1)} %u_all.1, bf16[32,512,256]{2,1,0:T(8,128)(2,1)} %get-tuple-element.13.f_all, ...), custom_call_target="tpu_custom_call" | custom-call | tf_op jit(solution)/shard_map/tail/pallas_call | solution.py:544
  (31 shorter events, 0.1 us)
Async XLA Ops:
  0.0 17.5 %copy-start = (f32[64,16]{0,1:T(8,128)S(1)}, f32[64,16]{0,1:T(8,128)}, u32[]{:S(2)}) copy-start(f32[64,16]{0,1:T(8,128)} %param.23) | copy-start | bytes 12292
  0.0 0.9 copy-start.9
  10.8 7.7 %copy-start.19 = (f32[64,16,16]{0,2,1:T(8,128)S(1)}, f32[64,16,16]{0,2,1:T(8,128)}, u32[]{:S(2)}) copy-start(f32[64,16,16]{0,2,1:T(8,128)} %param.22) | copy-start | bytes 196612
  10.8 7.7 %copy-start.20 = (f32[16,16,16]{2,1,0:T(8,128)S(1)}, f32[16,16,16]{2,1,0:T(8,128)}, u32[]{:S(2)}) copy-start(f32[16,16,16]{2,1,0:T(8,128)} %constant.81) | copy-start | bytes 49156
  10.8 34.4 %all-to-all-start = ((bf16[16,144,256]{2,1,0:T(8,128)(2,1)}), bf16[16,144,256]{2,1,0:T(8,128)(2,1)S(1)}, u32[]{:S(2)}, u32[]{:S(2)}) async-start(bf16[16,144,256]{2,1,0:T(8,128)(2,1)} %forward.1.after_ref), calls=%async_computation | async-start | bytes 2359296 | tf_op jit(solution)/shard_map/all_to_all | solution.py:453
  17.5 2.1 %copy-start.2 = (bf16[256,256]{1,0:T(8,128)(2,1)S(1)}, bf16[256,256]{1,0:T(8,128)(2,1)}, u32[]{:S(2)}) copy-start(bf16[256,256]{1,0:T(8,128)(2,1)} %constant.72.clone.flip_ref) | copy-start | bytes 393220
  17.5 2.1 %copy-start.5 = (f32[2,128,256]{2,1,0:T(8,128)S(1)}, f32[2,128,256]{2,1,0:T(8,128)}, u32[]{:S(2)}) copy-start(f32[2,128,256]{2,1,0:T(8,128)} %constant.71.clone.b_ref) | copy-start | bytes 786436
  17.5 2.1 %copy-start.10 = (f32[16,16,16]{2,1,0:T(8,128)S(1)}, f32[16,16,16]{2,1,0:T(8,128)}, u32[]{:S(2)}) copy-start(f32[16,16,16]{2,1,0:T(8,128)} %m_ref.1) | copy-start | bytes 49156
  17.5 2.1 %copy-start.15 = (f32[16,16]{1,0:T(8,128)S(1)}, f32[16,16]{1,0:T(8,128)}, u32[]{:S(2)}) copy-start(f32[16,16]{1,0:T(8,128)} %l_ref.1) | copy-start | bytes 3076
  19.6 1.0 copy-start.6
  20.5 0.9 copy-start.7
  21.5 0.9 copy-start.11
  22.4 0.7 copy-start.14
  23.1 0.7 copy-start.16
  26.1 12.7 %copy-start.21 = (f32[8,128]{1,0:T(8,128)S(1)}, f32[8,128]{1,0:T(8,128)}, u32[]{:S(2)}) copy-start(f32[8,128]{1,0:T(8,128)} %tile.10) | copy-start | bytes 12292
  26.2 12.7 %copy-start.17 = (f32[256,256]{1,0:T(8,128)S(1)}, f32[256,256]{1,0:T(8,128)}, u32[]{:S(2)}) copy-start(f32[256,256]{1,0:T(8,128)} %constant.82) | copy-start | bytes 786436
  26.2 12.7 %copy-start.18 = (f32[256,256]{1,0:T(8,128)S(1)}, f32[256,256]{1,0:T(8,128)}, u32[]{:S(2)}) copy-start(f32[256,256]{1,0:T(8,128)} %constant.73.clone) | copy-start | bytes 786436
  26.2 19.1 %copy-start.8 = (bf16[256,256]{1,0:T(8,128)(2,1)S(1)}, bf16[256,256]{1,0:T(8,128)(2,1)}, u32[]{:S(2)}) copy-start(bf16[256,256]{1,0:T(8,128)(2,1)} %constant.78.clone.order_ref) | copy-start | bytes 393220
  26.2 19.0 %copy-start.12 = (bf16[208,256]{1,0:T(8,128)(2,1)S(1)}, bf16[208,256]{1,0:T(8,128)(2,1)}, u32[]{:S(2)}) copy-start(bf16[208,256]{1,0:T(8,128)(2,1)} %constant.77.clone.b_ref) | copy-start | bytes 319492
  26.2 19.0 %copy-start.13 = (bf16[128,256]{1,0:T(8,128)(2,1)S(1)}, bf16[128,256]{1,0:T(8,128)(2,1)}, u32[]{:S(2)}) copy-start(bf16[128,256]{1,0:T(8,128)(2,1)} %constant.76.clone.a_ref) | copy-start | bytes 196612
  51.7 32.6 %all-to-all-start.1 = ((bf16[16,144,256]{2,1,0:T(8,128)(2,1)}), bf16[16,144,256]{2,1,0:T(8,128)(2,1)S(1)}, u32[]{:S(2)}, u32[]{:S(2)}) async-start(bf16[16,144,256]{2,1,0:T(8,128)(2,1)} %mix.1.after_ref), calls=%async_computation.1 | async-start | bytes 2359296 | tf_op jit(solution)/shard_map/all_to_all | solution.py:516
  56.5 27.8 %copy-start.3 = (bf16[512,144]{1,0:T(8,128)(2,1)S(1)}, bf16[512,144]{1,0:T(8,128)(2,1)}, u32[]{:S(2)}) copy-start(bf16[512,144]{1,0:T(8,128)(2,1)} %constant.80.clone.v_ref) | copy-start | bytes 442372
  56.6 27.8 %copy-start.4 = (bf16[512,256]{1,0:T(8,128)(2,1)S(1)}, bf16[512,256]{1,0:T(8,128)(2,1)}, u32[]{:S(2)}) copy-start(bf16[512,256]{1,0:T(8,128)(2,1)} %constant.79.clone.by_ref) | copy-start | bytes 786436
  84.3 43.6 %copy-start.1 = (f32[64,16]{0,1:T(8,128)S(1)}, f32[64,16]{0,1:T(8,128)}, u32[]{:S(2)}) copy-start(f32[64,16]{0,1:T(8,128)} %param.23) | copy-start | bytes 12292

commit v10 on v9

--- a/solution.py
+++ b/solution.py
@@ -174,6 +174,7 @@
         for k, _ in tiles:
             m_ref[k, devices * highs :] = jnp.zeros((depth * GROUP - devices * highs, LANE), F32)
     shifts = w_ref.shape[0]
+    few = math.isqrt(shifts)
     for q in range(GROUP):
         modes = [m_ref[k, pl.ds(q, depth, stride=GROUP), :] for k, _ in tiles]
         high, low = split(jnp.concatenate(modes, axis=1))
@@ -183,9 +184,13 @@
         mixed = []
         for k, lanes in tiles:
             part = coef[:, lanes]
-            total = part * w_ref[0]
-            for n in range(1, shifts):
-                total = total + pltpu.roll(part, n * (LANE // shifts), 1) * w_ref[n]
+            turned = [part] + [pltpu.roll(part, n * (LANE // shifts), 1) for n in range(1, few)]
+            total = None
+            for far in range(0, shifts, few):
+                inner = turned[0] * w_ref[far]
+                for n in range(1, few):
+                    inner = inner + turned[n] * w_ref[far + n]
+                total = pltpu.roll(inner, far * (LANE // shifts), 1) + total if far else inner
             mixed.append(total)
         high, low = split(jnp.concatenate(mixed, axis=1))
         right = jnp.concatenate([high, high, low, low], axis=0)
@@ -391,10 +396,13 @@
 
 def diagonals(matrices):
     n = matrices.shape[1]
-    ids = np.arange(n)
-    picks = (ids[None, :, None] == (ids[None, None, :] - ids[:, None, None]) % n).astype(np.float32)
-    rows = jnp.sum(matrices[None] * picks[:, None], axis=2)
-    return jnp.repeat(rows, LANE // n, axis=2)
+    few = math.isqrt(n)
+    shift, lane = np.divmod(np.arange(n * n), n)
+    to = (lane + shift // few * few) % n
+    picks = np.zeros((n * n, n * n), np.float32)
+    picks[(to - shift) % n * n + to, np.arange(n * n)] = 1
+    rows = jnp.dot(matrices.reshape(-1, n * n), picks, precision=lax.Precision.HIGHEST)
+    return jnp.repeat(jnp.transpose(rows.reshape(-1, n, n), (1, 0, 2)), LANE // n, axis=2)
 
 
 def fits(mesh_lat, rows, width_y, cells, chans, modes_x, modes_y):
@@ -407,6 +415,7 @@
         and width_y % 256 == 0
         and 4 * modes_y == SPAN
         and modes_x % 8 == 0
+        and math.isqrt(chans) ** 2 == chans
     )
 
 

time: 129 us -> 127 us (0.984)
  Pallas kernels: 89.8 us -> 87.8 us
  transfers between devices with their start and end apart: 2 -> 2, of which waited for: 2 -> 2; matrix products, arithmetic and copies ran while one was open for 2% -> 1% of each run, Pallas kernels for 23% -> 24%
where the time goes in v10:
time: 127 us; the launch traced here: 126 us
  Pallas kernels  87.8 us (69%)
  waiting for transfers between devices  18.7 us (15%)
  starting transfers between devices  11.4 us (9%)
  local copies, waits for them, and re-layouts  7.46 us (6%)
    pallas_call x1, Pallas kernels, shards(): pl.pallas_call(functools.partial(tail_kernel, 16), grid=(steps + 1,), in_...  42.6 us
    pallas_call x1, Pallas kernels, shards(): pl.pallas_call(local_far_kernel, grid=(rows // four,), in_specs=[pl.Block...  14.8 us
    all_to_all x1, waiting for transfers between devices, shards(): lax.all_to_all(mixed, 'lat', split_axis=0, concat_axis=0, tiled=True)  13 us
    pallas_call x1, Pallas kernels, shards(): pl.pallas_call(local_near_kernel, grid=(rows // four,), in_specs=[pl.Bloc...  12.7 us
    pallas_call x1, Pallas kernels, shards(): pl.pallas_call(functools.partial(forward_kernel, funcs, fine), grid=(step...  9.91 us
    all_to_all x1, starting transfers between devices, shards(): lax.all_to_all(sent, 'lat', split_axis=0, concat_axis=0, tiled=True)  6.55 us
    unnamed x44, local copies, waits for them, and re-layouts  6.13 us
    all_to_all x1, waiting for transfers between devices, shards(): lax.all_to_all(sent, 'lat', split_axis=0, concat_axis=0, tiled=True)  5.7 us
  transfers between devices with their start and end apart: 2, of which 2 were waited for; matrix products, arithmetic and copies ran while one was open for 1% of the time, Pallas kernels for 24%

profile of v10, /device:TPU:15, one launch (start us, length us, event | category | flops | bytes accessed | tf_op | source)
XLA Modules:
  0.0 126.1 jit_solution(18153212852370009171)
XLA Ops:
  0.0 0.0 copy-start.9
  0.0 1.0 copy-done.9
  1.0 9.9 %forward.1.after_ref = bf16[16,144,256]{2,1,0:T(8,128)(2,1)} custom-call(bf16[128,512]{1,0:T(8,128)(2,1)S(1)} %copy-done.9, bf16[32,512,512]{2,1,0:T(8,128)(2,1)} %u_all.1, bf16[32,512,512]{2,1,0:T(8,128)(2,1)} %u_all.1), custom_call_target="tpu_custom_call" | custom-call | tf_op jit(solution)/shard_map/forward/pallas_call | solution.py:445
  10.9 6.6 %all-to-all-start = ((bf16[16,144,256]{2,1,0:T(8,128)(2,1)}), bf16[16,144,256]{2,1,0:T(8,128)(2,1)S(1)}, u32[]{:S(2)}, u32[]{:S(2)}) async-start(bf16[16,144,256]{2,1,0:T(8,128)(2,1)} %forward.1.after_ref), calls=%async_computation | async-start | bytes 2359296 | tf_op jit(solution)/shard_map/all_to_all | solution.py:462
  17.5 0.1 constant_dynamic-slice_fusion
  17.5 0.1 copy.25
  17.6 0.1 broadcast_in_dim.6
  17.7 0.7 tile.10
  18.4 0.4 convolution_bitcast_fusion
  18.8 0.1 broadcast_bitcast_fusion
  18.9 0.3 copy.27.w_ref
  19.2 0.0 copy-start.6
  19.2 0.9 copy-done.6
  20.2 0.9 copy-done.7
  21.1 0.9 copy-done.10
  22.0 0.9 copy-done.11
  22.9 0.7 copy-done.15
  23.6 0.7 copy-done.16
  24.3 2.3 %prepare.1 = (bf16[512,256]{1,0:T(8,128)(2,1)S(1)}, bf16[512,256]{1,0:T(8,128)(2,1)S(1)}, bf16[2,768,256]{2,1,0:T(8,128)(2,1)S(1)}) custom-call(f32[16,16]{1,0:T(8,128)S(1)} %copy-done.15, f32[16,16,16]{2,1,0:T(8,128)S(1)} %copy-done.10, f32[16,16]{1,0:T(8,128)S(1)} %copy-done.16, f32[16,256]{1,0:T(8,128)S(1)} %copy-done.14, f32[256,16]{1,0:T(8,128)S(1)} %copy-done.11, ...), custom_call_target="tpu_custom_call" | custom-call | tf_op jit(solution)/shard_map/prepare/pallas_call | solution.py:474
  26.7 0.0 copy-start.18
  26.7 0.0 copy-start.19
  26.7 0.0 copy-start.8
  26.7 0.0 copy-start.12
  26.7 0.0 copy-start.13
  26.8 12.7 %local_near.1.after_ref.x0_all = f32[32,512,256]{2,1,0:T(8,128)} custom-call(bf16[32,512,512]{2,1,0:T(8,128)(2,1)} %u_all.1, bf16[512,256]{1,0:T(8,128)(2,1)S(1)} %get-tuple-element.10.l_ref), custom_call_target="tpu_custom_call" | custom-call | tf_op jit(solution)/shard_map/local_near/pallas_call | solution.py:486
  39.5 5.7 %all-to-all-done.r_ref = bf16[16,144,256]{2,1,0:T(8,128)(2,1)S(1)} async-done(((bf16[16,144,256]{2,1,0:T(8,128)(2,1)}), bf16[16,144,256]{2,1,0:T(8,128)(2,1)S(1)}, u32[]{:S(2)}, u32[]{:S(2)}) %all-to-all-start) | async-done | bytes 1179680 | tf_op jit(solution)/shard_map/all_to_all | solution.py:462
  45.2 5.5 %mix.1.after_ref = bf16[16,144,256]{2,1,0:T(8,128)(2,1)} custom-call(bf16[16,144,256]{2,1,0:T(8,128)(2,1)S(1)} %all-to-all-done.r_ref, bf16[128,256]{1,0:T(8,128)(2,1)S(1)} %copy-done.13, bf16[208,256]{1,0:T(8,128)(2,1)S(1)} %copy-done.12, f32[8,256]{1,0:T(8,128)S(1)} %broadcast_bitcast_fusion.1.g_ref, f32[16,64,128]{2,1,0:T(8,128)S(1)} %copy.27.w_ref, ...), custom_call_target="tpu_custom_call" | custom-call | tf_op jit(solution)/shard_map/mix/pallas_call | solution.py:513
  50.7 4.9 %all-to-all-start.1 = ((bf16[16,144,256]{2,1,0:T(8,128)(2,1)}), bf16[16,144,256]{2,1,0:T(8,128)(2,1)S(1)}, u32[]{:S(2)}, u32[]{:S(2)}) async-start(bf16[16,144,256]{2,1,0:T(8,128)(2,1)} %mix.1.after_ref), calls=%async_computation.1 | async-start | bytes 2359296 | tf_op jit(solution)/shard_map/all_to_all | solution.py:525
  55.6 0.0 copy-start.4
  55.6 14.8 %local_far.1 = (f32[32,512,256]{2,1,0:T(8,128)}, bf16[32,512,256]{2,1,0:T(8,128)(2,1)}) custom-call(bf16[32,512,512]{2,1,0:T(8,128)(2,1)} %u_all.1, bf16[512,256]{1,0:T(8,128)(2,1)S(1)} %get-tuple-element.11.l_ref, bf16[256,256]{1,0:T(8,128)(2,1)S(1)} %copy-done.2, bf16[16,144,256]{2,1,0:T(8,128)(2,1)} %mix.1.after_ref), custom_call_target="tpu_custom_call" | custom-call | tf_op jit(solution)/shard_map/local_far/pallas_call | solution.py:527
  70.4 13.0 %all-to-all-done.1.r_ref = bf16[16,144,256]{2,1,0:T(8,128)(2,1)S(1)} async-done(((bf16[16,144,256]{2,1,0:T(8,128)(2,1)}), bf16[16,144,256]{2,1,0:T(8,128)(2,1)S(1)}, u32[]{:S(2)}, u32[]{:S(2)}) %all-to-all-start.1) | async-done | bytes 1179680 | tf_op jit(solution)/shard_map/all_to_all | solution.py:525
  83.3 42.6 %tail.1 = bf16[32,512,512]{2,1,0:T(8,128)(2,1)} custom-call(bf16[16,144,256]{2,1,0:T(8,128)(2,1)S(1)} %all-to-all-done.1.r_ref, f32[32,512,256]{2,1,0:T(8,128)} %local_near.1.after_ref.x0_all, f32[32,512,256]{2,1,0:T(8,128)} %get-tuple-element.12.x1_all, bf16[32,512,512]{2,1,0:T(8,128)(2,1)} %u_all.1, bf16[32,512,256]{2,1,0:T(8,128)(2,1)} %get-tuple-element.13.f_all, ...), custom_call_target="tpu_custom_call" | custom-call | tf_op jit(solution)/shard_map/tail/pallas_call | solution.py:553
  (31 shorter events, 0.1 us)
Async XLA Ops:
  0.0 18.4 %copy-start = (f32[64,16,16]{0,2,1:T(8,128)S(1)}, f32[64,16,16]{0,2,1:T(8,128)}, u32[]{:S(2)}) copy-start(f32[64,16,16]{0,2,1:T(8,128)} %param.22) | copy-start | bytes 196612
  0.0 19.2 %copy-start.2 = (bf16[256,256]{1,0:T(8,128)(2,1)S(1)}, bf16[256,256]{1,0:T(8,128)(2,1)}, u32[]{:S(2)}) copy-start(bf16[256,256]{1,0:T(8,128)(2,1)} %constant.70.clone.flip_ref) | copy-start | bytes 393220
  0.0 19.2 %copy-start.5 = (f32[2,128,256]{2,1,0:T(8,128)S(1)}, f32[2,128,256]{2,1,0:T(8,128)}, u32[]{:S(2)}) copy-start(f32[2,128,256]{2,1,0:T(8,128)} %constant.69.clone.b_ref) | copy-start | bytes 786436
  0.0 1.0 copy-start.9
  1.0 16.5 %copy-start.21 = (f32[64,16]{0,1:T(8,128)S(1)}, f32[64,16]{0,1:T(8,128)}, u32[]{:S(2)}) copy-start(f32[64,16]{0,1:T(8,128)} %param.23) | copy-start | bytes 12292
  1.0 17.4 %copy-start.17 = (f32[16,16,256]{2,1,0:T(8,128)S(1)}, f32[16,16,256]{2,1,0:T(8,128)}, u32[]{:S(2)}) copy-start(f32[16,16,256]{2,1,0:T(8,128)} %constant.80) | copy-start | bytes 786436
  1.0 18.2 %copy-start.14 = (f32[16,256]{1,0:T(8,128)S(1)}, f32[16,256]{1,0:T(8,128)}, u32[]{:S(2)}) copy-start(f32[16,256]{1,0:T(8,128)} %constant.65.clone.e_ref) | copy-start | bytes 49156
  10.9 34.3 %all-to-all-start = ((bf16[16,144,256]{2,1,0:T(8,128)(2,1)}), bf16[16,144,256]{2,1,0:T(8,128)(2,1)S(1)}, u32[]{:S(2)}, u32[]{:S(2)}) async-start(bf16[16,144,256]{2,1,0:T(8,128)(2,1)} %forward.1.after_ref), calls=%async_computation | async-start | bytes 2359296 | tf_op jit(solution)/shard_map/all_to_all | solution.py:462
  19.2 1.0 copy-start.6
  20.2 0.9 copy-start.7
  21.1 0.9 copy-start.10
  22.0 0.9 copy-start.11
  22.9 0.7 copy-start.15
  23.6 0.7 copy-start.16
  26.7 12.8 %copy-start.20 = (f32[8,128]{1,0:T(8,128)S(1)}, f32[8,128]{1,0:T(8,128)}, u32[]{:S(2)}) copy-start(f32[8,128]{1,0:T(8,128)} %tile.10) | copy-start | bytes 12292
  26.7 12.8 %copy-start.18 = (f32[256,256]{1,0:T(8,128)S(1)}, f32[256,256]{1,0:T(8,128)}, u32[]{:S(2)}) copy-start(f32[256,256]{1,0:T(8,128)} %constant.81) | copy-start | bytes 786436
  26.7 12.7 %copy-start.19 = (f32[256,256]{1,0:T(8,128)S(1)}, f32[256,256]{1,0:T(8,128)}, u32[]{:S(2)}) copy-start(f32[256,256]{1,0:T(8,128)} %constant.71.clone) | copy-start | bytes 786436
  26.7 18.5 %copy-start.8 = (bf16[256,256]{1,0:T(8,128)(2,1)S(1)}, bf16[256,256]{1,0:T(8,128)(2,1)}, u32[]{:S(2)}) copy-start(bf16[256,256]{1,0:T(8,128)(2,1)} %constant.76.clone.order_ref) | copy-start | bytes 393220
  26.7 18.5 %copy-start.12 = (bf16[208,256]{1,0:T(8,128)(2,1)S(1)}, bf16[208,256]{1,0:T(8,128)(2,1)}, u32[]{:S(2)}) copy-start(bf16[208,256]{1,0:T(8,128)(2,1)} %constant.75.clone.b_ref) | copy-start | bytes 319492
  26.7 18.5 %copy-start.13 = (bf16[128,256]{1,0:T(8,128)(2,1)S(1)}, bf16[128,256]{1,0:T(8,128)(2,1)}, u32[]{:S(2)}) copy-start(bf16[128,256]{1,0:T(8,128)(2,1)} %constant.74.clone.a_ref) | copy-start | bytes 196612
  50.7 32.6 %all-to-all-start.1 = ((bf16[16,144,256]{2,1,0:T(8,128)(2,1)}), bf16[16,144,256]{2,1,0:T(8,128)(2,1)S(1)}, u32[]{:S(2)}, u32[]{:S(2)}) async-start(bf16[16,144,256]{2,1,0:T(8,128)(2,1)} %mix.1.after_ref), calls=%async_computation.1 | async-start | bytes 2359296 | tf_op jit(solution)/shard_map/all_to_all | solution.py:525
  55.6 27.8 %copy-start.3 = (bf16[512,144]{1,0:T(8,128)(2,1)S(1)}, bf16[512,144]{1,0:T(8,128)(2,1)}, u32[]{:S(2)}) copy-start(bf16[512,144]{1,0:T(8,128)(2,1)} %constant.78.clone.v_ref) | copy-start | bytes 442372
  55.6 27.8 %copy-start.4 = (bf16[512,256]{1,0:T(8,128)(2,1)S(1)}, bf16[512,256]{1,0:T(8,128)(2,1)}, u32[]{:S(2)}) copy-start(bf16[512,256]{1,0:T(8,128)(2,1)} %constant.77.clone.by_ref) | copy-start | bytes 786436
  83.3 42.6 %copy-start.1 = (f32[64,16,16]{0,2,1:T(8,128)S(1)}, f32[64,16,16]{0,2,1:T(8,128)}, u32[]{:S(2)}) copy-start(f32[64,16,16]{0,2,1:T(8,128)} %param.22) | copy-start | bytes 196612
